TPU v7x, 128 devices: a whole 4x4x4 slice. The times are simulated.
128 devices in a mesh: tq: 8 (over z, core), slab: 16 (over x, y).
Axes of the slice: x: 4, y: 4, z: 4, core: 2. Of those that a mesh axis runs over, the one named last changes fastest.
Arguments:
- vert_ph: bfloat16 [8, 4096, 4096], P('tq', 'slab'), may hold values from -6 to 6
- full_pp: bfloat16 [8, 4096, 4096], P('tq', 'slab'), may hold values from -6 to 6
- target: int32 [8, 4096], P('tq', 'slab'), may hold values from 0 to 32767, as said below
- shift: int32 [8, 4096], P('tq', 'slab'), may hold values from -16 to 16
- trans_mom: int32 [8], P('tq'), may hold values from 0 to 63
- trans_bose: int32 [8], P('tq'), may hold values from 0 to 31
- energies: float32 [64], replicated, may hold values from -4 to 4
- pair_table: int32 [64, 64], replicated, may hold values from 0 to 63, as said below
Outputs:
- gamma: float32 [8, 4096, 4096], P('tq', 'slab')
- ladder: float32 [8, 4096, 4096], P('tq', 'slab')
Inputs may be any that keep to these rules, and one draw needn't show every extreme that they name: `target`: rows are grouped by the device that holds them (transfer block on tq, outer-row block on slab, rows in the order transfer then outer row). The rows of one device name at most 3 rows held by any one device, and exactly 3 rows of one device. The momentum labels are a permutation of the points of a 8 x 8 periodic lattice; pair_table[a, b] is the label of the point of a minus the point of b.
All inputs are finite; a program needn't handle non-finite values.
Results may differ from a plain program's by a relative error of at most 0.003.
Values may be sent and summed in bfloat16 or wider, within the bound.
No kernel may reach another device: no remote copies, remote signals or barrier semaphores. Data moves between devices by JAX's collectives and lax.ppermute only.
A program may use at most 128 MiB of HBM per device.

v0:
```python
import jax
import jax.numpy as jnp
from jax import lax
from jax.sharding import PartitionSpec as P

NB = 32
NF = 64
NQ = 64


HUBBARD = 2.0
TEMPER = 0.25
PI_VALUE = 3.141592653589793


def bubble(band_pair, band_own, bose_freq):
    fermi_freq = (
        PI_VALUE
        * TEMPER
        * (2.0 * (jnp.arange(NF, dtype=jnp.int32) - NF // 2).astype(jnp.float32) + 1.0)
    )
    other_freq = bose_freq[:, None] - fermi_freq[None, :]
    numerator = (
        band_own[None, :, None] * band_pair[:, :, None]
        - (fermi_freq[None, :] * other_freq)[:, None, :]
    )
    left_denom = fermi_freq[None, None, :] ** 2 + band_own[None, :, None] ** 2
    right_denom = other_freq[:, None, :] ** 2 + band_pair[:, :, None] ** 2
    values = TEMPER * numerator / (left_denom * right_denom)
    return values.reshape(band_pair.shape[0], NQ * NF)


def per_device(vert_ph, full_pp, target, shift, trans_mom, trans_bose, energies, pair_table):
    n_tq = lax.axis_size("tq")
    n_slab = lax.axis_size("slab")
    devices = n_tq * n_slab
    local_trans = vert_ph.shape[0]
    rows_slab = vert_ph.shape[1]
    row_width = vert_ph.shape[2]
    rows_dev = local_trans * rows_slab
    capacity = max(2, 3 * rows_dev // (2 * devices))
    ph_rows = vert_ph.reshape(rows_dev, NQ, NF)
    freq_iota = jnp.arange(NF, dtype=jnp.int32)
    move_by = shift.reshape(rows_dev)
    mover = (freq_iota[None, :, None] == freq_iota[None, None, :] - move_by[:, None, None]).astype(
        jnp.bfloat16
    )
    shifted = jnp.einsum("rkm,rmj->rkj", ph_rows, mover, preferred_element_type=jnp.float32)
    shifted = shifted.astype(jnp.bfloat16).reshape(rows_dev, row_width)
    global_row = target.reshape(rows_dev)
    dest_trans = global_row // row_width
    dest_row = global_row % row_width
    dest_dev = dest_trans // local_trans * n_slab + dest_row // rows_slab
    dest_local = dest_trans % local_trans * rows_slab + dest_row % rows_slab
    member = (dest_dev[:, None] == jnp.arange(devices, dtype=jnp.int32)[None, :]).astype(jnp.int32)
    slot_index = jnp.sum(jnp.cumsum(member, axis=0) * member, axis=1) - 1
    flat_slot = dest_dev * capacity + slot_index
    placer = (
        jnp.arange(devices * capacity, dtype=jnp.int32)[:, None] == flat_slot[None, :]
    ).astype(jnp.bfloat16)
    payload = jnp.dot(placer, shifted, preferred_element_type=jnp.float32).astype(jnp.bfloat16)
    payload = payload.reshape(devices, capacity, row_width)
    label_code = dest_local + 1
    label_pair = jnp.stack([label_code // 256, label_code % 256], axis=1).astype(jnp.float32)
    label_box = jnp.dot(placer.astype(jnp.float32), label_pair, precision=lax.Precision.HIGHEST)
    label_box = label_box.reshape(devices, capacity, 2).astype(jnp.bfloat16)
    arrived = (
        lax.all_to_all(payload, ("tq", "slab"), split_axis=0, concat_axis=0, tiled=True),
        lax.all_to_all(label_box, ("tq", "slab"), split_axis=0, concat_axis=0, tiled=True),
    )
    incoming = arrived[0].reshape(devices * capacity, row_width)
    label_recv = arrived[1].reshape(devices * capacity, 2).astype(jnp.int32)
    code_recv = label_recv[:, 0] * 256 + label_recv[:, 1]
    where_to = jnp.where(code_recv > 0, code_recv - 1, rows_dev)
    collector = (jnp.arange(rows_dev, dtype=jnp.int32)[:, None] == where_to[None, :]).astype(
        jnp.bfloat16
    )
    summed = jnp.dot(collector, incoming, preferred_element_type=jnp.float32)
    gamma_pp = (HUBBARD + summed).reshape(local_trans, rows_slab, row_width)
    pick_mom = (trans_mom[:, None] == jnp.arange(NQ, dtype=jnp.int32)[None, :]).astype(jnp.float32)
    pair_rows = jnp.dot(pick_mom, pair_table.astype(jnp.float32), precision=lax.Precision.HIGHEST)
    picker = (
        pair_rows[:, :, None] == jnp.arange(NQ, dtype=jnp.int32).astype(jnp.float32)[None, None, :]
    ).astype(jnp.float32)
    band_pair = jnp.einsum("qkl,l->qk", picker, energies, precision=lax.Precision.HIGHEST)
    bose_freq = 2.0 * PI_VALUE * TEMPER * (trans_bose - NB // 2).astype(jnp.float32)
    pair_bubble = bubble(band_pair, energies, bose_freq)
    weighted = (gamma_pp * pair_bubble[:, None, :]).astype(jnp.bfloat16)
    ladder_out = jnp.einsum(
        "tnm,tmp->tnp",
        weighted,
        lax.all_gather(full_pp, "slab", axis=1, tiled=True),
        preferred_element_type=jnp.float32,
    )
    return (gamma_pp, ladder_out)


def solution(mesh):
    in_specs = (
        P("tq", "slab", None),
        P("tq", "slab", None),
        P("tq", "slab"),
        P("tq", "slab"),
        P("tq"),
        P("tq"),
        P(),
        P(),
    )
    out_specs = (P("tq", "slab", None), P("tq", "slab", None))
    return jax.shard_map(
        per_device, mesh=mesh, in_specs=in_specs, out_specs=out_specs, check_vma=False
    )
```

profile of v0, /device:TPU:0, one launch (start us, length us, event | category | flops | bytes accessed | tf_op | source)
XLA Modules:
  0.0 272.8 jit_solution(16482754987130761273)
XLA Ops:
  7.2 0.7 all-gather.2.cloned.1.call-update
  7.9 0.7 fusion.27
  9.0 0.7 fusion.28
  9.9 0.7 and_select_fusion.1
  10.6 0.7 multiply_add_fusion
  11.3 0.3 convolution_convert_fusion.1
  11.6 0.3 convert_element_type.75
  11.9 0.7 copy.25
  12.5 11.1 %all-to-all-start = ((bf16[128,3,2]{1,2,0:T(2,128)(2,1)}), bf16[128,3,2]{1,2,0:T(2,128)(2,1)S(1)}, u32[]{:S(2)}, u32[]{:S(2)}) async-start(bf16[128,3,2]{1,2,0:T(2,128)(2,1)} %copy.25), calls=%async_computation | async-start | bytes 131072 | tf_op jit(solution)/shard_map/all_to_all | solution.py:69
  23.7 3.5 %copy.28 = bf16[1,256,4096]{1,2,0:T(8,128)(2,1)S(1)} copy(bf16[1,256,4096]{2,1,0:T(8,128)(2,1)} %param.8) | data formatting | bytes 4194304 | tf_op args[0]
  27.2 6.6 %copy.29 = bf16[256,64,64]{2,1,0:T(8,128)(2,1)} copy(bf16[256,64,64]{0,2,1:T(8,128)(2,1)S(1)} %bitcast.53) | data formatting | bytes 4194304 | tf_op jit(solution)/shard_map/reshape | solution.py:42
  34.0 7.1 %convert_bitcast_fusion = bf16[256,64,64]{1,2,0:T(8,128)(2,1)} fusion(bf16[256,64,64]{2,1,0:T(8,128)(2,1)} %copy.29, s32[256,64]{1,0:T(8,128)S(1)} %iota_subtract_fusion), kind=kOutput, calls=%fused_computation.8 | convolution fusion | flops 136314880 | bytes 4259840 | tf_op jit(solution)/shard_map/rkm,rmj->rkj/dot_general | solution.py:48
  41.1 7.8 %copy.30 = bf16[256,64,64]{0,2,1:T(8,128)(2,1)} copy(bf16[256,64,64]{1,2,0:T(8,128)(2,1)} %convert_bitcast_fusion) | data formatting | bytes 4194304 | tf_op jit(solution)/shard_map/convert_element_type | solution.py:49
  48.9 2.7 convolution_convert_fusion
  51.6 4.4 %reshape.487 = bf16[128,3,4096]{2,1,0:T(4,128)(2,1)} reshape(bf16[384,4096]{1,0:T(8,128)(2,1)S(1)} %convolution_convert_fusion) | data formatting | bytes 6291456 | tf_op jit(solution)/shard_map/reshape | solution.py:62
  56.0 10.4 %all-to-all-start.1 = ((bf16[128,3,4096]{2,1,0:T(4,128)(2,1)}), bf16[128,3,4096]{2,1,0:T(4,128)(2,1)}, u32[]{:S(2)}, u32[]{:S(2)}) async-start(bf16[128,3,4096]{2,1,0:T(4,128)(2,1)} %reshape.487), calls=%async_computation.1 | async-start | bytes 8388608 | tf_op jit(solution)/shard_map/all_to_all | solution.py:68
  67.1 0.2 fusion.34
  67.4 0.2 broadcast_reduce_fusion
  69.2 0.2 reshape.491
  69.4 85.9 %all-to-all-done.1 = bf16[128,3,4096]{2,1,0:T(4,128)(2,1)} async-done(((bf16[128,3,4096]{2,1,0:T(4,128)(2,1)}), bf16[128,3,4096]{2,1,0:T(4,128)(2,1)}, u32[]{:S(2)}, u32[]{:S(2)}) %all-to-all-start.1) | async-done | bytes 3145760 | tf_op jit(solution)/shard_map/all_to_all | solution.py:68
  155.4 6.0 %reshape.488 = bf16[384,4096]{1,0:T(8,128)(2,1)S(1)} reshape(bf16[128,3,4096]{2,1,0:T(4,128)(2,1)} %all-to-all-done.1) | data formatting | bytes 6291456 | tf_op jit(solution)/shard_map/reshape | solution.py:71
  161.4 3.3 %convolution_add_fusion = f32[256,4096]{1,0:T(8,128)} fusion(bf16[384,4096]{1,0:T(8,128)(2,1)S(1)} %reshape.488, s32[384]{0:T(512)S(1)} %fusion.23), kind=kOutput, calls=%fused_computation.6 | convolution fusion | flops 806453248 | bytes 7341568 | tf_op jit(solution)/shard_map/dot_general | solution.py:78
  164.7 83.7 %all-gather.2.cloned.1.call-done = bf16[1,4096,4096]{2,1,0:T(8,128)(2,1)} async-done(((bf16[1,256,4096]{2,1,0:T(8,128)(2,1)}), bf16[1,4096,4096]{2,1,0:T(8,128)(2,1)}) %all-gather.2.cloned.1.call-update) | async-done | bytes 33554448 | tf_op jit(solution)/shard_map/all_gather | solution.py:92
  248.4 17.5 %fusion.3 = f32[1,256,4096]{2,1,0:T(8,128)} fusion(bf16[1,4096,4096]{2,1,0:T(8,128)(2,1)} %all-gather.2.cloned.1.call-done, f32[256,4096]{1,0:T(8,128)} %convolution_add_fusion, f32[4096]{0:T(1024)S(1)} %multiply_divide_fusion), kind=kOutput, calls=%fused_computation.5 | convolution fusion | flops 8592031744 | bytes 41959424 | tf_op jit(solution)/shard_map/tnm,tmp->tnp/dot_general | solution.py:89
  (39 shorter events, 1.8 us)
Async XLA Ops:
  7.2 241.2 %all-gather.2.cloned.1.call-start = ((), (), s32[]{:S(2)}) async-start(), calls=%async_computation.2 | async-start | bytes 35651584 | tf_op jit(solution)/shard_map/all_gather | solution.py:92
  12.5 43.4 %all-to-all-start = ((bf16[128,3,2]{1,2,0:T(2,128)(2,1)}), bf16[128,3,2]{1,2,0:T(2,128)(2,1)S(1)}, u32[]{:S(2)}, u32[]{:S(2)}) async-start(bf16[128,3,2]{1,2,0:T(2,128)(2,1)} %copy.25), calls=%async_computation | async-start | bytes 131072 | tf_op jit(solution)/shard_map/all_to_all | solution.py:69
  27.2 6.6 %copy-start.1 = (s32[1,256]{1,0:T(1,128)S(1)}, s32[1,256]{1,0:T(1,128)}, u32[]{:S(2)}) copy-start(s32[1,256]{1,0:T(1,128)} %param.11) | copy-start | bytes 3076
  55.9 11.0 %copy-start = (s32[64,64]{1,0:T(8,128)S(1)}, s32[64,64]{1,0:T(8,128)}, u32[]{:S(2)}) copy-start(s32[64,64]{1,0:T(8,128)} %param.15) | copy-start | bytes 49156
  56.0 11.2 %copy-start.2 = (f32[64]{0:T(128)S(1)}, f32[64]{0:T(128)}, u32[]{:S(2)}) copy-start(f32[64]{0:T(128)} %param.14) | copy-start | bytes 772
  56.0 99.4 %all-to-all-start.1 = ((bf16[128,3,4096]{2,1,0:T(4,128)(2,1)}), bf16[128,3,4096]{2,1,0:T(4,128)(2,1)}, u32[]{:S(2)}, u32[]{:S(2)}) async-start(bf16[128,3,4096]{2,1,0:T(4,128)(2,1)} %reshape.487), calls=%async_computation.1 | async-start | bytes 8388608 | tf_op jit(solution)/shard_map/all_to_all | solution.py:68
Sparse Core Ops, SparseCore 0:
  10.1 238.2 all-gather.1
where the time goes:
time: 275 us; the launch traced here: 273 us
  waiting for transfers between devices  170 us (62%)
  matrix products  31.2 us (11%)
  local copies, waits for them, and re-layouts  30.8 us (11%)
  starting transfers between devices  21.5 us (8%)
  between operations  15.5 us (6%)
  other arithmetic  3.42 us (1%)
    all_to_all x1, waiting for transfers between devices, per_device(): lax.all_to_all(payload, ('tq', 'slab'), split_axis=0, concat_axis=0, tile...  85.9 us
    all_gather x1, waiting for transfers between devices, per_device(): lax.all_gather(full_pp, 'slab', axis=1, tiled=True)  83.7 us
    dot_general x1, matrix products, per_device(): jnp.einsum('tnm,tmp->tnp', weighted, lax.all_gather(full_pp, 'slab', axis...  17.5 us
    all_to_all x1, starting transfers between devices, per_device(): lax.all_to_all(label_box, ('tq', 'slab'), split_axis=0, concat_axis=0, ti...  11.1 us
    all_to_all x1, starting transfers between devices, per_device(): lax.all_to_all(payload, ('tq', 'slab'), split_axis=0, concat_axis=0, tile...  10.4 us
    convert_element_type x1, local copies, waits for them, and re-layouts, per_device(): shifted = shifted.astype(jnp.bfloat16).reshape(rows_dev, row_width)  7.83 us
    dot_general x1, matrix products, per_device(): jnp.einsum('rkm,rmj->rkj', ph_rows, mover, preferred_element_type=jnp.flo...  7.08 us
    reshape x1, local copies, waits for them, and re-layouts, per_device(): ph_rows = vert_ph.reshape(rows_dev, NQ, NF)  6.63 us
  transfers between devices with their start and end apart: 3, of which 2 were waited for; matrix products, arithmetic and copies ran while one was open for 18% of the time, Pallas kernels for 0%

commit v1 on v0

v1 whole, which is shorter than its diff:
```python
import functools

import jax
import jax.numpy as jnp
from jax import lax
from jax.experimental import pallas as pl
from jax.experimental.pallas import tpu as pltpu
from jax.sharding import PartitionSpec as P

NB = 32
NF = 64
NQ = 64

HUBBARD = 2.0
TEMPER = 0.25
PI_VALUE = 3.141592653589793

AXES = ("tq", "slab")
DEVICES = 128
CAP = 3
ROWS = 256
WIDTH = 4096
LANES = 128
TILES = WIDTH // LANES
CHUNK = CAP * TILES
SIDE = 4
MIB = 1024 * 1024


def bubble(band_pair, band_own, bose_freq):
    fermi_freq = (
        PI_VALUE
        * TEMPER
        * (2.0 * (jnp.arange(NF, dtype=jnp.int32) - NF // 2).astype(jnp.float32) + 1.0)
    )
    other_freq = bose_freq[:, None] - fermi_freq[None, :]
    numerator = (
        band_own[None, :, None] * band_pair[:, :, None]
        - (fermi_freq[None, :] * other_freq)[:, None, :]
    )
    left_denom = fermi_freq[None, None, :] ** 2 + band_own[None, :, None] ** 2
    right_denom = other_freq[:, None, :] ** 2 + band_pair[:, :, None] ** 2
    values = TEMPER * numerator / (left_denom * right_denom)
    return values.reshape(band_pair.shape[0], NQ * NF)


def pairs_along(axis_of_core, step):
    pairs = []
    for tq in range(8):
        axis = axis_of_core[tq % 2]
        for x in range(SIDE):
            for y in range(SIDE):
                to_x = (x + step) % SIDE if axis == 0 else x
                to_y = (y + step) % SIDE if axis == 1 else y
                pairs.append(((tq * SIDE + x) * SIDE + y, (tq * SIDE + to_x) * SIDE + to_y))
    return pairs


def move_g(array, step):
    return lax.ppermute(array, AXES, pairs_along((0, 1), step))


def move_h(array, step):
    return lax.ppermute(array, AXES, pairs_along((1, 0), step))


def place_kernel(target_ref, shift_ref, rows_ref, out_ref, wide):
    dest = target_ref[...] // ROWS
    member = lax.broadcasted_iota(jnp.int32, (DEVICES, ROWS), 0) == dest
    before = (
        lax.broadcasted_iota(jnp.int32, (ROWS, ROWS), 0)
        < lax.broadcasted_iota(jnp.int32, (ROWS, ROWS), 1)
    ).astype(jnp.bfloat16)
    count = jnp.dot(
        member.astype(jnp.bfloat16), before, preferred_element_type=jnp.float32
    ).astype(jnp.int32)
    placer = jnp.concatenate(
        [(member & (count == k)).astype(jnp.bfloat16) for k in range(CAP)], axis=0
    )
    lane = lax.broadcasted_iota(jnp.int32, (ROWS, LANES), 1)
    from_freq = lane % NF - shift_ref[...]
    valid = (from_freq >= 0) & (from_freq < NF)
    from_lane = jnp.where(valid, lane - shift_ref[...], lane)
    for pair in range(TILES // 2):
        moved = []
        for tile in (2 * pair, 2 * pair + 1):
            block = rows_ref[:, tile * LANES : (tile + 1) * LANES].astype(jnp.float32)
            block = jnp.take_along_axis(block, from_lane, axis=1, mode="promise_in_bounds")
            moved.append(jnp.where(valid, block, 0.0).astype(jnp.bfloat16))
        placed = jnp.dot(
            placer, jnp.concatenate(moved, axis=1), preferred_element_type=jnp.float32
        )
        for k in range(CAP):
            for half in range(2):
                wide[pl.ds(k * TILES + 2 * pair + half, DEVICES, stride=CHUNK), :] = placed[
                    k * DEVICES : (k + 1) * DEVICES, half * LANES : (half + 1) * LANES
                ]

    @pl.loop(0, DEVICES // 4)
    def _(step):
        part = wide[pl.ds(pl.multiple_of(step * 4 * CHUNK, 4 * CHUNK), 4 * CHUNK), :]
        out_ref[pl.ds(pl.multiple_of(step * 4 * CHUNK, 4 * CHUNK), 4 * CHUNK), :] = part.astype(
            jnp.bfloat16
        )


def collect_kernel(
    where_ref, target_ref, bubble_ref, box_ref, gamma_ref, w0, w1, w2, w3, wide
):
    me, g, h, along_x, along_y = (where_ref[i] for i in range(5))
    target = target_ref[...]
    member = target // ROWS == me
    before = (
        lax.broadcasted_iota(jnp.int32, (ROWS, ROWS), 0)
        > lax.broadcasted_iota(jnp.int32, (ROWS, ROWS), 1)
    ).astype(jnp.bfloat16)
    count = jnp.dot(
        before, member.astype(jnp.bfloat16), preferred_element_type=jnp.float32
    ).astype(jnp.int32)
    row_of = lax.broadcasted_iota(jnp.int32, (ROWS, DEVICES), 0) + 1
    parts = []
    for k in range(CAP):
        local = jnp.sum(
            jnp.where(member & (count == k), target % ROWS + 1, 0), axis=0, keepdims=True
        )
        parts.append((row_of == local).astype(jnp.bfloat16))
    collector = jnp.concatenate(parts, axis=1)

    @pl.loop(0, DEVICES // 4)
    def _(step):
        rows = pl.ds(pl.multiple_of(step * 4 * CHUNK, 4 * CHUNK), 4 * CHUNK)
        wide[rows, :] = box_ref[rows, :].astype(jnp.float32)

    for d, w_ref in enumerate((w0, w1, w2, w3)):
        for o in range(SIDE):
            slab = ((g + o) % SIDE) * along_x + ((h + d) % SIDE) * along_y
            columns = pl.ds(pl.multiple_of(slab * ROWS, ROWS), ROWS)
            came = []
            for k in range(CAP):
                halves = [
                    wide[pl.ds(k * TILES + slab * 2 + half, DEVICES, stride=CHUNK), :]
                    for half in range(2)
                ]
                came.append(jnp.concatenate(halves, axis=1).astype(jnp.bfloat16))
            summed = jnp.dot(
                collector, jnp.concatenate(came, axis=0), preferred_element_type=jnp.float32
            )
            gamma = HUBBARD + summed
            gamma_ref[:, columns] = gamma
            w_ref[o] = (gamma * bubble_ref[:, columns]).astype(jnp.bfloat16)


def ladder_kernel(a_ref, own_ref, left_ref, right_ref, far_top_ref, far_low_ref, out_ref):
    total = jnp.dot(a_ref[0], own_ref[...], preferred_element_type=jnp.float32)
    total += jnp.dot(a_ref[1], right_ref[...], preferred_element_type=jnp.float32)
    far = jnp.concatenate([far_top_ref[...], far_low_ref[...]], axis=0)
    total += jnp.dot(a_ref[2], far, preferred_element_type=jnp.float32)
    total += jnp.dot(a_ref[3], left_ref[...], preferred_element_type=jnp.float32)
    out_ref[...] = total.astype(out_ref.dtype)


def part_ladder(weighted, full_parts, dtype):
    cut = 1024

    def columns(rows):
        return pl.BlockSpec((rows, cut), lambda n: (0, n))

    return pl.pallas_call(
        ladder_kernel,
        grid=(WIDTH // cut,),
        in_specs=[pl.BlockSpec((SIDE, ROWS, ROWS), lambda n: (0, 0, 0))]
        + [columns(part.shape[0]) for part in full_parts],
        out_specs=columns(ROWS),
        out_shape=jax.ShapeDtypeStruct((ROWS, WIDTH), dtype),
        compiler_params=pltpu.CompilerParams(vmem_limit_bytes=32 * MIB),
        cost_estimate=pl.CostEstimate(
            flops=2 * ROWS * 4 * ROWS * WIDTH, bytes_accessed=11 * MIB, transcendentals=0
        ),
        name="part_ladder",
    )(weighted, *full_parts)


def per_device(vert_ph, full_pp, target, shift, trans_mom, trans_bose, energies, pair_table):
    tq = lax.axis_index("tq")
    slab = lax.axis_index("slab")
    core = tq % 2
    x, y = slab // SIDE, slab % SIDE
    g = jnp.where(core == 0, x, y)
    h = jnp.where(core == 0, y, x)
    along_g = jnp.where(core == 0, SIDE, 1)
    where = jnp.stack([tq * 16 + slab, g, h, along_g, SIDE + 1 - along_g]).astype(jnp.int32)

    full = full_pp.reshape(ROWS, WIDTH)
    left = move_g(full, 1)
    right = move_g(full, 3)
    far_top = move_g(left[: ROWS // 2], 1)
    far_low = move_g(right[ROWS // 2 :], 3)
    full_parts = (full, left, right, far_top, far_low)

    all_target = lax.all_gather(target, AXES, axis=0, tiled=True)

    whole = pl.BlockSpec(memory_space=pltpu.VMEM)
    payload = pl.pallas_call(
        place_kernel,
        in_specs=[whole] * 3,
        out_specs=whole,
        out_shape=jax.ShapeDtypeStruct((DEVICES * CHUNK, LANES), jnp.bfloat16),
        scratch_shapes=[pltpu.VMEM((DEVICES * CHUNK, LANES), jnp.float32)],
        compiler_params=pltpu.CompilerParams(vmem_limit_bytes=32 * MIB),
        cost_estimate=pl.CostEstimate(
            flops=2 * 384 * ROWS * WIDTH, bytes_accessed=5 * MIB, transcendentals=0
        ),
        name="place",
    )(target, shift.reshape(ROWS, 1), vert_ph.reshape(ROWS, WIDTH))
    arrived = lax.all_to_all(
        payload.reshape(DEVICES, CHUNK, LANES), AXES, split_axis=0, concat_axis=0, tiled=True
    ).reshape(DEVICES * CHUNK, LANES)

    pick_mom = (trans_mom[:, None] == jnp.arange(NQ, dtype=jnp.int32)[None, :]).astype(jnp.float32)
    pair_rows = jnp.dot(pick_mom, pair_table.astype(jnp.float32), precision=lax.Precision.HIGHEST)
    picker = (
        pair_rows[:, :, None] == jnp.arange(NQ, dtype=jnp.int32).astype(jnp.float32)[None, None, :]
    ).astype(jnp.float32)
    band_pair = jnp.einsum("qkl,l->qk", picker, energies, precision=lax.Precision.HIGHEST)
    bose_freq = 2.0 * PI_VALUE * TEMPER * (trans_bose - NB // 2).astype(jnp.float32)
    pair_bubble = bubble(band_pair, energies, bose_freq)

    block = jax.ShapeDtypeStruct((SIDE, ROWS, ROWS), jnp.bfloat16)
    gamma, own, w1, w2, w3 = pl.pallas_call(
        collect_kernel,
        in_specs=[pl.BlockSpec(memory_space=pltpu.SMEM)] + [whole] * 3,
        out_specs=[whole] * 5,
        out_shape=[jax.ShapeDtypeStruct((ROWS, WIDTH), jnp.float32)] + [block] * 4,
        scratch_shapes=[pltpu.VMEM((DEVICES * CHUNK, LANES), jnp.float32)],
        compiler_params=pltpu.CompilerParams(vmem_limit_bytes=40 * MIB),
        cost_estimate=pl.CostEstimate(
            flops=2 * 384 * ROWS * WIDTH, bytes_accessed=9 * MIB, transcendentals=0
        ),
        name="collect",
    )(where, all_target.T, pair_bubble, arrived)

    ladder_parts = []
    for d, sent in ((2, w2), (1, w1), (3, w3)):
        part = part_ladder(move_h(sent, d), full_parts, jnp.bfloat16)
        ladder_parts.append(move_h(part, SIDE - d))
    ladder = part_ladder(own, full_parts, jnp.float32)
    for part in ladder_parts:
        ladder = ladder + part.astype(jnp.float32)
    return gamma[None], ladder[None]


def solution(mesh):
    in_specs = (
        P("tq", "slab", None),
        P("tq", "slab", None),
        P("tq", "slab"),
        P("tq", "slab"),
        P("tq"),
        P("tq"),
        P(),
        P(),
    )
    out_specs = (P("tq", "slab", None), P("tq", "slab", None))
    return jax.shard_map(
        per_device, mesh=mesh, in_specs=in_specs, out_specs=out_specs, check_vma=False
    )
```

time: 275 us -> 228 us (0.83)
  waiting for transfers between devices: 170 us -> 90 us
  blocking collectives: 0 us -> 63.7 us
  Pallas kernels: 0 us -> 35.4 us
  matrix products: 31.2 us -> 0.32 us
  local copies, waits for them, and re-layouts: 30.8 us -> 7.51 us
  between operations: 15.5 us -> 2.17 us
  starting transfers between devices: 21.5 us -> 25.1 us
    ppermute x0 -> x10, waiting for transfers between devices: none -> 89.9 us  [the longest x4 52.3 us: move_g(): return lax.ppermute(array, AXES, pairs_along((0, 1), step))]
    all_to_all x2 -> x1, waiting for transfers between devices: 85.9 us -> 0.01 us  [per_device(): lax.all_to_all(payload.reshape(DEVICES, CHUNK, LANES), AXES, split_axis=0...]
    all_gather x1 -> x0, waiting for transfers between devices: 83.7 us -> none  [per_device(): lax.all_gather(full_pp, 'slab', axis=1, tiled=True)]
    all_gather x0 -> x1, blocking collectives: none -> 63.7 us  [per_device(): all_target = lax.all_gather(target, AXES, axis=0, tiled=True)]
    pallas_call x0 -> x6, Pallas kernels: none -> 35.4 us  [the longest x4 18.8 us: part_ladder(): pl.pallas_call(ladder_kernel, grid=(WIDTH // cut,), in_specs=[pl.BlockSpe...]
    dot_general x5 -> x0, matrix products: 30.9 us -> none  [the longest x1 17.5 us: per_device(): jnp.einsum('tnm,tmp->tnp', weighted, lax.all_gather(full_pp, 'slab', axis...]
    reshape x3 -> x1, local copies, waits for them, and re-layouts: 17 us -> 0.81 us  [per_device(): shift.reshape(ROWS, 1)]
    ppermute x0 -> x10, starting transfers between devices: none -> 13.5 us  [the longest x6 9.33 us: move_h(): return lax.ppermute(array, AXES, pairs_along((1, 0), step))]
  transfers between devices with their start and end apart: 3 -> 11, of which waited for: 2 -> 4; matrix products, arithmetic and copies ran while one was open for 18% -> 2% of each run, Pallas kernels for 0% -> 12%
where the time goes in v1:
time: 228 us
  waiting for transfers between devices  90 us (39%)
  blocking collectives  63.7 us (28%)
  Pallas kernels  35.4 us (16%)
  starting transfers between devices  25.1 us (11%)
  local copies, waits for them, and re-layouts  7.51 us (3%)
  other arithmetic  3.35 us (1%)
    all_gather x1, blocking collectives, per_device(): all_target = lax.all_gather(target, AXES, axis=0, tiled=True)  63.7 us
    ppermute x4, waiting for transfers between devices, move_g(): return lax.ppermute(array, AXES, pairs_along((0, 1), step))  52.3 us
    ppermute x6, waiting for transfers between devices, move_h(): return lax.ppermute(array, AXES, pairs_along((1, 0), step))  37.7 us
    pallas_call x4, Pallas kernels, part_ladder(): pl.pallas_call(ladder_kernel, grid=(WIDTH // cut,), in_specs=[pl.BlockSpe...  18.8 us
    all_to_all x1, starting transfers between devices, per_device(): lax.all_to_all(payload.reshape(DEVICES, CHUNK, LANES), AXES, split_axis=0...  11.6 us
    pallas_call x1, Pallas kernels, per_device(): pl.pallas_call(collect_kernel, in_specs=[pl.BlockSpec(memory_space=pltpu....  9.51 us
    ppermute x6, starting transfers between devices, move_h(): return lax.ppermute(array, AXES, pairs_along((1, 0), step))  9.33 us
    pallas_call x1, Pallas kernels, per_device(): pl.pallas_call(place_kernel, in_specs=[whole] * 3, out_specs=whole, out_s...  7.05 us
  transfers between devices with their start and end apart: 11, of which 4 were waited for; matrix products, arithmetic and copies ran while one was open for 2% of the time, Pallas kernels for 12%

profile of v1, /device:TPU:0, one launch (start us, length us, event | category | flops | bytes accessed | tf_op | source)
XLA Modules:
  0.0 227.5 jit_solution(11130052119943890682)
XLA Ops:
  0.6 0.8 copy.13.shift_ref
  1.5 1.6 copy-done.1
  3.7 7.1 %place.1 = bf16[12288,128]{1,0:T(8,128)(2,1)} custom-call(s32[1,256]{1,0:T(1,128)S(1)} %copy-done.2, s32[256,1]{1,0:T(8,128)S(1)} %copy.13.shift_ref, bf16[256,4096]{1,0:T(8,128)(2,1)S(1)} %bitcast.44), custom_call_target="tpu_custom_call" | custom-call | flops 805306368 | bytes 5242880 | tf_op jit(solution)/shard_map/place/pallas_call | solution.py:203
  10.8 11.6 %all-to-all-start = ((bf16[128,96,128]{2,1,0:T(8,128)(2,1)}), bf16[128,96,128]{2,1,0:T(8,128)(2,1)}, u32[]{:S(2)}, u32[]{:S(2)}) async-start(bf16[128,96,128]{2,1,0:T(8,128)(2,1)} %bitcast.16), calls=%async_computation | async-start | bytes 6291456 | tf_op jit(solution)/shard_map/all_to_all | solution.py:215
  22.4 2.2 collective-permute-start.1
  27.1 52.3 %collective-permute-done.1.right_ref = bf16[256,4096]{1,0:T(8,128)(2,1)S(1)} collective-permute-done((bf16[256,4096]{1,0:T(8,128)(2,1)}, bf16[256,4096]{1,0:T(8,128)(2,1)S(1)}, u32[]{:S(2)}, u32[]{:S(2)}) %collective-permute-start.1) | collective-permute-done | bytes 2097184 | tf_op jit(solution)/shard_map/ppermute | solution.py:60
  79.4 1.1 slice.9
  80.5 1.6 collective-permute-start.3
  82.1 2.3 %slice.8 = bf16[128,4096]{1,0:T(8,128)(2,1)} slice(bf16[256,4096]{1,0:T(8,128)(2,1)} %collective-permute-done.left_ref), slice={[0:128], [0:4096]} | slice | bytes 2097152 | tf_op jit(solution)/shard_map/slice | solution.py:196
  85.0 63.7 %all-gather = s32[128,1,256]{2,1,0:T(1,128)S(1)} all-gather(s32[1,1,256]{2,1,0:T(1,128)S(1)} %bitcast.46), channel_id=1, replica_groups=mesh['tq'=8,'slab'=16] {'tq','slab'}, dimensions={0}, use_global_device_ids=true | all-gather | bytes 132096 | tf_op jit(solution)/shard_map/all_gather | solution.py:200
  148.8 9.5 %collect.1 = (f32[256,4096]{1,0:T(8,128)}, bf16[4,256,256]{2,1,0:T(8,128)(2,1)S(1)}, bf16[4,256,256]{2,1,0:T(8,128)(2,1)S(1)}, bf16[4,256,256]{2,1,0:T(8,128)(2,1)S(1)}, bf16[4,256,256]{2,1,0:T(8,128)(2,1)S(1)}) custom-call(s32[5]{0:T(128)S(1)} %stack.23.where_ref, s32[256,128]{1,0:T(8,128)S(1)} %bitcast.45, f32[1,4096]{1,0:T(1,128)S(1)} %multiply_divide_fusion.bubble_ref, ...), custom_call_target="tpu_custom_call" | custom-call | flops 805306368 | bytes 9437184 | tf_op jit(solution)/shard_map/collect/pallas_call | solution.py:229
  158.3 1.5 collective-permute-start.4
  159.8 2.3 %collective-permute-start.6 = (bf16[4,256,256]{2,1,0:T(8,128)(2,1)S(1)}, bf16[4,256,256]{2,1,0:T(8,128)(2,1)S(1)}, u32[]{:S(2)}, u32[]{:S(2)}) collective-permute-start(bf16[4,256,256]{2,1,0:T(8,128)(2,1)S(1)} %get-tuple-element.10), channel_id=1, source_target_pairs={{0,1},{1,2},{2,3},{3,0},{4,5},{5,6},{6,7},{7,4},{8,9},{9,10},{10,1... | collective-permute-start | bytes 1572872 | tf_op jit(solution)/shard_map/ppermute | solution.py:64
  162.1 0.9 collective-permute-start.8
  163.1 6.1 %collective-permute-done.4.a_ref = bf16[4,256,256]{2,1,0:T(8,128)(2,1)S(1)} collective-permute-done((bf16[4,256,256]{2,1,0:T(8,128)(2,1)S(1)}, bf16[4,256,256]{2,1,0:T(8,128)(2,1)S(1)}, u32[]{:S(2)}, u32[]{:S(2)}) %collective-permute-start.4) | collective-permute-done | bytes 524320 | tf_op jit(solution)/shard_map/ppermute | solution.py:64
  169.1 4.7 %part_ladder.5 = bf16[256,4096]{1,0:T(8,128)(2,1)S(1)} custom-call(bf16[4,256,256]{2,1,0:T(8,128)(2,1)S(1)} %collective-permute-done.4.a_ref, bf16[256,4096]{1,0:T(8,128)(2,1)S(1)} %bitcast.40, bf16[256,4096]{1,0:T(8,128)(2,1)} %collective-permute-done.left_ref, bf16[256,4096]{1,0:T(8,128)(2,1)S(1)} %collective-permute-done.1.right_ref, ...), custom_call_target="tpu_custom_call" | custom-call | flops 2147483648 | bytes 11534336 | tf_op jit(solution)/shard_map/part_ladder/pallas_call | solution.py:168
  173.8 1.6 collective-permute-start.5
  175.4 4.7 %part_ladder.6 = bf16[256,4096]{1,0:T(8,128)(2,1)S(1)} custom-call(bf16[4,256,256]{2,1,0:T(8,128)(2,1)S(1)} %collective-permute-done.6.a_ref, bf16[256,4096]{1,0:T(8,128)(2,1)S(1)} %bitcast.41, bf16[256,4096]{1,0:T(8,128)(2,1)} %collective-permute-done.left_ref, bf16[256,4096]{1,0:T(8,128)(2,1)S(1)} %collective-permute-done.1.right_ref, ...), custom_call_target="tpu_custom_call" | custom-call | flops 2147483648 | bytes 11534336 | tf_op jit(solution)/shard_map/part_ladder/pallas_call | solution.py:168
  180.1 3.0 %collective-permute-start.7 = (bf16[256,4096]{1,0:T(8,128)(2,1)S(1)}, bf16[256,4096]{1,0:T(8,128)(2,1)S(1)}, u32[]{:S(2)}, u32[]{:S(2)}) collective-permute-start(bf16[256,4096]{1,0:T(8,128)(2,1)S(1)} %part_ladder.6), channel_id=1, source_target_pairs={{0,3},{1,0},{2,1},{3,2},{4,7},{5,4},{6,5},{7,6},{8,11},{9,8},{10,9... | collective-permute-start | bytes 6291464 | tf_op jit(solution)/shard_map/ppermute | solution.py:64
  183.1 4.7 %part_ladder.7 = bf16[256,4096]{1,0:T(8,128)(2,1)S(1)} custom-call(bf16[4,256,256]{2,1,0:T(8,128)(2,1)S(1)} %collective-permute-done.8.a_ref, bf16[256,4096]{1,0:T(8,128)(2,1)S(1)} %bitcast.42, bf16[256,4096]{1,0:T(8,128)(2,1)} %collective-permute-done.left_ref, bf16[256,4096]{1,0:T(8,128)(2,1)S(1)} %collective-permute-done.1.right_ref, ...), custom_call_target="tpu_custom_call" | custom-call | flops 2147483648 | bytes 11534336 | tf_op jit(solution)/shard_map/part_ladder/pallas_call | solution.py:168
  187.8 4.8 %part_ladder.4 = f32[256,4096]{1,0:T(8,128)S(1)} custom-call(bf16[4,256,256]{2,1,0:T(8,128)(2,1)S(1)} %get-tuple-element.8.a_ref, bf16[256,4096]{1,0:T(8,128)(2,1)S(1)} %bitcast.43, bf16[256,4096]{1,0:T(8,128)(2,1)} %collective-permute-done.left_ref, bf16[256,4096]{1,0:T(8,128)(2,1)S(1)} %collective-permute-done.1.right_ref, ...), custom_call_target="tpu_custom_call" | custom-call | flops 2147483648 | bytes 11534336 | tf_op jit(solution)/shard_map/part_ladder/pallas_call | solution.py:168
  192.6 8.9 %collective-permute-done.5 = bf16[256,4096]{1,0:T(8,128)(2,1)S(1)} collective-permute-done((bf16[256,4096]{1,0:T(8,128)(2,1)S(1)}, bf16[256,4096]{1,0:T(8,128)(2,1)S(1)}, u32[]{:S(2)}, u32[]{:S(2)}) %collective-permute-start.5) | collective-permute-done | bytes 2097184 | tf_op jit(solution)/shard_map/ppermute | solution.py:64
  201.6 22.7 %collective-permute-done.7 = bf16[256,4096]{1,0:T(8,128)(2,1)S(1)} collective-permute-done((bf16[256,4096]{1,0:T(8,128)(2,1)S(1)}, bf16[256,4096]{1,0:T(8,128)(2,1)S(1)}, u32[]{:S(2)}, u32[]{:S(2)}) %collective-permute-start.7) | collective-permute-done | bytes 2097184 | tf_op jit(solution)/shard_map/ppermute | solution.py:64
  224.2 3.3 %add_bitcast_fusion = f32[1,256,4096]{2,1,0:T(8,128)} fusion(bf16[256,4096]{1,0:T(8,128)(2,1)S(1)} %collective-permute-done.9, bf16[256,4096]{1,0:T(8,128)(2,1)S(1)} %collective-permute-done.7, f32[256,4096]{1,0:T(8,128)S(1)} %part_ladder.4, bf16[256,4096]{1,0:T(8,128)(2,1)S(1)} %collective-permute-done.5), kind=kLoop, calls=%fused_computation | loop fusion | flops 6291456 | bytes 14680064 | tf_op jit(solution)/shard_map/broadcast_in_dim | solution.py:249
  (41 shorter events, 2.6 us)
Async XLA Ops:
  1.4 1.6 copy-start.1
  3.0 0.7 copy-start.2
  10.8 15.2 %copy-start.4 = (s32[64,64]{1,0:T(8,128)S(1)}, s32[64,64]{1,0:T(8,128)}, u32[]{:S(2)}) copy-start(s32[64,64]{1,0:T(8,128)} %param.15) | copy-start | bytes 49156
  10.8 15.4 %copy-start.5 = (f32[64]{0:T(128)S(1)}, f32[64]{0:T(128)}, u32[]{:S(2)}) copy-start(f32[64]{0:T(128)} %param.14) | copy-start | bytes 772
  10.8 138.1 %all-to-all-start = ((bf16[128,96,128]{2,1,0:T(8,128)(2,1)}), bf16[128,96,128]{2,1,0:T(8,128)(2,1)}, u32[]{:S(2)}, u32[]{:S(2)}) async-start(bf16[128,96,128]{2,1,0:T(8,128)(2,1)} %bitcast.16), calls=%async_computation | async-start | bytes 6291456 | tf_op jit(solution)/shard_map/all_to_all | solution.py:215
  22.4 57.0 %collective-permute-start.1 = (bf16[256,4096]{1,0:T(8,128)(2,1)}, bf16[256,4096]{1,0:T(8,128)(2,1)S(1)}, u32[]{:S(2)}, u32[]{:S(2)}) collective-permute-start(bf16[256,4096]{1,0:T(8,128)(2,1)} %bitcast.38), channel_id=1, source_target_pairs={{0,12},{1,13},{2,14},{3,15},{4,0},{5,1},{6,2},{7,3},{8,4},{9,5},{1... | collective-permute-start | bytes 6291464 | tf_op jit(solution)/shard_map/ppermute | solution.py:60
  24.6 57.5 %collective-permute-start = (bf16[256,4096]{1,0:T(8,128)(2,1)}, bf16[256,4096]{1,0:T(8,128)(2,1)}, u32[]{:S(2)}, u32[]{:S(2)}) collective-permute-start(bf16[256,4096]{1,0:T(8,128)(2,1)} %bitcast.39), channel_id=1, source_target_pairs={{0,4},{1,5},{2,6},{3,7},{4,8},{5,9},{6,10},{7,11},{8,12},{9,13},{1... | collective-permute-start | bytes 6291464 | tf_op jit(solution)/shard_map/ppermute | solution.py:60
  27.1 57.8 %copy-start.3 = (s32[1,256]{1,0:T(1,128)S(1)}, s32[1,256]{1,0:T(1,128)}, u32[]{:S(2)}) copy-start(s32[1,256]{1,0:T(1,128)} %target_ref.1) | copy-start | bytes 3076
  80.5 82.5 %collective-permute-start.3 = (bf16[128,4096]{1,0:T(8,128)(2,1)}, bf16[128,4096]{1,0:T(8,128)(2,1)S(1)}, u32[]{:S(2)}, u32[]{:S(2)}) collective-permute-start(bf16[128,4096]{1,0:T(8,128)(2,1)} %slice.9), channel_id=1, source_target_pairs={{0,12},{1,13},{2,14},{3,15},{4,0},{5,1},{6,2},{7,3},{8,4},{9,5},{1... | collective-permute-start | bytes 3145736 | tf_op jit(solution)/shard_map/ppermute | solution.py:60
  84.4 78.7 %collective-permute-start.2 = (bf16[128,4096]{1,0:T(8,128)(2,1)}, bf16[128,4096]{1,0:T(8,128)(2,1)}, u32[]{:S(2)}, u32[]{:S(2)}) collective-permute-start(bf16[128,4096]{1,0:T(8,128)(2,1)} %slice.8), channel_id=1, source_target_pairs={{0,4},{1,5},{2,6},{3,7},{4,8},{5,9},{6,10},{7,11},{8,12},{9,13},{1... | collective-permute-start | bytes 3145736 | tf_op jit(solution)/shard_map/ppermute | solution.py:60
  148.8 20.3 %copy-start = (bf16[1,256,4096]{2,1,0:T(8,128)(2,1)S(1)}, bf16[1,256,4096]{2,1,0:T(8,128)(2,1)}, u32[]{:S(2)}) copy-start(bf16[1,256,4096]{2,1,0:T(8,128)(2,1)} %param.9) | copy-start | bytes 6291460
  158.3 10.8 %collective-permute-start.4 = (bf16[4,256,256]{2,1,0:T(8,128)(2,1)S(1)}, bf16[4,256,256]{2,1,0:T(8,128)(2,1)S(1)}, u32[]{:S(2)}, u32[]{:S(2)}) collective-permute-start(bf16[4,256,256]{2,1,0:T(8,128)(2,1)S(1)} %get-tuple-element.9), channel_id=1, source_target_pairs={{0,2},{1,3},{2,0},{3,1},{4,6},{5,7},{6,4},{7,5},{8,10},{9,11},{10,... | collective-permute-start | bytes 1572872 | tf_op jit(solution)/shard_map/ppermute | solution.py:64
  159.8 15.6 %collective-permute-start.6 = (bf16[4,256,256]{2,1,0:T(8,128)(2,1)S(1)}, bf16[4,256,256]{2,1,0:T(8,128)(2,1)S(1)}, u32[]{:S(2)}, u32[]{:S(2)}) collective-permute-start(bf16[4,256,256]{2,1,0:T(8,128)(2,1)S(1)} %get-tuple-element.10), channel_id=1, source_target_pairs={{0,1},{1,2},{2,3},{3,0},{4,5},{5,6},{6,7},{7,4},{8,9},{9,10},{10,1... | collective-permute-start | bytes 1572872 | tf_op jit(solution)/shard_map/ppermute | solution.py:64
  162.1 20.9 %collective-permute-start.8 = (bf16[4,256,256]{2,1,0:T(8,128)(2,1)S(1)}, bf16[4,256,256]{2,1,0:T(8,128)(2,1)S(1)}, u32[]{:S(2)}, u32[]{:S(2)}) collective-permute-start(bf16[4,256,256]{2,1,0:T(8,128)(2,1)S(1)} %get-tuple-element.11), channel_id=1, source_target_pairs={{0,3},{1,0},{2,1},{3,2},{4,7},{5,4},{6,5},{7,6},{8,11},{9,8},{10,9... | collective-permute-start | bytes 1572872 | tf_op jit(solution)/shard_map/ppermute | solution.py:64
  173.8 27.7 %collective-permute-start.5 = (bf16[256,4096]{1,0:T(8,128)(2,1)S(1)}, bf16[256,4096]{1,0:T(8,128)(2,1)S(1)}, u32[]{:S(2)}, u32[]{:S(2)}) collective-permute-start(bf16[256,4096]{1,0:T(8,128)(2,1)S(1)} %part_ladder.5), channel_id=1, source_target_pairs={{0,2},{1,3},{2,0},{3,1},{4,6},{5,7},{6,4},{7,5},{8,10},{9,11},{10,... | collective-permute-start | bytes 6291464 | tf_op jit(solution)/shard_map/ppermute | solution.py:64
  180.1 44.1 %collective-permute-start.7 = (bf16[256,4096]{1,0:T(8,128)(2,1)S(1)}, bf16[256,4096]{1,0:T(8,128)(2,1)S(1)}, u32[]{:S(2)}, u32[]{:S(2)}) collective-permute-start(bf16[256,4096]{1,0:T(8,128)(2,1)S(1)} %part_ladder.6), channel_id=1, source_target_pairs={{0,3},{1,0},{2,1},{3,2},{4,7},{5,4},{6,5},{7,6},{8,11},{9,8},{10,9... | collective-permute-start | bytes 6291464 | tf_op jit(solution)/shard_map/ppermute | solution.py:64
  187.7 36.5 %collective-permute-start.9 = (bf16[256,4096]{1,0:T(8,128)(2,1)S(1)}, bf16[256,4096]{1,0:T(8,128)(2,1)S(1)}, u32[]{:S(2)}, u32[]{:S(2)}) collective-permute-start(bf16[256,4096]{1,0:T(8,128)(2,1)S(1)} %part_ladder.7), channel_id=1, source_target_pairs={{0,1},{1,2},{2,3},{3,0},{4,5},{5,6},{6,7},{7,4},{8,9},{9,10},{10,1... | collective-permute-start | bytes 6291464 | tf_op jit(solution)/shard_map/ppermute | solution.py:64

commit v2 on v1

--- a/solution.py
+++ b/solution.py
@@ -22,7 +22,8 @@
 WIDTH = 4096
 LANES = 128
 TILES = WIDTH // LANES
-CHUNK = CAP * TILES
+LABELS = CAP * TILES
+CHUNK = LABELS + 8
 SIDE = 4
 MIB = 1024 * 1024
 
@@ -96,6 +97,18 @@
                     k * DEVICES : (k + 1) * DEVICES, half * LANES : (half + 1) * LANES
                 ]
 
+    codes = lax.dot_general(
+        placer,
+        jnp.broadcast_to(target_ref[...] % ROWS + 1, (LANES, ROWS)).astype(jnp.bfloat16),
+        (((1,), (1,)), ((), ())),
+        preferred_element_type=jnp.float32,
+    )
+    column = lax.broadcasted_iota(jnp.int32, (DEVICES, LANES), 1)
+    label = jnp.zeros((DEVICES, LANES), jnp.float32)
+    for k in range(CAP):
+        label = jnp.where(column == k, codes[k * DEVICES : (k + 1) * DEVICES], label)
+    wide[pl.ds(LABELS, DEVICES, stride=CHUNK), :] = label
+
     @pl.loop(0, DEVICES // 4)
     def _(step):
         part = wide[pl.ds(pl.multiple_of(step * 4 * CHUNK, 4 * CHUNK), 4 * CHUNK), :]
@@ -105,35 +118,23 @@
 
 
 def collect_kernel(
-    where_ref, target_ref, bubble_ref, box_ref, gamma_ref, w0, w1, w2, w3, wide
+    where_ref, bubble_ref, box_ref, gamma_ref, w0, w1, w2, w3, wide
 ):
-    me, g, h, along_x, along_y = (where_ref[i] for i in range(5))
-    target = target_ref[...]
-    member = target // ROWS == me
-    before = (
-        lax.broadcasted_iota(jnp.int32, (ROWS, ROWS), 0)
-        > lax.broadcasted_iota(jnp.int32, (ROWS, ROWS), 1)
-    ).astype(jnp.bfloat16)
-    count = jnp.dot(
-        before, member.astype(jnp.bfloat16), preferred_element_type=jnp.float32
-    ).astype(jnp.int32)
-    row_of = lax.broadcasted_iota(jnp.int32, (ROWS, DEVICES), 0) + 1
-    parts = []
-    for k in range(CAP):
-        local = jnp.sum(
-            jnp.where(member & (count == k), target % ROWS + 1, 0), axis=0, keepdims=True
-        )
-        parts.append((row_of == local).astype(jnp.bfloat16))
-    collector = jnp.concatenate(parts, axis=1)
-
+    g, h, along_g, along_h = (where_ref[i] for i in range(4))
     @pl.loop(0, DEVICES // 4)
     def _(step):
         rows = pl.ds(pl.multiple_of(step * 4 * CHUNK, 4 * CHUNK), 4 * CHUNK)
         wide[rows, :] = box_ref[rows, :].astype(jnp.float32)
 
+    label = jnp.transpose(wide[pl.ds(LABELS, DEVICES, stride=CHUNK), :]).astype(jnp.int32)
+    row_of = lax.broadcasted_iota(jnp.int32, (ROWS, DEVICES), 0) + 1
+    collector = jnp.concatenate(
+        [(row_of == label[k : k + 1]).astype(jnp.bfloat16) for k in range(CAP)], axis=1
+    )
+
     for d, w_ref in enumerate((w0, w1, w2, w3)):
         for o in range(SIDE):
-            slab = ((g + o) % SIDE) * along_x + ((h + d) % SIDE) * along_y
+            slab = ((g + o) % SIDE) * along_g + ((h + d) % SIDE) * along_h
             columns = pl.ds(pl.multiple_of(slab * ROWS, ROWS), ROWS)
             came = []
             for k in range(CAP):
@@ -150,12 +151,12 @@
             w_ref[o] = (gamma * bubble_ref[:, columns]).astype(jnp.bfloat16)
 
 
-def ladder_kernel(a_ref, own_ref, left_ref, right_ref, far_top_ref, far_low_ref, out_ref):
+def ladder_kernel(a_ref, own_ref, *refs):
+    out_ref = refs[-1]
     total = jnp.dot(a_ref[0], own_ref[...], preferred_element_type=jnp.float32)
-    total += jnp.dot(a_ref[1], right_ref[...], preferred_element_type=jnp.float32)
-    far = jnp.concatenate([far_top_ref[...], far_low_ref[...]], axis=0)
-    total += jnp.dot(a_ref[2], far, preferred_element_type=jnp.float32)
-    total += jnp.dot(a_ref[3], left_ref[...], preferred_element_type=jnp.float32)
+    for o in range(1, SIDE):
+        block = jnp.concatenate([refs[2 * o - 2][...], refs[2 * o - 1][...]], axis=0)
+        total += jnp.dot(a_ref[o], block, preferred_element_type=jnp.float32)
     out_ref[...] = total.astype(out_ref.dtype)
 
 
@@ -188,16 +189,14 @@
     g = jnp.where(core == 0, x, y)
     h = jnp.where(core == 0, y, x)
     along_g = jnp.where(core == 0, SIDE, 1)
-    where = jnp.stack([tq * 16 + slab, g, h, along_g, SIDE + 1 - along_g]).astype(jnp.int32)
+    where = jnp.stack([g, h, along_g, SIDE + 1 - along_g]).astype(jnp.int32)
 
     full = full_pp.reshape(ROWS, WIDTH)
-    left = move_g(full, 1)
-    right = move_g(full, 3)
-    far_top = move_g(left[: ROWS // 2], 1)
-    far_low = move_g(right[ROWS // 2 :], 3)
-    full_parts = (full, left, right, far_top, far_low)
-
-    all_target = lax.all_gather(target, AXES, axis=0, tiled=True)
+    top, low = full[: ROWS // 2], full[ROWS // 2 :]
+    left_top = move_g(top, 1)
+    right_low = move_g(low, 3)
+    left_low = move_g(low, 1)
+    right_top = move_g(top, 3)
 
     whole = pl.BlockSpec(memory_space=pltpu.VMEM)
     payload = pl.pallas_call(
@@ -212,9 +211,15 @@
         ),
         name="place",
     )(target, shift.reshape(ROWS, 1), vert_ph.reshape(ROWS, WIDTH))
+    payload, left_top, right_low = lax.optimization_barrier((payload, left_top, right_low))
     arrived = lax.all_to_all(
         payload.reshape(DEVICES, CHUNK, LANES), AXES, split_axis=0, concat_axis=0, tiled=True
     ).reshape(DEVICES * CHUNK, LANES)
+
+    arrived, left_top, right_low = lax.optimization_barrier((arrived, left_top, right_low))
+    far_top = move_g(left_top, 1)
+    far_low = move_g(right_low, 3)
+    full_parts = (full, right_top, right_low, far_top, far_low, left_top, left_low)
 
     pick_mom = (trans_mom[:, None] == jnp.arange(NQ, dtype=jnp.int32)[None, :]).astype(jnp.float32)
     pair_rows = jnp.dot(pick_mom, pair_table.astype(jnp.float32), precision=lax.Precision.HIGHEST)
@@ -228,7 +233,7 @@
     block = jax.ShapeDtypeStruct((SIDE, ROWS, ROWS), jnp.bfloat16)
     gamma, own, w1, w2, w3 = pl.pallas_call(
         collect_kernel,
-        in_specs=[pl.BlockSpec(memory_space=pltpu.SMEM)] + [whole] * 3,
+        in_specs=[pl.BlockSpec(memory_space=pltpu.SMEM)] + [whole] * 2,
         out_specs=[whole] * 5,
         out_shape=[jax.ShapeDtypeStruct((ROWS, WIDTH), jnp.float32)] + [block] * 4,
         scratch_shapes=[pltpu.VMEM((DEVICES * CHUNK, LANES), jnp.float32)],
@@ -237,7 +242,7 @@
             flops=2 * 384 * ROWS * WIDTH, bytes_accessed=9 * MIB, transcendentals=0
         ),
         name="collect",
-    )(where, all_target.T, pair_bubble, arrived)
+    )(where, pair_bubble, arrived)
 
     ladder_parts = []
     for d, sent in ((2, w2), (1, w1), (3, w3)):

time: 228 us -> 163 us (0.71)
  blocking collectives: 63.7 us -> 0 us
  Pallas kernels: 35.4 us -> 29 us
  waiting for transfers between devices: 90 us -> 94.2 us
  starting transfers between devices: 25.1 us -> 27.8 us
    all_gather x1 -> x0, blocking collectives: 63.7 us -> none  [per_device(): all_target = lax.all_gather(target, AXES, axis=0, tiled=True)]
    all_to_all x1, waiting for transfers between devices: 0.01 us -> 37 us  [per_device(): lax.all_to_all(payload.reshape(DEVICES, CHUNK, LANES), AXES, split_axis=0...]
    ppermute x4 -> x6, waiting for transfers between devices: 52.3 us -> 16.4 us  [move_g(): return lax.ppermute(array, AXES, pairs_along((0, 1), step))]
    pallas_call x1, Pallas kernels: 7.05 us -> 2.58 us  [per_device(): pl.pallas_call(place_kernel, in_specs=[whole] * 3, out_specs=whole, out_s...]
    ppermute x4 -> x6, starting transfers between devices: 4.2 us -> 8.18 us  [move_g(): return lax.ppermute(array, AXES, pairs_along((0, 1), step))]
    pallas_call x1, Pallas kernels: 9.51 us -> 6.29 us  [per_device(): pl.pallas_call(collect_kernel, in_specs=[pl.BlockSpec(memory_space=pltpu....]
    ppermute x6, waiting for transfers between devices: 37.7 us -> 40.8 us  [move_h(): return lax.ppermute(array, AXES, pairs_along((1, 0), step))]
    all_to_all x1, starting transfers between devices: 11.6 us -> 9.07 us  [per_device(): lax.all_to_all(payload.reshape(DEVICES, CHUNK, LANES), AXES, split_axis=0...]
  transfers between devices with their start and end apart: 11 -> 13, of which waited for: 4 -> 7; matrix products, arithmetic and copies ran while one was open for 2% -> 1% of each run, Pallas kernels for 12% -> 18%
where the time goes in v2:
time: 163 us
  waiting for transfers between devices  94.2 us (58%)
  Pallas kernels  29 us (18%)
  starting transfers between devices  27.8 us (17%)
  local copies, waits for them, and re-layouts  5.94 us (4%)
  other arithmetic  3.43 us (2%)
  between operations  2.18 us (1%)
    ppermute x6, waiting for transfers between devices, move_h(): return lax.ppermute(array, AXES, pairs_along((1, 0), step))  40.8 us
    all_to_all x1, waiting for transfers between devices, per_device(): lax.all_to_all(payload.reshape(DEVICES, CHUNK, LANES), AXES, split_axis=0...  37 us
    pallas_call x4, Pallas kernels, part_ladder(): pl.pallas_call(ladder_kernel, grid=(WIDTH // cut,), in_specs=[pl.BlockSpe...  20.2 us
    ppermute x6, waiting for transfers between devices, move_g(): return lax.ppermute(array, AXES, pairs_along((0, 1), step))  16.4 us
    ppermute x6, starting transfers between devices, move_h(): return lax.ppermute(array, AXES, pairs_along((1, 0), step))  10.5 us
    all_to_all x1, starting transfers between devices, per_device(): lax.all_to_all(payload.reshape(DEVICES, CHUNK, LANES), AXES, split_axis=0...  9.07 us
    ppermute x6, starting transfers between devices, move_g(): return lax.ppermute(array, AXES, pairs_along((0, 1), step))  8.18 us
    pallas_call x1, Pallas kernels, per_device(): pl.pallas_call(collect_kernel, in_specs=[pl.BlockSpec(memory_space=pltpu....  6.29 us
  transfers between devices with their start and end apart: 13, of which 7 were waited for; matrix products, arithmetic and copies ran while one was open for 1% of the time, Pallas kernels for 18%

profile of v2, /device:TPU:0, one launch (start us, length us, event | category | flops | bytes accessed | tf_op | source)
XLA Modules:
  0.0 162.9 jit_solution(12025634959755433548)
XLA Ops:
  0.7 3.2 %slice_bitcast_fusion = (bf16[128,4096]{1,0:T(8,128)(2,1)}, bf16[128,4096]{1,0:T(8,128)(2,1)}) fusion(bf16[1,256,4096]{2,1,0:T(8,128)(2,1)} %param.9), kind=kLoop, calls=%fused_computation.3 | loop fusion | bytes 4194304 | tf_op jit(solution)/shard_map/slice | solution.py:195
  3.9 2.8 %collective-permute-start.1 = (bf16[128,4096]{1,0:T(8,128)(2,1)}, bf16[128,4096]{1,0:T(8,128)(2,1)S(1)}, u32[]{:S(2)}, u32[]{:S(2)}) collective-permute-start(bf16[128,4096]{1,0:T(8,128)(2,1)} %get-tuple-element.24), channel_id=1, source_target_pairs={{0,12},{1,13},{2,14},{3,15},{4,0},{5,1},{6,2},{7,3},{8,4},{9,5},{1... | collective-permute-start | bytes 3145736 | tf_op jit(solution)/shard_map/ppermute | solution.py:61
  6.9 2.6 %place.1 = bf16[13312,128]{1,0:T(8,128)(2,1)S(1)} custom-call(s32[1,256]{1,0:T(1,128)S(1)} %copy-done.3, s32[256,1]{1,0:T(8,128)S(1)} %copy.10.shift_ref, bf16[256,4096]{1,0:T(8,128)(2,1)S(1)} %bitcast.42), custom_call_target="tpu_custom_call" | custom-call | flops 805306368 | bytes 5242880 | tf_op jit(solution)/shard_map/place/pallas_call | solution.py:202
  9.5 1.7 %copy-done.1 = bf16[13312,128]{1,0:T(8,128)(2,1)} copy-done((bf16[13312,128]{1,0:T(8,128)(2,1)}, bf16[13312,128]{1,0:T(8,128)(2,1)S(1)}, u32[]{:S(2)}) %copy-start.1) | copy-done | bytes 3407896
  11.2 8.1 %collective-permute-done.1.refs_1_ = bf16[128,4096]{1,0:T(8,128)(2,1)S(1)} collective-permute-done((bf16[128,4096]{1,0:T(8,128)(2,1)}, bf16[128,4096]{1,0:T(8,128)(2,1)S(1)}, u32[]{:S(2)}, u32[]{:S(2)}) %collective-permute-start.1) | collective-permute-done | bytes 1048608 | tf_op jit(solution)/shard_map/ppermute | solution.py:61
  19.4 3.7 %collective-permute-done.refs_4_ = bf16[128,4096]{1,0:T(8,128)(2,1)} collective-permute-done((bf16[128,4096]{1,0:T(8,128)(2,1)}, bf16[128,4096]{1,0:T(8,128)(2,1)}, u32[]{:S(2)}, u32[]{:S(2)}) %collective-permute-start) | collective-permute-done | bytes 1048608 | tf_op jit(solution)/shard_map/ppermute | solution.py:61
  23.1 9.1 %all-to-all-start = ((bf16[128,104,128]{2,1,0:T(8,128)(2,1)}), bf16[128,104,128]{2,1,0:T(8,128)(2,1)}, u32[]{:S(2)}, u32[]{:S(2)}) async-start(bf16[128,104,128]{2,1,0:T(8,128)(2,1)} %bitcast.41), calls=%async_computation | async-start | bytes 6815744 | tf_op jit(solution)/shard_map/all_to_all | solution.py:215
  33.1 2.3 %collective-permute-start.2 = (bf16[128,4096]{1,0:T(8,128)(2,1)}, bf16[128,4096]{1,0:T(8,128)(2,1)}, u32[]{:S(2)}, u32[]{:S(2)}) collective-permute-start(bf16[128,4096]{1,0:T(8,128)(2,1)} %get-tuple-element.25), channel_id=1, source_target_pairs={{0,12},{1,13},{2,14},{3,15},{4,0},{5,1},{6,2},{7,3},{8,4},{9,5},{1... | collective-permute-start | bytes 3145736 | tf_op jit(solution)/shard_map/ppermute | solution.py:61
  38.0 37.0 %all-to-all-done = bf16[128,104,128]{2,1,0:T(8,128)(2,1)} async-done(((bf16[128,104,128]{2,1,0:T(8,128)(2,1)}), bf16[128,104,128]{2,1,0:T(8,128)(2,1)}, u32[]{:S(2)}, u32[]{:S(2)}) %all-to-all-start) | async-done | bytes 3407904 | tf_op jit(solution)/shard_map/all_to_all | solution.py:215
  77.2 6.3 %collect.1 = (f32[256,4096]{1,0:T(8,128)}, bf16[4,256,256]{2,1,0:T(8,128)(2,1)S(1)}, bf16[4,256,256]{2,1,0:T(8,128)(2,1)S(1)}, bf16[4,256,256]{2,1,0:T(8,128)(2,1)S(1)}, bf16[4,256,256]{2,1,0:T(8,128)(2,1)S(1)}) custom-call(s32[4]{0:T(128)S(1)} %pad_add_fusion.where_ref, f32[1,4096]{1,0:T(1,128)S(1)} %multiply_divide_fusion.bubble_ref, ...), custom_call_target="tpu_custom_call" | custom-call | flops 805306368 | bytes 9437184 | tf_op jit(solution)/shard_map/collect/pallas_call | solution.py:234
  83.5 1.3 collective-permute-start.6
  84.8 1.5 collective-permute-start.8
  86.3 1.7 %collective-permute-start.10 = (bf16[4,256,256]{2,1,0:T(8,128)(2,1)S(1)}, bf16[4,256,256]{2,1,0:T(8,128)(2,1)S(1)}, u32[]{:S(2)}, u32[]{:S(2)}) collective-permute-start(bf16[4,256,256]{2,1,0:T(8,128)(2,1)S(1)} %get-tuple-element.23), channel_id=1, source_target_pairs={{0,3},{1,0},{2,1},{3,2},{4,7},{5,4},{6,5},{7,6},{8,11},{9,8},{10,9... | collective-permute-start | bytes 1572872 | tf_op jit(solution)/shard_map/ppermute | solution.py:65
  88.0 11.2 %collective-permute-done.6.a_ref = bf16[4,256,256]{2,1,0:T(8,128)(2,1)S(1)} collective-permute-done((bf16[4,256,256]{2,1,0:T(8,128)(2,1)S(1)}, bf16[4,256,256]{2,1,0:T(8,128)(2,1)S(1)}, u32[]{:S(2)}, u32[]{:S(2)}) %collective-permute-start.6) | collective-permute-done | bytes 524320 | tf_op jit(solution)/shard_map/ppermute | solution.py:65
  99.2 4.6 %collective-permute-done.3.refs_2_ = bf16[128,4096]{1,0:T(8,128)(2,1)} collective-permute-done((bf16[128,4096]{1,0:T(8,128)(2,1)}, bf16[128,4096]{1,0:T(8,128)(2,1)}, u32[]{:S(2)}, u32[]{:S(2)}) %collective-permute-start.3) | collective-permute-done | bytes 1048608 | tf_op jit(solution)/shard_map/ppermute | solution.py:61
  103.8 5.0 %part_ladder.5 = bf16[256,4096]{1,0:T(8,128)(2,1)S(1)} custom-call(bf16[4,256,256]{2,1,0:T(8,128)(2,1)S(1)} %collective-permute-done.6.a_ref, bf16[256,4096]{1,0:T(8,128)(2,1)S(1)} %bitcast.37, bf16[128,4096]{1,0:T(8,128)(2,1)} %collective-permute-done.2.refs_0_, bf16[128,4096]{1,0:T(8,128)(2,1)S(1)} %collective-permute-done.1.refs_1_, ...), custom_call_target="tpu_custom_call" | custom-call | flops 2147483648 | bytes 11534336 | tf_op jit(solution)/shard_map/part_ladder/pallas_call | solution.py:169
  108.8 3.8 %collective-permute-start.7 = (bf16[256,4096]{1,0:T(8,128)(2,1)S(1)}, bf16[256,4096]{1,0:T(8,128)(2,1)S(1)}, u32[]{:S(2)}, u32[]{:S(2)}) collective-permute-start(bf16[256,4096]{1,0:T(8,128)(2,1)S(1)} %part_ladder.5), channel_id=1, source_target_pairs={{0,2},{1,3},{2,0},{3,1},{4,6},{5,7},{6,4},{7,5},{8,10},{9,11},{10,... | collective-permute-start | bytes 6291464 | tf_op jit(solution)/shard_map/ppermute | solution.py:65
  112.6 5.0 %part_ladder.6 = bf16[256,4096]{1,0:T(8,128)(2,1)S(1)} custom-call(bf16[4,256,256]{2,1,0:T(8,128)(2,1)S(1)} %collective-permute-done.8.a_ref, bf16[256,4096]{1,0:T(8,128)(2,1)S(1)} %bitcast.38, bf16[128,4096]{1,0:T(8,128)(2,1)} %collective-permute-done.2.refs_0_, bf16[128,4096]{1,0:T(8,128)(2,1)S(1)} %collective-permute-done.1.refs_1_, ...), custom_call_target="tpu_custom_call" | custom-call | flops 2147483648 | bytes 11534336 | tf_op jit(solution)/shard_map/part_ladder/pallas_call | solution.py:169
  117.7 1.2 collective-permute-start.9
  118.9 5.0 %part_ladder.7 = bf16[256,4096]{1,0:T(8,128)(2,1)S(1)} custom-call(bf16[4,256,256]{2,1,0:T(8,128)(2,1)S(1)} %collective-permute-done.10.a_ref, bf16[256,4096]{1,0:T(8,128)(2,1)S(1)} %bitcast.39, bf16[128,4096]{1,0:T(8,128)(2,1)} %collective-permute-done.2.refs_0_, bf16[128,4096]{1,0:T(8,128)(2,1)S(1)} %collective-permute-done.1.refs_1_, ...), custom_call_target="tpu_custom_call" | custom-call | flops 2147483648 | bytes 11534336 | tf_op jit(solution)/shard_map/part_ladder/pallas_call | solution.py:169
  124.8 5.1 %part_ladder.4 = f32[256,4096]{1,0:T(8,128)S(1)} custom-call(bf16[4,256,256]{2,1,0:T(8,128)(2,1)S(1)} %get-tuple-element.18.a_ref, bf16[256,4096]{1,0:T(8,128)(2,1)S(1)} %bitcast.40, bf16[128,4096]{1,0:T(8,128)(2,1)} %collective-permute-done.2.refs_0_, bf16[128,4096]{1,0:T(8,128)(2,1)S(1)} %collective-permute-done.1.refs_1_, ...), custom_call_target="tpu_custom_call" | custom-call | flops 2147483648 | bytes 11534336 | tf_op jit(solution)/shard_map/part_ladder/pallas_call | solution.py:169
  130.0 6.8 %collective-permute-done.7 = bf16[256,4096]{1,0:T(8,128)(2,1)S(1)} collective-permute-done((bf16[256,4096]{1,0:T(8,128)(2,1)S(1)}, bf16[256,4096]{1,0:T(8,128)(2,1)S(1)}, u32[]{:S(2)}, u32[]{:S(2)}) %collective-permute-start.7) | collective-permute-done | bytes 2097184 | tf_op jit(solution)/shard_map/ppermute | solution.py:65
  136.7 22.9 %collective-permute-done.9 = bf16[256,4096]{1,0:T(8,128)(2,1)S(1)} collective-permute-done((bf16[256,4096]{1,0:T(8,128)(2,1)S(1)}, bf16[256,4096]{1,0:T(8,128)(2,1)S(1)}, u32[]{:S(2)}, u32[]{:S(2)}) %collective-permute-start.9) | collective-permute-done | bytes 2097184 | tf_op jit(solution)/shard_map/ppermute | solution.py:65
  159.6 3.3 %add_bitcast_fusion = f32[1,256,4096]{2,1,0:T(8,128)} fusion(bf16[256,4096]{1,0:T(8,128)(2,1)S(1)} %collective-permute-done.11, bf16[256,4096]{1,0:T(8,128)(2,1)S(1)} %collective-permute-done.9, f32[256,4096]{1,0:T(8,128)S(1)} %part_ladder.4, bf16[256,4096]{1,0:T(8,128)(2,1)S(1)} %collective-permute-done.7), kind=kLoop, calls=%fused_computation | loop fusion | flops 6291456 | bytes 14680064 | tf_op jit(solution)/shard_map/broadcast_in_dim | solution.py:254
  (44 shorter events, 5.4 us)
Async XLA Ops:
  0.6 6.1 %copy-start.5 = (s32[1,256]{1,0:T(1,128)S(1)}, s32[1,256]{1,0:T(1,128)}, u32[]{:S(2)}) copy-start(s32[1,256]{1,0:T(1,128)} %param.11) | copy-start | bytes 3076
  0.6 6.2 %copy-start.3 = (s32[1,256]{1,0:T(1,128)S(1)}, s32[1,256]{1,0:T(1,128)}, u32[]{:S(2)}) copy-start(s32[1,256]{1,0:T(1,128)} %target_ref.1) | copy-start | bytes 3076
  0.6 6.2 %copy-start.2 = (bf16[1,256,4096]{2,1,0:T(8,128)(2,1)S(1)}, bf16[1,256,4096]{2,1,0:T(8,128)(2,1)}, u32[]{:S(2)}) copy-start(bf16[1,256,4096]{2,1,0:T(8,128)(2,1)} %param.8) | copy-start | bytes 6291460
  3.9 15.5 %collective-permute-start.1 = (bf16[128,4096]{1,0:T(8,128)(2,1)}, bf16[128,4096]{1,0:T(8,128)(2,1)S(1)}, u32[]{:S(2)}, u32[]{:S(2)}) collective-permute-start(bf16[128,4096]{1,0:T(8,128)(2,1)} %get-tuple-element.24), channel_id=1, source_target_pairs={{0,12},{1,13},{2,14},{3,15},{4,0},{5,1},{6,2},{7,3},{8,4},{9,5},{1... | collective-permute-start | bytes 3145736 | tf_op jit(solution)/shard_map/ppermute | solution.py:61
  6.7 16.3 %collective-permute-start = (bf16[128,4096]{1,0:T(8,128)(2,1)}, bf16[128,4096]{1,0:T(8,128)(2,1)}, u32[]{:S(2)}, u32[]{:S(2)}) collective-permute-start(bf16[128,4096]{1,0:T(8,128)(2,1)} %get-tuple-element.25), channel_id=1, source_target_pairs={{0,4},{1,5},{2,6},{3,7},{4,8},{5,9},{6,10},{7,11},{8,12},{9,13},{1... | collective-permute-start | bytes 3145736 | tf_op jit(solution)/shard_map/ppermute | solution.py:61
  9.5 1.8 %copy-start.1 = (bf16[13312,128]{1,0:T(8,128)(2,1)}, bf16[13312,128]{1,0:T(8,128)(2,1)S(1)}, u32[]{:S(2)}) copy-start(bf16[13312,128]{1,0:T(8,128)(2,1)S(1)} %place.1) | copy-start | bytes 10223620
  23.1 13.8 %copy-start.4 = (s32[64,64]{1,0:T(8,128)S(1)}, s32[64,64]{1,0:T(8,128)}, u32[]{:S(2)}) copy-start(s32[64,64]{1,0:T(8,128)} %param.15) | copy-start | bytes 49156
  23.1 14.0 %copy-start.6 = (f32[64]{0:T(128)S(1)}, f32[64]{0:T(128)}, u32[]{:S(2)}) copy-start(f32[64]{0:T(128)} %param.14) | copy-start | bytes 772
  23.1 51.9 %all-to-all-start = ((bf16[128,104,128]{2,1,0:T(8,128)(2,1)}), bf16[128,104,128]{2,1,0:T(8,128)(2,1)}, u32[]{:S(2)}, u32[]{:S(2)}) async-start(bf16[128,104,128]{2,1,0:T(8,128)(2,1)} %bitcast.41), calls=%async_computation | async-start | bytes 6815744 | tf_op jit(solution)/shard_map/all_to_all | solution.py:215
  32.1 71.6 %copy-start = (bf16[1,256,4096]{2,1,0:T(8,128)(2,1)S(1)}, bf16[1,256,4096]{2,1,0:T(8,128)(2,1)}, u32[]{:S(2)}) copy-start(bf16[1,256,4096]{2,1,0:T(8,128)(2,1)} %param.9) | copy-start | bytes 6291460
  32.2 52.6 %collective-permute-start.5 = (bf16[128,4096]{1,0:T(8,128)(2,1)}, bf16[128,4096]{1,0:T(8,128)(2,1)}, u32[]{:S(2)}, u32[]{:S(2)}) collective-permute-start(bf16[128,4096]{1,0:T(8,128)(2,1)} %get-tuple-element.24), channel_id=1, source_target_pairs={{0,4},{1,5},{2,6},{3,7},{4,8},{5,9},{6,10},{7,11},{8,12},{9,13},{1... | collective-permute-start | bytes 3145736 | tf_op jit(solution)/shard_map/ppermute | solution.py:61
  33.1 53.1 %collective-permute-start.2 = (bf16[128,4096]{1,0:T(8,128)(2,1)}, bf16[128,4096]{1,0:T(8,128)(2,1)}, u32[]{:S(2)}, u32[]{:S(2)}) collective-permute-start(bf16[128,4096]{1,0:T(8,128)(2,1)} %get-tuple-element.25), channel_id=1, source_target_pairs={{0,12},{1,13},{2,14},{3,15},{4,0},{5,1},{6,2},{7,3},{8,4},{9,5},{1... | collective-permute-start | bytes 3145736 | tf_op jit(solution)/shard_map/ppermute | solution.py:61
  75.0 24.2 %collective-permute-start.4 = (bf16[128,4096]{1,0:T(8,128)(2,1)S(1)}, bf16[128,4096]{1,0:T(8,128)(2,1)}, u32[]{:S(2)}, u32[]{:S(2)}) collective-permute-start(bf16[128,4096]{1,0:T(8,128)(2,1)S(1)} %collective-permute-done.1.refs_1_), channel_id=1, source_target_pairs={{0,12},{1,13},{2,14},{3,15},{4,0},{5,1},{6,2},{7,3},{8,4},{9,5},{1... | collective-permute-start | bytes 3145736 | tf_op jit(solution)/shard_map/ppermute | solution.py:61
  76.1 27.7 %collective-permute-start.3 = (bf16[128,4096]{1,0:T(8,128)(2,1)}, bf16[128,4096]{1,0:T(8,128)(2,1)}, u32[]{:S(2)}, u32[]{:S(2)}) collective-permute-start(bf16[128,4096]{1,0:T(8,128)(2,1)} %collective-permute-done.refs_4_), channel_id=1, source_target_pairs={{0,4},{1,5},{2,6},{3,7},{4,8},{5,9},{6,10},{7,11},{8,12},{9,13},{1... | collective-permute-start | bytes 3145736 | tf_op jit(solution)/shard_map/ppermute | solution.py:61
  83.5 15.7 %collective-permute-start.6 = (bf16[4,256,256]{2,1,0:T(8,128)(2,1)S(1)}, bf16[4,256,256]{2,1,0:T(8,128)(2,1)S(1)}, u32[]{:S(2)}, u32[]{:S(2)}) collective-permute-start(bf16[4,256,256]{2,1,0:T(8,128)(2,1)S(1)} %get-tuple-element.21), channel_id=1, source_target_pairs={{0,2},{1,3},{2,0},{3,1},{4,6},{5,7},{6,4},{7,5},{8,10},{9,11},{10,... | collective-permute-start | bytes 1572872 | tf_op jit(solution)/shard_map/ppermute | solution.py:65
  84.8 27.9 %collective-permute-start.8 = (bf16[4,256,256]{2,1,0:T(8,128)(2,1)S(1)}, bf16[4,256,256]{2,1,0:T(8,128)(2,1)S(1)}, u32[]{:S(2)}, u32[]{:S(2)}) collective-permute-start(bf16[4,256,256]{2,1,0:T(8,128)(2,1)S(1)} %get-tuple-element.22), channel_id=1, source_target_pairs={{0,1},{1,2},{2,3},{3,0},{4,5},{5,6},{6,7},{7,4},{8,9},{9,10},{10,1... | collective-permute-start | bytes 1572872 | tf_op jit(solution)/shard_map/ppermute | solution.py:65
  86.3 32.6 %collective-permute-start.10 = (bf16[4,256,256]{2,1,0:T(8,128)(2,1)S(1)}, bf16[4,256,256]{2,1,0:T(8,128)(2,1)S(1)}, u32[]{:S(2)}, u32[]{:S(2)}) collective-permute-start(bf16[4,256,256]{2,1,0:T(8,128)(2,1)S(1)} %get-tuple-element.23), channel_id=1, source_target_pairs={{0,3},{1,0},{2,1},{3,2},{4,7},{5,4},{6,5},{7,6},{8,11},{9,8},{10,9... | collective-permute-start | bytes 1572872 | tf_op jit(solution)/shard_map/ppermute | solution.py:65
  108.8 27.9 %collective-permute-start.7 = (bf16[256,4096]{1,0:T(8,128)(2,1)S(1)}, bf16[256,4096]{1,0:T(8,128)(2,1)S(1)}, u32[]{:S(2)}, u32[]{:S(2)}) collective-permute-start(bf16[256,4096]{1,0:T(8,128)(2,1)S(1)} %part_ladder.5), channel_id=1, source_target_pairs={{0,2},{1,3},{2,0},{3,1},{4,6},{5,7},{6,4},{7,5},{8,10},{9,11},{10,... | collective-permute-start | bytes 6291464 | tf_op jit(solution)/shard_map/ppermute | solution.py:65
  117.7 42.0 %collective-permute-start.9 = (bf16[256,4096]{1,0:T(8,128)(2,1)S(1)}, bf16[256,4096]{1,0:T(8,128)(2,1)S(1)}, u32[]{:S(2)}, u32[]{:S(2)}) collective-permute-start(bf16[256,4096]{1,0:T(8,128)(2,1)S(1)} %part_ladder.6), channel_id=1, source_target_pairs={{0,3},{1,0},{2,1},{3,2},{4,7},{5,4},{6,5},{7,6},{8,11},{9,8},{10,9... | collective-permute-start | bytes 6291464 | tf_op jit(solution)/shard_map/ppermute | solution.py:65
  123.9 35.7 %collective-permute-start.11 = (bf16[256,4096]{1,0:T(8,128)(2,1)S(1)}, bf16[256,4096]{1,0:T(8,128)(2,1)S(1)}, u32[]{:S(2)}, u32[]{:S(2)}) collective-permute-start(bf16[256,4096]{1,0:T(8,128)(2,1)S(1)} %part_ladder.7), channel_id=1, source_target_pairs={{0,1},{1,2},{2,3},{3,0},{4,5},{5,6},{6,7},{7,4},{8,9},{9,10},{10,1... | collective-permute-start | bytes 6291464 | tf_op jit(solution)/shard_map/ppermute | solution.py:65

commit v3 on v2

--- a/solution.py
+++ b/solution.py
@@ -25,6 +25,8 @@
 LABELS = CAP * TILES
 CHUNK = LABELS + 8
 SIDE = 4
+HALF = WIDTH // 2
+CUT = 1024
 MIB = 1024 * 1024
 
 
@@ -151,34 +153,67 @@
             w_ref[o] = (gamma * bubble_ref[:, columns]).astype(jnp.bfloat16)
 
 
-def ladder_kernel(a_ref, own_ref, *refs):
+def ladder_kernel(parts, a_ref, *refs):
     out_ref = refs[-1]
-    total = jnp.dot(a_ref[0], own_ref[...], preferred_element_type=jnp.float32)
+    total = jnp.dot(a_ref[0], refs[0][...], preferred_element_type=jnp.float32)
     for o in range(1, SIDE):
-        block = jnp.concatenate([refs[2 * o - 2][...], refs[2 * o - 1][...]], axis=0)
+        block = jnp.concatenate([refs[2 * o - 1][...], refs[2 * o][...]], axis=0)
         total += jnp.dot(a_ref[o], block, preferred_element_type=jnp.float32)
+    for other in refs[parts:-1]:
+        total += other[...].astype(jnp.float32)
     out_ref[...] = total.astype(out_ref.dtype)
 
 
-def part_ladder(weighted, full_parts, dtype):
-    cut = 1024
-
-    def columns(rows):
-        return pl.BlockSpec((rows, cut), lambda n: (0, n))
+def part_ladder(weighted, full_parts, side, dtype, *others):
+    steps = HALF // CUT
+
+    def columns(rows, first):
+        return pl.BlockSpec((rows, CUT), lambda n: (0, first + n))
 
     return pl.pallas_call(
-        ladder_kernel,
-        grid=(WIDTH // cut,),
+        functools.partial(ladder_kernel, len(full_parts)),
+        grid=(steps,),
         in_specs=[pl.BlockSpec((SIDE, ROWS, ROWS), lambda n: (0, 0, 0))]
-        + [columns(part.shape[0]) for part in full_parts],
-        out_specs=columns(ROWS),
-        out_shape=jax.ShapeDtypeStruct((ROWS, WIDTH), dtype),
+        + [columns(part.shape[0], side * steps) for part in full_parts]
+        + [columns(ROWS, 0) for _ in others],
+        out_specs=columns(ROWS, 0),
+        out_shape=jax.ShapeDtypeStruct((ROWS, HALF), dtype),
         compiler_params=pltpu.CompilerParams(vmem_limit_bytes=32 * MIB),
         cost_estimate=pl.CostEstimate(
-            flops=2 * ROWS * 4 * ROWS * WIDTH, bytes_accessed=11 * MIB, transcendentals=0
+            flops=2 * ROWS * 4 * ROWS * HALF, bytes_accessed=6 * MIB, transcendentals=0
         ),
         name="part_ladder",
-    )(weighted, *full_parts)
+    )(weighted, *full_parts, *others)
+
+
+def join_kernel(left_a, left_b, right_a, right_b, out_ref):
+    n = pl.program_id(0)
+
+    @pl.when(n < HALF // CUT)
+    def _():
+        out_ref[...] = left_a[...] + left_b[...].astype(jnp.float32)
+
+    @pl.when(n >= HALF // CUT)
+    def _():
+        out_ref[...] = right_a[...] + right_b[...].astype(jnp.float32)
+
+
+def join(*parts):
+    steps = HALF // CUT
+    left = pl.BlockSpec((ROWS, CUT), lambda n: (0, jnp.minimum(n, steps - 1)))
+    right = pl.BlockSpec((ROWS, CUT), lambda n: (0, jnp.maximum(n - steps, 0)))
+    return pl.pallas_call(
+        join_kernel,
+        grid=(2 * steps,),
+        in_specs=[left, left, right, right],
+        out_specs=pl.BlockSpec((ROWS, CUT), lambda n: (0, n)),
+        out_shape=jax.ShapeDtypeStruct((ROWS, WIDTH), jnp.float32),
+        compiler_params=pltpu.CompilerParams(vmem_limit_bytes=32 * MIB),
+        cost_estimate=pl.CostEstimate(
+            flops=ROWS * WIDTH, bytes_accessed=10 * MIB, transcendentals=0
+        ),
+        name="join",
+    )(*parts)
 
 
 def per_device(vert_ph, full_pp, target, shift, trans_mom, trans_bose, energies, pair_table):
@@ -211,14 +246,13 @@
         ),
         name="place",
     )(target, shift.reshape(ROWS, 1), vert_ph.reshape(ROWS, WIDTH))
-    payload, left_top, right_low = lax.optimization_barrier((payload, left_top, right_low))
     arrived = lax.all_to_all(
         payload.reshape(DEVICES, CHUNK, LANES), AXES, split_axis=0, concat_axis=0, tiled=True
     ).reshape(DEVICES * CHUNK, LANES)
 
-    arrived, left_top, right_low = lax.optimization_barrier((arrived, left_top, right_low))
     far_top = move_g(left_top, 1)
     far_low = move_g(right_low, 3)
+    arrived, left_low, right_top = lax.optimization_barrier((arrived, left_low, right_top))
     full_parts = (full, right_top, right_low, far_top, far_low, left_top, left_low)
 
     pick_mom = (trans_mom[:, None] == jnp.arange(NQ, dtype=jnp.int32)[None, :]).astype(jnp.float32)
@@ -244,13 +278,19 @@
         name="collect",
     )(where, pair_bubble, arrived)
 
-    ladder_parts = []
-    for d, sent in ((2, w2), (1, w1), (3, w3)):
-        part = part_ladder(move_h(sent, d), full_parts, jnp.bfloat16)
-        ladder_parts.append(move_h(part, SIDE - d))
-    ladder = part_ladder(own, full_parts, jnp.float32)
-    for part in ladder_parts:
-        ladder = ladder + part.astype(jnp.float32)
+    part = functools.partial(part_ladder, full_parts=full_parts)
+    bf16, f32 = jnp.bfloat16, jnp.float32
+    from_far, from_low, from_high = move_h(w2, 2), move_h(w1, 1), move_h(w3, 3)
+    from_far, from_low, from_high = lax.optimization_barrier((from_far, from_low, from_high))
+    far_left = move_h(part(from_far, side=0, dtype=bf16), 1)
+    far_right = move_h(part(from_far, side=1, dtype=bf16), 3)
+    high_right = move_h(part(from_high, side=1, dtype=bf16), 1)
+    low_left = move_h(part(from_low, side=0, dtype=bf16), 3)
+    high_left = move_h(part_ladder(from_high, full_parts, 0, bf16, far_left), 1)
+    low_right = move_h(part_ladder(from_low, full_parts, 1, bf16, far_right), 3)
+    own_left = part_ladder(own, full_parts, 0, f32, low_left)
+    own_right = part_ladder(own, full_parts, 1, f32, high_right)
+    ladder = join(own_left, high_left, own_right, low_right)
     return gamma[None], ladder[None]
 
 

time: 163 us -> 151 us (0.926)
  waiting for transfers between devices: 94.2 us -> 69.9 us
  starting transfers between devices: 27.8 us -> 36.7 us
  Pallas kernels: 29 us -> 34.5 us
  other arithmetic: 3.43 us -> 0.16 us
    all_to_all x1, waiting for transfers between devices: 37 us -> 0.01 us  [per_device(): lax.all_to_all(payload.reshape(DEVICES, CHUNK, LANES), AXES, split_axis=0...]
    ppermute x6, waiting for transfers between devices: 16.4 us -> 48.4 us  [move_g(): return lax.ppermute(array, AXES, pairs_along((0, 1), step))]
    ppermute x6 -> x9, waiting for transfers between devices: 40.8 us -> 21.6 us  [move_h(): return lax.ppermute(array, AXES, pairs_along((1, 0), step))]
    ppermute x6 -> x9, starting transfers between devices: 10.5 us -> 16.6 us  [move_h(): return lax.ppermute(array, AXES, pairs_along((1, 0), step))]
    pallas_call x4 -> x9, Pallas kernels: 20.2 us -> 25.7 us  [the longest x8 22.8 us: part_ladder(): pl.pallas_call(functools.partial(ladder_kernel, len(full_parts)), grid=(s...]
    broadcast_in_dim x1 -> x0, other arithmetic: 3.28 us -> none  [per_device(): return (gamma[None], ladder[None])]
    all_to_all x1, starting transfers between devices: 9.07 us -> 11.6 us  [per_device(): lax.all_to_all(payload.reshape(DEVICES, CHUNK, LANES), AXES, split_axis=0...]
    unnamed x14 -> x12, local copies, waits for them, and re-layouts: 1.77 us -> 4.03 us
  transfers between devices with their start and end apart: 13 -> 16, of which waited for: 7 -> 11; matrix products, arithmetic and copies ran while one was open for 1% -> 2% of each run, Pallas kernels for 18% -> 17%
where the time goes in v3:
time: 151 us
  waiting for transfers between devices  69.9 us (46%)
  starting transfers between devices  36.7 us (24%)
  Pallas kernels  34.5 us (23%)
  local copies, waits for them, and re-layouts  7.15 us (5%)
  between operations  2.22 us (1%)
    ppermute x6, waiting for transfers between devices, move_g(): return lax.ppermute(array, AXES, pairs_along((0, 1), step))  48.4 us
    pallas_call x8, Pallas kernels, part_ladder(): pl.pallas_call(functools.partial(ladder_kernel, len(full_parts)), grid=(s...  22.8 us
    ppermute x9, waiting for transfers between devices, move_h(): return lax.ppermute(array, AXES, pairs_along((1, 0), step))  21.6 us
    ppermute x9, starting transfers between devices, move_h(): return lax.ppermute(array, AXES, pairs_along((1, 0), step))  16.6 us
    all_to_all x1, starting transfers between devices, per_device(): lax.all_to_all(payload.reshape(DEVICES, CHUNK, LANES), AXES, split_axis=0...  11.6 us
    ppermute x6, starting transfers between devices, move_g(): return lax.ppermute(array, AXES, pairs_along((0, 1), step))  8.5 us
    pallas_call x1, Pallas kernels, per_device(): pl.pallas_call(collect_kernel, in_specs=[pl.BlockSpec(memory_space=pltpu....  6.27 us
    unnamed x12, local copies, waits for them, and re-layouts  4.03 us
  transfers between devices with their start and end apart: 16, of which 11 were waited for; matrix products, arithmetic and copies ran while one was open for 2% of the time, Pallas kernels for 17%

profile of v3, /device:TPU:0, one launch (start us, length us, event | category | flops | bytes accessed | tf_op | source)
XLA Modules:
  0.0 151.0 jit_solution(109397127368831761)
XLA Ops:
  3.7 2.6 %place.1 = bf16[13312,128]{1,0:T(8,128)(2,1)S(1)} custom-call(s32[1,256]{1,0:T(1,128)S(1)} %copy-done.3, s32[256,1]{1,0:T(8,128)S(1)} %copy.10.shift_ref, bf16[256,4096]{1,0:T(8,128)(2,1)S(1)} %bitcast.45), custom_call_target="tpu_custom_call" | custom-call | flops 805306368 | bytes 5242880 | tf_op jit(solution)/shard_map/place/pallas_call | solution.py:237
  8.1 11.6 %all-to-all-start = ((bf16[128,104,128]{2,1,0:T(8,128)(2,1)}), bf16[128,104,128]{2,1,0:T(8,128)(2,1)}, u32[]{:S(2)}, u32[]{:S(2)}) async-start(bf16[128,104,128]{2,1,0:T(8,128)(2,1)} %bitcast.44), calls=%async_computation | async-start | bytes 6815744 | tf_op jit(solution)/shard_map/all_to_all | solution.py:249
  22.1 2.3 %collective-permute-start.2 = (bf16[128,4096]{1,0:T(8,128)(2,1)}, bf16[128,4096]{1,0:T(8,128)(2,1)}, u32[]{:S(2)}, u32[]{:S(2)}) collective-permute-start(bf16[128,4096]{1,0:T(8,128)(2,1)} %get-tuple-element.25), channel_id=1, source_target_pairs={{0,12},{1,13},{2,14},{3,15},{4,0},{5,1},{6,2},{7,3},{8,4},{9,5},{1... | collective-permute-start | bytes 3145736 | tf_op jit(solution)/shard_map/ppermute | solution.py:63
  29.0 40.4 %collective-permute-done.3.refs_5_ = bf16[128,4096]{1,0:T(8,128)(2,1)S(1)} collective-permute-done((bf16[128,4096]{1,0:T(8,128)(2,1)}, bf16[128,4096]{1,0:T(8,128)(2,1)S(1)}, u32[]{:S(2)}, u32[]{:S(2)}) %collective-permute-start.3) | collective-permute-done | bytes 1048608 | tf_op jit(solution)/shard_map/ppermute | solution.py:63
  69.5 3.2 %collective-permute-start.5 = (bf16[128,4096]{1,0:T(8,128)(2,1)}, bf16[128,4096]{1,0:T(8,128)(2,1)}, u32[]{:S(2)}, u32[]{:S(2)}) collective-permute-start(bf16[128,4096]{1,0:T(8,128)(2,1)} %collective-permute-done.2.refs_2_), channel_id=1, source_target_pairs={{0,12},{1,13},{2,14},{3,15},{4,0},{5,1},{6,2},{7,3},{8,4},{9,5},{1... | collective-permute-start | bytes 3145736 | tf_op jit(solution)/shard_map/ppermute | solution.py:63
  72.9 6.7 %collective-permute-done.1.refs_1_ = bf16[128,4096]{1,0:T(8,128)(2,1)} collective-permute-done((bf16[128,4096]{1,0:T(8,128)(2,1)}, bf16[128,4096]{1,0:T(8,128)(2,1)}, u32[]{:S(2)}, u32[]{:S(2)}) %collective-permute-start.1) | collective-permute-done | bytes 1048608 | tf_op jit(solution)/shard_map/ppermute | solution.py:63
  80.8 6.3 %collect.1 = (f32[256,4096]{1,0:T(8,128)}, bf16[4,256,256]{2,1,0:T(8,128)(2,1)S(1)}, bf16[4,256,256]{2,1,0:T(8,128)(2,1)S(1)}, bf16[4,256,256]{2,1,0:T(8,128)(2,1)S(1)}, bf16[4,256,256]{2,1,0:T(8,128)(2,1)S(1)}) custom-call(s32[4]{0:T(128)S(1)} %pad_add_fusion.where_ref, f32[1,4096]{1,0:T(1,128)S(1)} %multiply_divide_fusion.bubble_ref, ...), custom_call_target="tpu_custom_call" | custom-call | flops 805306368 | bytes 9437184 | tf_op jit(solution)/shard_map/collect/pallas_call | solution.py:268
  87.1 3.0 %collective-permute-start.6 = (bf16[4,256,256]{2,1,0:T(8,128)(2,1)S(1)}, bf16[4,256,256]{2,1,0:T(8,128)(2,1)S(1)}, u32[]{:S(2)}, u32[]{:S(2)}) collective-permute-start(bf16[4,256,256]{2,1,0:T(8,128)(2,1)S(1)} %get-tuple-element.18), channel_id=1, source_target_pairs={{0,2},{1,3},{2,0},{3,1},{4,6},{5,7},{6,4},{7,5},{8,10},{9,11},{10,... | collective-permute-start | bytes 1572872 | tf_op jit(solution)/shard_map/ppermute | solution.py:67
  90.8 2.6 %collective-permute-start.8 = (bf16[4,256,256]{2,1,0:T(8,128)(2,1)S(1)}, bf16[4,256,256]{2,1,0:T(8,128)(2,1)S(1)}, u32[]{:S(2)}, u32[]{:S(2)}) collective-permute-start(bf16[4,256,256]{2,1,0:T(8,128)(2,1)S(1)} %get-tuple-element.20), channel_id=1, source_target_pairs={{0,3},{1,0},{2,1},{3,2},{4,7},{5,4},{6,5},{7,6},{8,11},{9,8},{10,9... | collective-permute-start | bytes 1572872 | tf_op jit(solution)/shard_map/ppermute | solution.py:67
  93.3 4.6 %collective-permute-done.6.a_ref = bf16[4,256,256]{2,1,0:T(8,128)(2,1)S(1)} collective-permute-done((bf16[4,256,256]{2,1,0:T(8,128)(2,1)S(1)}, bf16[4,256,256]{2,1,0:T(8,128)(2,1)S(1)}, u32[]{:S(2)}, u32[]{:S(2)}) %collective-permute-start.6) | collective-permute-done | bytes 524320 | tf_op jit(solution)/shard_map/ppermute | solution.py:67
  98.0 5.5 %collective-permute-done.7.a_ref = bf16[4,256,256]{2,1,0:T(8,128)(2,1)S(1)} collective-permute-done((bf16[4,256,256]{2,1,0:T(8,128)(2,1)S(1)}, bf16[4,256,256]{2,1,0:T(8,128)(2,1)S(1)}, u32[]{:S(2)}, u32[]{:S(2)}) %collective-permute-start.7) | collective-permute-done | bytes 524320 | tf_op jit(solution)/shard_map/ppermute | solution.py:67
  103.6 2.8 %part_ladder.10 = bf16[256,2048]{1,0:T(8,128)(2,1)S(1)} custom-call(bf16[4,256,256]{2,1,0:T(8,128)(2,1)S(1)} %collective-permute-done.6.a_ref, bf16[256,4096]{1,0:T(8,128)(2,1)S(1)} %bitcast.36, bf16[128,4096]{1,0:T(8,128)(2,1)} %collective-permute-done.1.refs_1_, bf16[128,4096]{1,0:T(8,128)(2,1)} %collective-permute-done.2.refs_2_, ...), custom_call_target="tpu_custom_call" | custom-call | flops 1073741824 | bytes 6291456 | tf_op jit(solution)/shard_map/part_ladder/pallas_call | solution.py:173
  107.9 2.8 %part_ladder.14 = bf16[256,2048]{1,0:T(8,128)(2,1)S(1)} custom-call(bf16[4,256,256]{2,1,0:T(8,128)(2,1)S(1)} %collective-permute-done.6.a_ref, bf16[256,4096]{1,0:T(8,128)(2,1)S(1)} %bitcast.37, bf16[128,4096]{1,0:T(8,128)(2,1)} %collective-permute-done.1.refs_1_, bf16[128,4096]{1,0:T(8,128)(2,1)} %collective-permute-done.2.refs_2_, ...), custom_call_target="tpu_custom_call" | custom-call | flops 1073741824 | bytes 6291456 | tf_op jit(solution)/shard_map/part_ladder/pallas_call | solution.py:173
  112.6 2.8 %part_ladder.12 = bf16[256,2048]{1,0:T(8,128)(2,1)S(1)} custom-call(bf16[4,256,256]{2,1,0:T(8,128)(2,1)S(1)} %collective-permute-done.8.a_ref, bf16[256,4096]{1,0:T(8,128)(2,1)S(1)} %bitcast.38, bf16[128,4096]{1,0:T(8,128)(2,1)} %collective-permute-done.1.refs_1_, bf16[128,4096]{1,0:T(8,128)(2,1)} %collective-permute-done.2.refs_2_, ...), custom_call_target="tpu_custom_call" | custom-call | flops 1073741824 | bytes 6291456 | tf_op jit(solution)/shard_map/part_ladder/pallas_call | solution.py:173
  115.7 2.8 %part_ladder.8 = bf16[256,2048]{1,0:T(8,128)(2,1)S(1)} custom-call(bf16[4,256,256]{2,1,0:T(8,128)(2,1)S(1)} %collective-permute-done.7.a_ref, bf16[256,4096]{1,0:T(8,128)(2,1)S(1)} %bitcast.39, bf16[128,4096]{1,0:T(8,128)(2,1)} %collective-permute-done.1.refs_1_, bf16[128,4096]{1,0:T(8,128)(2,1)} %collective-permute-done.2.refs_2_, ...), custom_call_target="tpu_custom_call" | custom-call | flops 1073741824 | bytes 6291456 | tf_op jit(solution)/shard_map/part_ladder/pallas_call | solution.py:173
  118.5 3.3 %collective-permute-start.9 = (bf16[256,2048]{1,0:T(8,128)(2,1)S(1)}, bf16[256,2048]{1,0:T(8,128)(2,1)S(1)}, u32[]{:S(2)}, u32[]{:S(2)}) collective-permute-start(bf16[256,2048]{1,0:T(8,128)(2,1)S(1)} %part_ladder.8), channel_id=1, source_target_pairs={{0,3},{1,0},{2,1},{3,2},{4,7},{5,4},{6,5},{7,6},{8,11},{9,8},{10,9... | collective-permute-start | bytes 3145736 | tf_op jit(solution)/shard_map/ppermute | solution.py:67
  122.5 2.8 %part_ladder.11 = bf16[256,2048]{1,0:T(8,128)(2,1)S(1)} custom-call(bf16[4,256,256]{2,1,0:T(8,128)(2,1)S(1)} %collective-permute-done.8.a_ref, bf16[256,4096]{1,0:T(8,128)(2,1)S(1)} %bitcast.40, bf16[128,4096]{1,0:T(8,128)(2,1)} %collective-permute-done.1.refs_1_, bf16[128,4096]{1,0:T(8,128)(2,1)} %collective-permute-done.2.refs_2_, ...), custom_call_target="tpu_custom_call" | custom-call | flops 1073741824 | bytes 6291456 | tf_op jit(solution)/shard_map/part_ladder/pallas_call | solution.py:173
  125.6 2.8 %part_ladder.15 = bf16[256,2048]{1,0:T(8,128)(2,1)S(1)} custom-call(bf16[4,256,256]{2,1,0:T(8,128)(2,1)S(1)} %collective-permute-done.7.a_ref, bf16[256,4096]{1,0:T(8,128)(2,1)S(1)} %bitcast.41, bf16[128,4096]{1,0:T(8,128)(2,1)} %collective-permute-done.1.refs_1_, bf16[128,4096]{1,0:T(8,128)(2,1)} %collective-permute-done.2.refs_2_, ...), custom_call_target="tpu_custom_call" | custom-call | flops 1073741824 | bytes 6291456 | tf_op jit(solution)/shard_map/part_ladder/pallas_call | solution.py:173
  128.4 3.1 %collective-permute-start.14 = (bf16[256,2048]{1,0:T(8,128)(2,1)S(1)}, bf16[256,2048]{1,0:T(8,128)(2,1)S(1)}, u32[]{:S(2)}, u32[]{:S(2)}) collective-permute-start(bf16[256,2048]{1,0:T(8,128)(2,1)S(1)} %part_ladder.15), channel_id=1, source_target_pairs={{0,3},{1,0},{2,1},{3,2},{4,7},{5,4},{6,5},{7,6},{8,11},{9,8},{10,9... | collective-permute-start | bytes 3145736 | tf_op jit(solution)/shard_map/ppermute | solution.py:67
  133.7 2.9 %part_ladder.13.right_a = f32[256,2048]{1,0:T(8,128)S(1)} custom-call(bf16[4,256,256]{2,1,0:T(8,128)(2,1)S(1)} %get-tuple-element.15.a_ref, bf16[256,4096]{1,0:T(8,128)(2,1)S(1)} %bitcast.42, bf16[128,4096]{1,0:T(8,128)(2,1)} %collective-permute-done.1.refs_1_, bf16[128,4096]{1,0:T(8,128)(2,1)} %collective-permute-done.2.refs_2_, ...), custom_call_target="tpu_custom_call" | custom-call | flops 1073741824 | bytes 6291456 | tf_op jit(solution)/shard_map/part_ladder/pallas_call | solution.py:173
  136.8 2.9 %part_ladder.9.left_a = f32[256,2048]{1,0:T(8,128)S(1)} custom-call(bf16[4,256,256]{2,1,0:T(8,128)(2,1)S(1)} %get-tuple-element.15.a_ref, bf16[256,4096]{1,0:T(8,128)(2,1)S(1)} %bitcast.43, bf16[128,4096]{1,0:T(8,128)(2,1)} %collective-permute-done.1.refs_1_, bf16[128,4096]{1,0:T(8,128)(2,1)} %collective-permute-done.2.refs_2_, ...), custom_call_target="tpu_custom_call" | custom-call | flops 1073741824 | bytes 6291456 | tf_op jit(solution)/shard_map/part_ladder/pallas_call | solution.py:173
  139.7 5.3 %collective-permute-done.11.left_b = bf16[256,2048]{1,0:T(8,128)(2,1)S(1)} collective-permute-done((bf16[256,2048]{1,0:T(8,128)(2,1)S(1)}, bf16[256,2048]{1,0:T(8,128)(2,1)S(1)}, u32[]{:S(2)}, u32[]{:S(2)}) %collective-permute-start.11) | collective-permute-done | bytes 1048608 | tf_op jit(solution)/shard_map/ppermute | solution.py:67
  145.0 3.1 %collective-permute-done.14.right_b = bf16[256,2048]{1,0:T(8,128)(2,1)S(1)} collective-permute-done((bf16[256,2048]{1,0:T(8,128)(2,1)S(1)}, bf16[256,2048]{1,0:T(8,128)(2,1)S(1)}, u32[]{:S(2)}, u32[]{:S(2)}) %collective-permute-start.14) | collective-permute-done | bytes 1048608 | tf_op jit(solution)/shard_map/ppermute | solution.py:67
  148.0 2.9 %join.1 = f32[256,4096]{1,0:T(8,128)} custom-call(f32[256,2048]{1,0:T(8,128)S(1)} %part_ladder.9.left_a, bf16[256,2048]{1,0:T(8,128)(2,1)S(1)} %collective-permute-done.11.left_b, f32[256,2048]{1,0:T(8,128)S(1)} %part_ladder.13.right_a, bf16[256,2048]{1,0:T(8,128)(2,1)S(1)} %collective-permute-done.14.right_b), custom_call_target="tpu_custom_call" | custom-call | flops 1048576 | bytes 10485760 | tf_op jit(solution)/shard_map/join/pallas_call | solution.py:205
  (52 shorter events, 19.4 us)
Async XLA Ops:
  1.4 1.6 %copy-start.2 = (bf16[1,256,4096]{2,1,0:T(8,128)(2,1)S(1)}, bf16[1,256,4096]{2,1,0:T(8,128)(2,1)}, u32[]{:S(2)}) copy-start(bf16[1,256,4096]{2,1,0:T(8,128)(2,1)} %param.8) | copy-start | bytes 6291460
  3.0 0.7 copy-start.3
  6.3 1.8 %copy-start.1 = (bf16[13312,128]{1,0:T(8,128)(2,1)}, bf16[13312,128]{1,0:T(8,128)(2,1)S(1)}, u32[]{:S(2)}) copy-start(bf16[13312,128]{1,0:T(8,128)(2,1)S(1)} %place.1) | copy-start | bytes 10223620
  8.1 11.6 %copy-start = (bf16[1,256,4096]{2,1,0:T(8,128)(2,1)S(1)}, bf16[1,256,4096]{2,1,0:T(8,128)(2,1)}, u32[]{:S(2)}) copy-start(bf16[1,256,4096]{2,1,0:T(8,128)(2,1)} %param.9) | copy-start | bytes 6291460
  8.1 72.7 %all-to-all-start = ((bf16[128,104,128]{2,1,0:T(8,128)(2,1)}), bf16[128,104,128]{2,1,0:T(8,128)(2,1)}, u32[]{:S(2)}, u32[]{:S(2)}) async-start(bf16[128,104,128]{2,1,0:T(8,128)(2,1)} %bitcast.44), calls=%async_computation | async-start | bytes 6815744 | tf_op jit(solution)/shard_map/all_to_all | solution.py:249
  19.7 8.2 %copy-start.4 = (s32[64,64]{1,0:T(8,128)S(1)}, s32[64,64]{1,0:T(8,128)}, u32[]{:S(2)}) copy-start(s32[64,64]{1,0:T(8,128)} %param.15) | copy-start | bytes 49156
  19.7 8.3 %copy-start.5 = (f32[64]{0:T(128)S(1)}, f32[64]{0:T(128)}, u32[]{:S(2)}) copy-start(f32[64]{0:T(128)} %param.14) | copy-start | bytes 772
  21.3 48.2 %collective-permute-start.3 = (bf16[128,4096]{1,0:T(8,128)(2,1)}, bf16[128,4096]{1,0:T(8,128)(2,1)S(1)}, u32[]{:S(2)}, u32[]{:S(2)}) collective-permute-start(bf16[128,4096]{1,0:T(8,128)(2,1)} %get-tuple-element.24), channel_id=1, source_target_pairs={{0,4},{1,5},{2,6},{3,7},{4,8},{5,9},{6,10},{7,11},{8,12},{9,13},{1... | collective-permute-start | bytes 3145736 | tf_op jit(solution)/shard_map/ppermute | solution.py:63
  22.1 47.3 %collective-permute-start.2 = (bf16[128,4096]{1,0:T(8,128)(2,1)}, bf16[128,4096]{1,0:T(8,128)(2,1)}, u32[]{:S(2)}, u32[]{:S(2)}) collective-permute-start(bf16[128,4096]{1,0:T(8,128)(2,1)} %get-tuple-element.25), channel_id=1, source_target_pairs={{0,12},{1,13},{2,14},{3,15},{4,0},{5,1},{6,2},{7,3},{8,4},{9,5},{1... | collective-permute-start | bytes 3145736 | tf_op jit(solution)/shard_map/ppermute | solution.py:63
  24.5 55.1 %collective-permute-start.1 = (bf16[128,4096]{1,0:T(8,128)(2,1)}, bf16[128,4096]{1,0:T(8,128)(2,1)}, u32[]{:S(2)}, u32[]{:S(2)}) collective-permute-start(bf16[128,4096]{1,0:T(8,128)(2,1)} %get-tuple-element.24), channel_id=1, source_target_pairs={{0,12},{1,13},{2,14},{3,15},{4,0},{5,1},{6,2},{7,3},{8,4},{9,5},{1... | collective-permute-start | bytes 3145736 | tf_op jit(solution)/shard_map/ppermute | solution.py:63
  25.4 55.4 %collective-permute-start = (bf16[128,4096]{1,0:T(8,128)(2,1)}, bf16[128,4096]{1,0:T(8,128)(2,1)}, u32[]{:S(2)}, u32[]{:S(2)}) collective-permute-start(bf16[128,4096]{1,0:T(8,128)(2,1)} %get-tuple-element.25), channel_id=1, source_target_pairs={{0,4},{1,5},{2,6},{3,7},{4,8},{5,9},{6,10},{7,11},{8,12},{9,13},{1... | collective-permute-start | bytes 3145736 | tf_op jit(solution)/shard_map/ppermute | solution.py:63
  69.5 34.1 %collective-permute-start.4 = (bf16[128,4096]{1,0:T(8,128)(2,1)S(1)}, bf16[128,4096]{1,0:T(8,128)(2,1)}, u32[]{:S(2)}, u32[]{:S(2)}) collective-permute-start(bf16[128,4096]{1,0:T(8,128)(2,1)S(1)} %collective-permute-done.3.refs_5_), channel_id=1, source_target_pairs={{0,4},{1,5},{2,6},{3,7},{4,8},{5,9},{6,10},{7,11},{8,12},{9,13},{1... | collective-permute-start | bytes 3145736 | tf_op jit(solution)/shard_map/ppermute | solution.py:63
  69.5 34.1 %collective-permute-start.5 = (bf16[128,4096]{1,0:T(8,128)(2,1)}, bf16[128,4096]{1,0:T(8,128)(2,1)}, u32[]{:S(2)}, u32[]{:S(2)}) collective-permute-start(bf16[128,4096]{1,0:T(8,128)(2,1)} %collective-permute-done.2.refs_2_), channel_id=1, source_target_pairs={{0,12},{1,13},{2,14},{3,15},{4,0},{5,1},{6,2},{7,3},{8,4},{9,5},{1... | collective-permute-start | bytes 3145736 | tf_op jit(solution)/shard_map/ppermute | solution.py:63
  87.1 10.9 %collective-permute-start.6 = (bf16[4,256,256]{2,1,0:T(8,128)(2,1)S(1)}, bf16[4,256,256]{2,1,0:T(8,128)(2,1)S(1)}, u32[]{:S(2)}, u32[]{:S(2)}) collective-permute-start(bf16[4,256,256]{2,1,0:T(8,128)(2,1)S(1)} %get-tuple-element.18), channel_id=1, source_target_pairs={{0,2},{1,3},{2,0},{3,1},{4,6},{5,7},{6,4},{7,5},{8,10},{9,11},{10,... | collective-permute-start | bytes 1572872 | tf_op jit(solution)/shard_map/ppermute | solution.py:67
  90.1 13.4 %collective-permute-start.7 = (bf16[4,256,256]{2,1,0:T(8,128)(2,1)S(1)}, bf16[4,256,256]{2,1,0:T(8,128)(2,1)S(1)}, u32[]{:S(2)}, u32[]{:S(2)}) collective-permute-start(bf16[4,256,256]{2,1,0:T(8,128)(2,1)S(1)} %get-tuple-element.19), channel_id=1, source_target_pairs={{0,1},{1,2},{2,3},{3,0},{4,5},{5,6},{6,7},{7,4},{8,9},{9,10},{10,1... | collective-permute-start | bytes 1572872 | tf_op jit(solution)/shard_map/ppermute | solution.py:67
  90.8 12.8 %collective-permute-start.8 = (bf16[4,256,256]{2,1,0:T(8,128)(2,1)S(1)}, bf16[4,256,256]{2,1,0:T(8,128)(2,1)S(1)}, u32[]{:S(2)}, u32[]{:S(2)}) collective-permute-start(bf16[4,256,256]{2,1,0:T(8,128)(2,1)S(1)} %get-tuple-element.20), channel_id=1, source_target_pairs={{0,3},{1,0},{2,1},{3,2},{4,7},{5,4},{6,5},{7,6},{8,11},{9,8},{10,9... | collective-permute-start | bytes 1572872 | tf_op jit(solution)/shard_map/ppermute | solution.py:67
  106.4 16.1 %collective-permute-start.10 = (bf16[256,2048]{1,0:T(8,128)(2,1)S(1)}, bf16[256,2048]{1,0:T(8,128)(2,1)S(1)}, u32[]{:S(2)}, u32[]{:S(2)}) collective-permute-start(bf16[256,2048]{1,0:T(8,128)(2,1)S(1)} %part_ladder.10), channel_id=1, source_target_pairs={{0,1},{1,2},{2,3},{3,0},{4,5},{5,6},{6,7},{7,4},{8,9},{9,10},{10,1... | collective-permute-start | bytes 3145736 | tf_op jit(solution)/shard_map/ppermute | solution.py:67
  110.7 14.9 %collective-permute-start.13 = (bf16[256,2048]{1,0:T(8,128)(2,1)S(1)}, bf16[256,2048]{1,0:T(8,128)(2,1)S(1)}, u32[]{:S(2)}, u32[]{:S(2)}) collective-permute-start(bf16[256,2048]{1,0:T(8,128)(2,1)S(1)} %part_ladder.14), channel_id=1, source_target_pairs={{0,3},{1,0},{2,1},{3,2},{4,7},{5,4},{6,5},{7,6},{8,11},{9,8},{10,9... | collective-permute-start | bytes 3145736 | tf_op jit(solution)/shard_map/ppermute | solution.py:67
  115.4 18.3 %collective-permute-start.12 = (bf16[256,2048]{1,0:T(8,128)(2,1)S(1)}, bf16[256,2048]{1,0:T(8,128)(2,1)S(1)}, u32[]{:S(2)}, u32[]{:S(2)}) collective-permute-start(bf16[256,2048]{1,0:T(8,128)(2,1)S(1)} %part_ladder.12), channel_id=1, source_target_pairs={{0,1},{1,2},{2,3},{3,0},{4,5},{5,6},{6,7},{7,4},{8,9},{9,10},{10,1... | collective-permute-start | bytes 3145736 | tf_op jit(solution)/shard_map/ppermute | solution.py:67
  118.5 18.3 %collective-permute-start.9 = (bf16[256,2048]{1,0:T(8,128)(2,1)S(1)}, bf16[256,2048]{1,0:T(8,128)(2,1)S(1)}, u32[]{:S(2)}, u32[]{:S(2)}) collective-permute-start(bf16[256,2048]{1,0:T(8,128)(2,1)S(1)} %part_ladder.8), channel_id=1, source_target_pairs={{0,3},{1,0},{2,1},{3,2},{4,7},{5,4},{6,5},{7,6},{8,11},{9,8},{10,9... | collective-permute-start | bytes 3145736 | tf_op jit(solution)/shard_map/ppermute | solution.py:67
  125.3 19.6 %collective-permute-start.11 = (bf16[256,2048]{1,0:T(8,128)(2,1)S(1)}, bf16[256,2048]{1,0:T(8,128)(2,1)S(1)}, u32[]{:S(2)}, u32[]{:S(2)}) collective-permute-start(bf16[256,2048]{1,0:T(8,128)(2,1)S(1)} %part_ladder.11), channel_id=1, source_target_pairs={{0,1},{1,2},{2,3},{3,0},{4,5},{5,6},{6,7},{7,4},{8,9},{9,10},{10,1... | collective-permute-start | bytes 3145736 | tf_op jit(solution)/shard_map/ppermute | solution.py:67
  128.4 19.6 %collective-permute-start.14 = (bf16[256,2048]{1,0:T(8,128)(2,1)S(1)}, bf16[256,2048]{1,0:T(8,128)(2,1)S(1)}, u32[]{:S(2)}, u32[]{:S(2)}) collective-permute-start(bf16[256,2048]{1,0:T(8,128)(2,1)S(1)} %part_ladder.15), channel_id=1, source_target_pairs={{0,3},{1,0},{2,1},{3,2},{4,7},{5,4},{6,5},{7,6},{8,11},{9,8},{10,9... | collective-permute-start | bytes 3145736 | tf_op jit(solution)/shard_map/ppermute | solution.py:67

commit v4 on v3

v4 whole, which is shorter than its diff:
```python
import functools

import jax
import jax.numpy as jnp
from jax import lax
from jax.experimental import pallas as pl
from jax.experimental.pallas import tpu as pltpu
from jax.sharding import PartitionSpec as P

NB = 32
NF = 64
NQ = 64

HUBBARD = 2.0
TEMPER = 0.25
PI_VALUE = 3.141592653589793

AXES = ("tq", "slab")
DEVICES = 128
CAP = 3
ROWS = 256
WIDTH = 4096
LANES = 128
TILES = WIDTH // LANES
LABELS = CAP * TILES
CHUNK = LABELS + 8
SIDE = 4
HALF = WIDTH // 2
CUT = 1024
MIB = 1024 * 1024


def bubble_kernel(mom_ref, bose_ref, energy_ref, table_ref, out_ref):
    exact = functools.partial(
        jnp.dot, precision=lax.Precision.HIGHEST, preferred_element_type=jnp.float32
    )
    energies = jnp.broadcast_to(energy_ref[...], (8, NQ))
    partner = table_ref[pl.ds(mom_ref[0], 1), :]
    picker = lax.broadcasted_iota(jnp.int32, (NQ, NQ), 0) == partner
    pair = exact(energies, picker.astype(jnp.float32))
    first = lax.broadcasted_iota(jnp.int32, (8, NQ), 0) == 0
    column = lax.broadcasted_iota(jnp.int32, (NQ, WIDTH), 1)
    spread = lax.broadcasted_iota(jnp.int32, (NQ, WIDTH), 0) == column // NF
    bands = exact(jnp.where(first, energies, pair), spread.astype(jnp.float32))
    band_own, band_pair = bands[:1], bands[1:2]
    freq = lax.broadcasted_iota(jnp.int32, (1, WIDTH), 1) % NF - NF // 2
    fermi = PI_VALUE * TEMPER * (2.0 * freq.astype(jnp.float32) + 1.0)
    bose = (bose_ref[0] - NB // 2).astype(jnp.float32) * (2.0 * PI_VALUE * TEMPER)
    other = bose - fermi
    top = TEMPER * (band_own * band_pair - fermi * other)
    below = (fermi * fermi + band_own * band_own) * (other * other + band_pair * band_pair)
    out_ref[...] = top / below


def pairs_along(axis_of_core, step):
    pairs = []
    for tq in range(8):
        axis = axis_of_core[tq % 2]
        for x in range(SIDE):
            for y in range(SIDE):
                to_x = (x + step) % SIDE if axis == 0 else x
                to_y = (y + step) % SIDE if axis == 1 else y
                pairs.append(((tq * SIDE + x) * SIDE + y, (tq * SIDE + to_x) * SIDE + to_y))
    return pairs


def move_g(array, step):
    return lax.ppermute(array, AXES, pairs_along((0, 1), step))


def move_h(array, step):
    return lax.ppermute(array, AXES, pairs_along((1, 0), step))


def one_hot(flags):
    return flags.astype(jnp.bfloat16)


def row_slots(target_ref):
    dest = target_ref[...] // ROWS
    member = lax.broadcasted_iota(jnp.int32, (DEVICES, ROWS), 0) == dest
    before = one_hot(
        lax.broadcasted_iota(jnp.int32, (ROWS, ROWS), 0)
        < lax.broadcasted_iota(jnp.int32, (ROWS, ROWS), 1)
    )
    count = jnp.dot(one_hot(member), before, preferred_element_type=jnp.float32)
    return dest, member, before, count


def read_codes(placer, values):
    return lax.dot_general(
        placer,
        jnp.broadcast_to(values, (LANES, ROWS)).astype(jnp.bfloat16),
        (((1,), (1,)), ((), ())),
        preferred_element_type=jnp.float32,
    )


def labels(*columns):
    rows = columns[0].shape[0]
    lane = lax.broadcasted_iota(jnp.int32, (rows, LANES), 1)
    label = jnp.zeros((rows, LANES), jnp.float32)
    for at, column in enumerate(columns):
        label = jnp.where(lane == at, column, label)
    return label


def fetch_rows(rows_ref, held, sems):
    quarter = WIDTH // 4
    copies = []
    for at in range(4):
        columns = pl.ds(at * quarter, quarter)
        copies.append(
            pltpu.make_async_copy(rows_ref.at[:, columns], held.at[:, columns], sems.at[at])
        )
        copies[-1].start()
    return copies


def place_columns(shift_ref, held, copies, placer, put):
    shift = jnp.transpose(jnp.broadcast_to(shift_ref[...].astype(jnp.float32), (LANES, ROWS)))
    shift = shift.astype(jnp.int32)
    lane = lax.broadcasted_iota(jnp.int32, (ROWS, LANES), 1)
    from_freq = lane % NF - shift
    valid = (from_freq >= 0) & (from_freq < NF)
    from_lane = jnp.where(valid, lane - shift, lane)
    for pair in range(TILES // 2):
        if pair % (TILES // 8) == 0:
            copies[pair // (TILES // 8)].wait()
        moved = []
        for tile in (2 * pair, 2 * pair + 1):
            block = held[:, tile * LANES : (tile + 1) * LANES].astype(jnp.float32)
            block = jnp.take_along_axis(block, from_lane, axis=1, mode="promise_in_bounds")
            moved.append(jnp.where(valid, block, 0.0).astype(jnp.bfloat16))
        placed = jnp.dot(
            placer, jnp.concatenate(moved, axis=1), preferred_element_type=jnp.float32
        )
        for half in range(2):
            put(2 * pair + half, placed[:, half * LANES : (half + 1) * LANES])


def send_out(wide, packed, out_ref, sem, size, parts):
    copies = []
    rows = size // parts
    for at in range(parts):
        part = pl.ds(at * rows, rows)
        packed[part, :] = wide[part, :].astype(jnp.bfloat16)
        copies.append(pltpu.make_async_copy(packed.at[part, :], out_ref.at[part, :], sem.at[at]))
        copies[-1].start()
    return copies


def place_kernel(
    target_ref, shift_ref, rows_ref, out_ref, held, wide, packed, in_sems, out_sems
):
    copies = fetch_rows(rows_ref, held, in_sems)
    _, member, _, count = row_slots(target_ref)
    placer = jnp.concatenate([one_hot(member & (count == k)) for k in range(CAP)], axis=0)

    def put(tile, placed):
        for k in range(CAP):
            wide[pl.ds(k * TILES + tile, DEVICES, stride=CHUNK), :] = placed[
                k * DEVICES : (k + 1) * DEVICES
            ]

    place_columns(shift_ref, held, copies, placer, put)
    codes = read_codes(placer, target_ref[...] % ROWS + 1)
    wide[pl.ds(LABELS, DEVICES, stride=CHUNK), :] = labels(
        *(codes[k * DEVICES : (k + 1) * DEVICES] for k in range(CAP))
    )
    for copy in send_out(wide, packed, out_ref, out_sems, DEVICES * CHUNK, 4):
        copy.wait()


def collect_kernel(
    where_ref, bubble_ref, box_ref, gamma_ref, w0, w1, w2, w3,
    box, wide, gamma_held, in_sems, out_sems,
):
    parts = 8
    rows = DEVICES * CHUNK // parts
    copies = []
    for at in range(parts):
        part = pl.ds(at * rows, rows)
        copies.append(
            pltpu.make_async_copy(box_ref.at[part, :], box.at[part, :], in_sems.at[at])
        )
        copies[-1].start()
    g, h, along_g, along_h = (where_ref[i] for i in range(4))
    for at in range(parts):
        copies[at].wait()
        part = pl.ds(at * rows, rows)
        wide[part, :] = box[part, :].astype(jnp.float32)
    label = jnp.transpose(wide[pl.ds(LABELS, DEVICES, stride=CHUNK), :]).astype(jnp.int32)
    row_of = lax.broadcasted_iota(jnp.int32, (ROWS, DEVICES), 0) + 1
    collector = jnp.concatenate([one_hot(row_of == label[k : k + 1]) for k in range(CAP)], axis=1)

    copies = []
    for d, w_ref in enumerate((w0, w1, w2, w3)):
        for o in range(SIDE):
            slab = ((g + o) % SIDE) * along_g + ((h + d) % SIDE) * along_h
            columns = pl.ds(pl.multiple_of(slab * ROWS, ROWS), ROWS)
            came = []
            for k in range(CAP):
                halves = [
                    wide[pl.ds(k * TILES + slab * 2 + half, DEVICES, stride=CHUNK), :]
                    for half in range(2)
                ]
                came.append(jnp.concatenate(halves, axis=1).astype(jnp.bfloat16))
            summed = jnp.dot(
                collector, jnp.concatenate(came, axis=0), preferred_element_type=jnp.float32
            )
            gamma = HUBBARD + summed
            at = d * SIDE + o
            gamma_held[at] = gamma
            copies.append(
                pltpu.make_async_copy(
                    gamma_held.at[at], gamma_ref.at[:, columns], out_sems.at[at]
                )
            )
            copies[-1].start()
            w_ref[o] = (gamma * bubble_ref[:, columns]).astype(jnp.bfloat16)
    for copy in copies:
        copy.wait()


def ladder_kernel(parts, a_ref, *refs):
    out_ref = refs[-1]
    total = jnp.dot(a_ref[0], refs[0][...], preferred_element_type=jnp.float32)
    for o in range(1, SIDE):
        block = jnp.concatenate([refs[2 * o - 1][...], refs[2 * o][...]], axis=0)
        total += jnp.dot(a_ref[o], block, preferred_element_type=jnp.float32)
    for other in refs[parts:-1]:
        total += other[...].astype(jnp.float32)
    out_ref[...] = total.astype(out_ref.dtype)


def part_ladder(weighted, full_parts, side, dtype, *others):
    steps = HALF // CUT

    def columns(rows, first):
        return pl.BlockSpec((rows, CUT), lambda n: (0, first + n))

    return pl.pallas_call(
        functools.partial(ladder_kernel, len(full_parts)),
        grid=(steps,),
        in_specs=[pl.BlockSpec((SIDE, ROWS, ROWS), lambda n: (0, 0, 0))]
        + [columns(part.shape[0], side * steps) for part in full_parts]
        + [columns(ROWS, 0) for _ in others],
        out_specs=columns(ROWS, 0),
        out_shape=jax.ShapeDtypeStruct((ROWS, HALF), dtype),
        compiler_params=pltpu.CompilerParams(vmem_limit_bytes=14 * MIB),
        cost_estimate=pl.CostEstimate(
            flops=2 * ROWS * 4 * ROWS * HALF, bytes_accessed=6 * MIB, transcendentals=0
        ),
        name="part_ladder",
    )(weighted, *full_parts, *others)


def join_kernel(*refs):
    left, right, out_ref = refs[-3:]
    out_ref[...] = left[...] + right[...].astype(jnp.float32)


def join(side, own, other, into=()):
    steps = HALF // CUT
    part = pl.BlockSpec((ROWS, CUT), lambda n: (0, n))
    return pl.pallas_call(
        join_kernel,
        grid=(steps,),
        in_specs=[pl.BlockSpec(memory_space=pl.ANY)] * len(into) + [part, part],
        out_specs=pl.BlockSpec((ROWS, CUT), lambda n: (0, side * steps + n)),
        out_shape=jax.ShapeDtypeStruct((ROWS, WIDTH), jnp.float32),
        input_output_aliases={0: 0} if into else {},
        compiler_params=pltpu.CompilerParams(vmem_limit_bytes=8 * MIB),
        cost_estimate=pl.CostEstimate(
            flops=ROWS * HALF, bytes_accessed=5 * MIB, transcendentals=0
        ),
        name="join",
    )(*into, own, other)


def per_device(vert_ph, full_pp, target, shift, trans_mom, trans_bose, energies, pair_table):
    tq = lax.axis_index("tq")
    slab = lax.axis_index("slab")
    core = tq % 2
    x, y = slab // SIDE, slab % SIDE
    g = jnp.where(core == 0, x, y)
    h = jnp.where(core == 0, y, x)
    along_g = jnp.where(core == 0, SIDE, 1)
    where = jnp.stack([g, h, along_g, SIDE + 1 - along_g]).astype(jnp.int32)

    full = full_pp.reshape(ROWS, WIDTH)
    top, low = full[: ROWS // 2], full[ROWS // 2 :]
    left_top = move_g(top, 1)
    right_low = move_g(low, 3)
    left_low = move_g(low, 1)
    right_top = move_g(top, 3)

    whole = pl.BlockSpec(memory_space=pltpu.VMEM)
    hbm = pl.BlockSpec(memory_space=pltpu.HBM)
    slots = (DEVICES * CHUNK, LANES)
    payload = pl.pallas_call(
        place_kernel,
        in_specs=[whole, whole, hbm],
        out_specs=hbm,
        out_shape=jax.ShapeDtypeStruct(slots, jnp.bfloat16),
        scratch_shapes=[
            pltpu.VMEM((ROWS, WIDTH), jnp.bfloat16),
            pltpu.VMEM(slots, jnp.float32),
            pltpu.VMEM(slots, jnp.bfloat16),
            pltpu.SemaphoreType.DMA((4,)),
            pltpu.SemaphoreType.DMA((4,)),
        ],
        compiler_params=pltpu.CompilerParams(vmem_limit_bytes=60 * MIB),
        cost_estimate=pl.CostEstimate(
            flops=2 * 384 * ROWS * WIDTH, bytes_accessed=5 * MIB, transcendentals=0
        ),
        name="place",
    )(target, shift, vert_ph.reshape(ROWS, WIDTH))
    arrived = lax.all_to_all(
        payload.reshape(DEVICES, CHUNK, LANES), AXES, split_axis=0, concat_axis=0, tiled=True
    ).reshape(DEVICES * CHUNK, LANES)

    far_top = move_g(left_top, 1)
    far_low = move_g(right_low, 3)
    arrived, left_low, right_top = lax.optimization_barrier((arrived, left_low, right_top))
    full_parts = (full, right_top, right_low, far_top, far_low, left_top, left_low)

    scalar = pl.BlockSpec(memory_space=pltpu.SMEM)
    pair_bubble = pl.pallas_call(
        bubble_kernel,
        in_specs=[scalar, scalar, whole, whole],
        out_specs=whole,
        out_shape=jax.ShapeDtypeStruct((1, WIDTH), jnp.float32),
        compiler_params=pltpu.CompilerParams(vmem_limit_bytes=16 * MIB),
        cost_estimate=pl.CostEstimate(
            flops=10**11, bytes_accessed=1024 * MIB, transcendentals=0
        ),
        name="bubble",
    )(trans_mom, trans_bose, energies.reshape(1, NQ), pair_table)

    block = jax.ShapeDtypeStruct((SIDE, ROWS, ROWS), jnp.bfloat16)
    gamma, own, w1, w2, w3 = pl.pallas_call(
        collect_kernel,
        in_specs=[pl.BlockSpec(memory_space=pltpu.SMEM), whole, hbm],
        out_specs=[hbm] + [whole] * 4,
        out_shape=[jax.ShapeDtypeStruct((ROWS, WIDTH), jnp.float32)] + [block] * 4,
        scratch_shapes=[
            pltpu.VMEM(slots, jnp.bfloat16),
            pltpu.VMEM(slots, jnp.float32),
            pltpu.VMEM((SIDE * SIDE, ROWS, ROWS), jnp.float32),
            pltpu.SemaphoreType.DMA((8,)),
            pltpu.SemaphoreType.DMA((SIDE * SIDE,)),
        ],
        compiler_params=pltpu.CompilerParams(vmem_limit_bytes=24 * MIB),
        cost_estimate=pl.CostEstimate(
            flops=2 * 384 * ROWS * WIDTH, bytes_accessed=9 * MIB, transcendentals=0
        ),
        name="collect",
    )(where, pair_bubble, arrived)

    part = functools.partial(part_ladder, full_parts=full_parts)
    bf16, f32 = jnp.bfloat16, jnp.float32
    from_far, from_low, from_high = move_h(w2, 2), move_h(w1, 1), move_h(w3, 3)
    far_left = move_h(part(from_far, side=0, dtype=bf16), 1)
    from_far, from_low, from_high = lax.optimization_barrier((from_far, from_low, from_high))
    far_right = move_h(part(from_far, side=1, dtype=bf16), 3)
    high_right = move_h(part(from_high, side=1, dtype=bf16), 1)
    low_left = move_h(part(from_low, side=0, dtype=bf16), 3)
    high_left = move_h(part_ladder(from_high, full_parts, 0, bf16, far_left), 1)
    low_right = move_h(part_ladder(from_low, full_parts, 1, bf16, far_right), 3)
    own_left = part_ladder(own, full_parts, 0, f32, low_left)
    own_right = part_ladder(own, full_parts, 1, f32, high_right)
    ladder = join(0, own_left, high_left)
    ladder = join(1, own_right, low_right, (ladder,))
    return gamma[None], ladder[None]


def solution(mesh):
    in_specs = (
        P("tq", "slab", None),
        P("tq", "slab", None),
        P("tq", "slab"),
        P("tq", "slab"),
        P("tq"),
        P("tq"),
        P(),
        P(),
    )
    out_specs = (P("tq", "slab", None), P("tq", "slab", None))
    return jax.shard_map(
        per_device, mesh=mesh, in_specs=in_specs, out_specs=out_specs, check_vma=False
    )
```

time: 151 us -> 138 us (0.914)
  starting transfers between devices: 36.7 us -> 30.2 us
  waiting for transfers between devices: 69.9 us -> 63.8 us
  local copies, waits for them, and re-layouts: 7.15 us -> 3.08 us
  Pallas kernels: 34.5 us -> 38.4 us
    ppermute x6, waiting for transfers between devices: 48.4 us -> 11.5 us  [move_g(): return lax.ppermute(array, AXES, pairs_along((0, 1), step))]
    all_to_all x1, waiting for transfers between devices: 0.01 us -> 31.3 us  [per_device(): lax.all_to_all(payload.reshape(DEVICES, CHUNK, LANES), AXES, split_axis=0...]
    ppermute x9, starting transfers between devices: 16.6 us -> 11.2 us  [move_h(): return lax.ppermute(array, AXES, pairs_along((1, 0), step))]
    pallas_call x2 -> x4, Pallas kernels: 5.51 us -> 10.4 us  [the longest x1 6.46 us: per_device(): pl.pallas_call(place_kernel, in_specs=[whole, whole, hbm], out_specs=hbm,...]
    unnamed x12 -> x6, local copies, waits for them, and re-layouts: 4.03 us -> 0.02 us
    all_to_all x1, starting transfers between devices: 11.6 us -> 9.2 us  [per_device(): lax.all_to_all(payload.reshape(DEVICES, CHUNK, LANES), AXES, split_axis=0...]
    slice x1, local copies, waits for them, and re-layouts: 1.55 us -> 3.06 us  [per_device(): top, low = (full[:ROWS // 2], full[ROWS // 2:])]
  transfers between devices with their start and end apart: 16 -> 16, of which waited for: 11 -> 11; matrix products, arithmetic and copies ran while one was open for 2% -> 0% of each run, Pallas kernels for 17% -> 27%
where the time goes in v4:
time: 138 us
  waiting for transfers between devices  63.8 us (46%)
  Pallas kernels  38.4 us (28%)
  starting transfers between devices  30.2 us (22%)
  local copies, waits for them, and re-layouts  3.08 us (2%)
  between operations  2.11 us (2%)
    all_to_all x1, waiting for transfers between devices, per_device(): lax.all_to_all(payload.reshape(DEVICES, CHUNK, LANES), AXES, split_axis=0...  31.3 us
    pallas_call x8, Pallas kernels, part_ladder(): pl.pallas_call(functools.partial(ladder_kernel, len(full_parts)), grid=(s...  22.7 us
    ppermute x9, waiting for transfers between devices, move_h(): return lax.ppermute(array, AXES, pairs_along((1, 0), step))  21 us
    ppermute x6, waiting for transfers between devices, move_g(): return lax.ppermute(array, AXES, pairs_along((0, 1), step))  11.5 us
    ppermute x9, starting transfers between devices, move_h(): return lax.ppermute(array, AXES, pairs_along((1, 0), step))  11.2 us
    ppermute x6, starting transfers between devices, move_g(): return lax.ppermute(array, AXES, pairs_along((0, 1), step))  9.78 us
    all_to_all x1, starting transfers between devices, per_device(): lax.all_to_all(payload.reshape(DEVICES, CHUNK, LANES), AXES, split_axis=0...  9.2 us
    pallas_call x1, Pallas kernels, per_device(): pl.pallas_call(place_kernel, in_specs=[whole, whole, hbm], out_specs=hbm,...  6.46 us
  transfers between devices with their start and end apart: 16, of which 11 were waited for; matrix products, arithmetic and copies ran while one was open for 0% of the time, Pallas kernels for 27%

profile of v4, /device:TPU:0, one launch (start us, length us, event | category | flops | bytes accessed | tf_op | source)
XLA Modules:
  0.0 137.6 jit_solution(14021530486376353164)
XLA Ops:
  0.6 3.1 %slice_bitcast_fusion = (bf16[128,4096]{1,0:T(8,128)(2,1)}, bf16[128,4096]{1,0:T(8,128)(2,1)}) fusion(bf16[1,256,4096]{2,1,0:T(8,128)(2,1)} %param.9), kind=kLoop, calls=%fused_computation | loop fusion | bytes 4194304 | tf_op jit(solution)/shard_map/slice | solution.py:293
  7.3 2.9 %collective-permute-start.1 = (bf16[128,4096]{1,0:T(8,128)(2,1)}, bf16[128,4096]{1,0:T(8,128)(2,1)}, u32[]{:S(2)}, u32[]{:S(2)}) collective-permute-start(bf16[128,4096]{1,0:T(8,128)(2,1)} %get-tuple-element.24), channel_id=1, source_target_pairs={{0,12},{1,13},{2,14},{3,15},{4,0},{5,1},{6,2},{7,3},{8,4},{9,5},{1... | collective-permute-start | bytes 3145736 | tf_op jit(solution)/shard_map/ppermute | solution.py:68
  10.2 6.5 %place.1 = bf16[13312,128]{1,0:T(8,128)(2,1)} custom-call(s32[1,256]{1,0:T(1,128)} %target_ref.1, s32[1,256]{1,0:T(1,128)} %shift_ref.1, bf16[256,4096]{1,0:T(8,128)(2,1)} %bitcast.26), custom_call_target="tpu_custom_call" | custom-call | flops 805306368 | bytes 5242880 | tf_op jit(solution)/shard_map/place/pallas_call | solution.py:302
  16.7 9.2 %all-to-all-start = ((bf16[128,104,128]{2,1,0:T(8,128)(2,1)}), bf16[128,104,128]{2,1,0:T(8,128)(2,1)}, u32[]{:S(2)}, u32[]{:S(2)}) async-start(bf16[128,104,128]{2,1,0:T(8,128)(2,1)} %bitcast.25), calls=%async_computation | async-start | bytes 6815744 | tf_op jit(solution)/shard_map/all_to_all | solution.py:320
  28.1 2.3 %collective-permute-start.5 = (bf16[128,4096]{1,0:T(8,128)(2,1)}, bf16[128,4096]{1,0:T(8,128)(2,1)}, u32[]{:S(2)}, u32[]{:S(2)}) collective-permute-start(bf16[128,4096]{1,0:T(8,128)(2,1)} %collective-permute-done.2.refs_2_), channel_id=1, source_target_pairs={{0,12},{1,13},{2,14},{3,15},{4,0},{5,1},{6,2},{7,3},{8,4},{9,5},{1... | collective-permute-start | bytes 3145736 | tf_op jit(solution)/shard_map/ppermute | solution.py:68
  31.2 5.2 %collective-permute-done.refs_6_ = bf16[128,4096]{1,0:T(8,128)(2,1)} collective-permute-done((bf16[128,4096]{1,0:T(8,128)(2,1)}, bf16[128,4096]{1,0:T(8,128)(2,1)}, u32[]{:S(2)}, u32[]{:S(2)}) %collective-permute-start) | collective-permute-done | bytes 1048608 | tf_op jit(solution)/shard_map/ppermute | solution.py:68
  36.4 6.3 %collective-permute-done.1.refs_1_ = bf16[128,4096]{1,0:T(8,128)(2,1)} collective-permute-done((bf16[128,4096]{1,0:T(8,128)(2,1)}, bf16[128,4096]{1,0:T(8,128)(2,1)}, u32[]{:S(2)}, u32[]{:S(2)}) %collective-permute-start.1) | collective-permute-done | bytes 1048608 | tf_op jit(solution)/shard_map/ppermute | solution.py:68
  42.7 31.3 %all-to-all-done = bf16[128,104,128]{2,1,0:T(8,128)(2,1)} async-done(((bf16[128,104,128]{2,1,0:T(8,128)(2,1)}), bf16[128,104,128]{2,1,0:T(8,128)(2,1)}, u32[]{:S(2)}, u32[]{:S(2)}) %all-to-all-start) | async-done | bytes 3407904 | tf_op jit(solution)/shard_map/all_to_all | solution.py:320
  74.0 5.3 %collect.1 = (f32[256,4096]{1,0:T(8,128)}, bf16[4,256,256]{2,1,0:T(8,128)(2,1)S(1)}, bf16[4,256,256]{2,1,0:T(8,128)(2,1)S(1)}, bf16[4,256,256]{2,1,0:T(8,128)(2,1)S(1)}, bf16[4,256,256]{2,1,0:T(8,128)(2,1)S(1)}) custom-call(s32[4]{0:T(128)S(1)} %pad_add_fusion.where_ref, f32[1,4096]{1,0:T(1,128)S(1)} %bubble.1.bubble_ref, bf16[13312,128]{1,0:T(8,128)(2,1)} %bitcast.7.box_ref), custom_call_target="tpu_custom_call" | custom-call | flops 805306368 | bytes 9437184 | tf_op jit(solution)/shard_map/collect/pallas_call | solution.py:343
  80.7 2.6 %collective-permute-start.8 = (bf16[4,256,256]{2,1,0:T(8,128)(2,1)S(1)}, bf16[4,256,256]{2,1,0:T(8,128)(2,1)S(1)}, u32[]{:S(2)}, u32[]{:S(2)}) collective-permute-start(bf16[4,256,256]{2,1,0:T(8,128)(2,1)S(1)} %get-tuple-element.20), channel_id=1, source_target_pairs={{0,3},{1,0},{2,1},{3,2},{4,7},{5,4},{6,5},{7,6},{8,11},{9,8},{10,9... | collective-permute-start | bytes 1572872 | tf_op jit(solution)/shard_map/ppermute | solution.py:72
  83.3 6.8 %collective-permute-done.6.a_ref = bf16[4,256,256]{2,1,0:T(8,128)(2,1)S(1)} collective-permute-done((bf16[4,256,256]{2,1,0:T(8,128)(2,1)S(1)}, bf16[4,256,256]{2,1,0:T(8,128)(2,1)S(1)}, u32[]{:S(2)}, u32[]{:S(2)}) %collective-permute-start.6) | collective-permute-done | bytes 524320 | tf_op jit(solution)/shard_map/ppermute | solution.py:72
  90.2 2.8 %part_ladder.10 = bf16[256,2048]{1,0:T(8,128)(2,1)S(1)} custom-call(bf16[4,256,256]{2,1,0:T(8,128)(2,1)S(1)} %collective-permute-done.6.a_ref, bf16[256,4096]{1,0:T(8,128)(2,1)S(1)} %bitcast.15, bf16[128,4096]{1,0:T(8,128)(2,1)} %collective-permute-done.1.refs_1_, bf16[128,4096]{1,0:T(8,128)(2,1)} %collective-permute-done.2.refs_2_, ...), custom_call_target="tpu_custom_call" | custom-call | flops 1073741824 | bytes 6291456 | tf_op jit(solution)/shard_map/part_ladder/pallas_call | solution.py:243
  95.7 2.8 %part_ladder.14 = bf16[256,2048]{1,0:T(8,128)(2,1)S(1)} custom-call(bf16[4,256,256]{2,1,0:T(8,128)(2,1)S(1)} %collective-permute-done.6.a_ref, bf16[256,4096]{1,0:T(8,128)(2,1)S(1)} %bitcast.16, bf16[128,4096]{1,0:T(8,128)(2,1)} %collective-permute-done.1.refs_1_, bf16[128,4096]{1,0:T(8,128)(2,1)} %collective-permute-done.2.refs_2_, ...), custom_call_target="tpu_custom_call" | custom-call | flops 1073741824 | bytes 6291456 | tf_op jit(solution)/shard_map/part_ladder/pallas_call | solution.py:243
  99.4 2.8 %part_ladder.12 = bf16[256,2048]{1,0:T(8,128)(2,1)S(1)} custom-call(bf16[4,256,256]{2,1,0:T(8,128)(2,1)S(1)} %collective-permute-done.8.a_ref, bf16[256,4096]{1,0:T(8,128)(2,1)S(1)} %bitcast.17, bf16[128,4096]{1,0:T(8,128)(2,1)} %collective-permute-done.1.refs_1_, bf16[128,4096]{1,0:T(8,128)(2,1)} %collective-permute-done.2.refs_2_, ...), custom_call_target="tpu_custom_call" | custom-call | flops 1073741824 | bytes 6291456 | tf_op jit(solution)/shard_map/part_ladder/pallas_call | solution.py:243
  103.7 2.8 %part_ladder.8 = bf16[256,2048]{1,0:T(8,128)(2,1)S(1)} custom-call(bf16[4,256,256]{2,1,0:T(8,128)(2,1)S(1)} %collective-permute-done.7.a_ref, bf16[256,4096]{1,0:T(8,128)(2,1)S(1)} %bitcast.18, bf16[128,4096]{1,0:T(8,128)(2,1)} %collective-permute-done.1.refs_1_, bf16[128,4096]{1,0:T(8,128)(2,1)} %collective-permute-done.2.refs_2_, ...), custom_call_target="tpu_custom_call" | custom-call | flops 1073741824 | bytes 6291456 | tf_op jit(solution)/shard_map/part_ladder/pallas_call | solution.py:243
  106.5 1.9 %collective-permute-start.9 = (bf16[256,2048]{1,0:T(8,128)(2,1)S(1)}, bf16[256,2048]{1,0:T(8,128)(2,1)S(1)}, u32[]{:S(2)}, u32[]{:S(2)}) collective-permute-start(bf16[256,2048]{1,0:T(8,128)(2,1)S(1)} %part_ladder.8), channel_id=1, source_target_pairs={{0,3},{1,0},{2,1},{3,2},{4,7},{5,4},{6,5},{7,6},{8,11},{9,8},{10,9... | collective-permute-start | bytes 3145736 | tf_op jit(solution)/shard_map/ppermute | solution.py:72
  109.1 2.8 %part_ladder.11 = bf16[256,2048]{1,0:T(8,128)(2,1)S(1)} custom-call(bf16[4,256,256]{2,1,0:T(8,128)(2,1)S(1)} %collective-permute-done.8.a_ref, bf16[256,4096]{1,0:T(8,128)(2,1)S(1)} %bitcast.19, bf16[128,4096]{1,0:T(8,128)(2,1)} %collective-permute-done.1.refs_1_, bf16[128,4096]{1,0:T(8,128)(2,1)} %collective-permute-done.2.refs_2_, ...), custom_call_target="tpu_custom_call" | custom-call | flops 1073741824 | bytes 6291456 | tf_op jit(solution)/shard_map/part_ladder/pallas_call | solution.py:243
  113.5 2.8 %part_ladder.15 = bf16[256,2048]{1,0:T(8,128)(2,1)S(1)} custom-call(bf16[4,256,256]{2,1,0:T(8,128)(2,1)S(1)} %collective-permute-done.7.a_ref, bf16[256,4096]{1,0:T(8,128)(2,1)S(1)} %bitcast.20, bf16[128,4096]{1,0:T(8,128)(2,1)} %collective-permute-done.1.refs_1_, bf16[128,4096]{1,0:T(8,128)(2,1)} %collective-permute-done.2.refs_2_, ...), custom_call_target="tpu_custom_call" | custom-call | flops 1073741824 | bytes 6291456 | tf_op jit(solution)/shard_map/part_ladder/pallas_call | solution.py:243
  116.4 1.9 %collective-permute-start.14 = (bf16[256,2048]{1,0:T(8,128)(2,1)S(1)}, bf16[256,2048]{1,0:T(8,128)(2,1)S(1)}, u32[]{:S(2)}, u32[]{:S(2)}) collective-permute-start(bf16[256,2048]{1,0:T(8,128)(2,1)S(1)} %part_ladder.15), channel_id=1, source_target_pairs={{0,3},{1,0},{2,1},{3,2},{4,7},{5,4},{6,5},{7,6},{8,11},{9,8},{10,9... | collective-permute-start | bytes 3145736 | tf_op jit(solution)/shard_map/ppermute | solution.py:72
  118.3 2.0 %collective-permute-done.12.refs_7_ = bf16[256,2048]{1,0:T(8,128)(2,1)S(1)} collective-permute-done((bf16[256,2048]{1,0:T(8,128)(2,1)S(1)}, bf16[256,2048]{1,0:T(8,128)(2,1)S(1)}, u32[]{:S(2)}, u32[]{:S(2)}) %collective-permute-start.12) | collective-permute-done | bytes 1048608 | tf_op jit(solution)/shard_map/ppermute | solution.py:72
  120.3 2.9 %part_ladder.13.refs_1_ = f32[256,2048]{1,0:T(8,128)S(1)} custom-call(bf16[4,256,256]{2,1,0:T(8,128)(2,1)S(1)} %get-tuple-element.15.a_ref, bf16[256,4096]{1,0:T(8,128)(2,1)S(1)} %bitcast.21, bf16[128,4096]{1,0:T(8,128)(2,1)} %collective-permute-done.1.refs_1_, bf16[128,4096]{1,0:T(8,128)(2,1)} %collective-permute-done.2.refs_2_, ...), custom_call_target="tpu_custom_call" | custom-call | flops 1073741824 | bytes 6291456 | tf_op jit(solution)/shard_map/part_ladder/pallas_call | solution.py:243
  124.8 2.9 %part_ladder.9.refs_0_ = f32[256,2048]{1,0:T(8,128)S(1)} custom-call(bf16[4,256,256]{2,1,0:T(8,128)(2,1)S(1)} %get-tuple-element.15.a_ref, bf16[256,4096]{1,0:T(8,128)(2,1)S(1)} %bitcast.22, bf16[128,4096]{1,0:T(8,128)(2,1)} %collective-permute-done.1.refs_1_, bf16[128,4096]{1,0:T(8,128)(2,1)} %collective-permute-done.2.refs_2_, ...), custom_call_target="tpu_custom_call" | custom-call | flops 1073741824 | bytes 6291456 | tf_op jit(solution)/shard_map/part_ladder/pallas_call | solution.py:243
  127.7 3.8 %collective-permute-done.11.refs_1_ = bf16[256,2048]{1,0:T(8,128)(2,1)S(1)} collective-permute-done((bf16[256,2048]{1,0:T(8,128)(2,1)S(1)}, bf16[256,2048]{1,0:T(8,128)(2,1)S(1)}, u32[]{:S(2)}, u32[]{:S(2)}) %collective-permute-start.11) | collective-permute-done | bytes 1048608 | tf_op jit(solution)/shard_map/ppermute | solution.py:72
  133.2 2.9 %collective-permute-done.14.refs_2_ = bf16[256,2048]{1,0:T(8,128)(2,1)S(1)} collective-permute-done((bf16[256,2048]{1,0:T(8,128)(2,1)S(1)}, bf16[256,2048]{1,0:T(8,128)(2,1)S(1)}, u32[]{:S(2)}, u32[]{:S(2)}) %collective-permute-start.14) | collective-permute-done | bytes 1048608 | tf_op jit(solution)/shard_map/ppermute | solution.py:72
  (29 shorter events, 18.9 us)
Async XLA Ops:
  3.7 23.5 %collective-permute-start.3 = (bf16[128,4096]{1,0:T(8,128)(2,1)}, bf16[128,4096]{1,0:T(8,128)(2,1)S(1)}, u32[]{:S(2)}, u32[]{:S(2)}) collective-permute-start(bf16[128,4096]{1,0:T(8,128)(2,1)} %get-tuple-element.24), channel_id=1, source_target_pairs={{0,4},{1,5},{2,6},{3,7},{4,8},{5,9},{6,10},{7,11},{8,12},{9,13},{1... | collective-permute-start | bytes 3145736 | tf_op jit(solution)/shard_map/ppermute | solution.py:68
  5.3 22.9 %collective-permute-start.2 = (bf16[128,4096]{1,0:T(8,128)(2,1)}, bf16[128,4096]{1,0:T(8,128)(2,1)}, u32[]{:S(2)}, u32[]{:S(2)}) collective-permute-start(bf16[128,4096]{1,0:T(8,128)(2,1)} %get-tuple-element.25), channel_id=1, source_target_pairs={{0,12},{1,13},{2,14},{3,15},{4,0},{5,1},{6,2},{7,3},{8,4},{9,5},{1... | collective-permute-start | bytes 3145736 | tf_op jit(solution)/shard_map/ppermute | solution.py:68
  6.9 29.5 %collective-permute-start = (bf16[128,4096]{1,0:T(8,128)(2,1)}, bf16[128,4096]{1,0:T(8,128)(2,1)}, u32[]{:S(2)}, u32[]{:S(2)}) collective-permute-start(bf16[128,4096]{1,0:T(8,128)(2,1)} %get-tuple-element.25), channel_id=1, source_target_pairs={{0,4},{1,5},{2,6},{3,7},{4,8},{5,9},{6,10},{7,11},{8,12},{9,13},{1... | collective-permute-start | bytes 3145736 | tf_op jit(solution)/shard_map/ppermute | solution.py:68
  7.3 35.4 %collective-permute-start.1 = (bf16[128,4096]{1,0:T(8,128)(2,1)}, bf16[128,4096]{1,0:T(8,128)(2,1)}, u32[]{:S(2)}, u32[]{:S(2)}) collective-permute-start(bf16[128,4096]{1,0:T(8,128)(2,1)} %get-tuple-element.24), channel_id=1, source_target_pairs={{0,12},{1,13},{2,14},{3,15},{4,0},{5,1},{6,2},{7,3},{8,4},{9,5},{1... | collective-permute-start | bytes 3145736 | tf_op jit(solution)/shard_map/ppermute | solution.py:68
  16.6 13.8 %copy-start.1 = (s32[64,64]{1,0:T(8,128)S(1)}, s32[64,64]{1,0:T(8,128)}, u32[]{:S(2)}) copy-start(s32[64,64]{1,0:T(8,128)} %table_ref.1) | copy-start | bytes 49156
  16.6 13.8 %copy-start.2 = (f32[64]{0:T(128)S(1)}, f32[64]{0:T(128)}, u32[]{:S(2)}) copy-start(f32[64]{0:T(128)} %param.14) | copy-start | bytes 772
  16.7 57.3 %all-to-all-start = ((bf16[128,104,128]{2,1,0:T(8,128)(2,1)}), bf16[128,104,128]{2,1,0:T(8,128)(2,1)}, u32[]{:S(2)}, u32[]{:S(2)}) async-start(bf16[128,104,128]{2,1,0:T(8,128)(2,1)} %bitcast.25), calls=%async_computation | async-start | bytes 6815744 | tf_op jit(solution)/shard_map/all_to_all | solution.py:320
  27.2 56.1 %collective-permute-start.4 = (bf16[128,4096]{1,0:T(8,128)(2,1)S(1)}, bf16[128,4096]{1,0:T(8,128)(2,1)}, u32[]{:S(2)}, u32[]{:S(2)}) collective-permute-start(bf16[128,4096]{1,0:T(8,128)(2,1)S(1)} %collective-permute-done.3.refs_5_), channel_id=1, source_target_pairs={{0,4},{1,5},{2,6},{3,7},{4,8},{5,9},{6,10},{7,11},{8,12},{9,13},{1... | collective-permute-start | bytes 3145736 | tf_op jit(solution)/shard_map/ppermute | solution.py:68
  28.1 55.2 %collective-permute-start.5 = (bf16[128,4096]{1,0:T(8,128)(2,1)}, bf16[128,4096]{1,0:T(8,128)(2,1)}, u32[]{:S(2)}, u32[]{:S(2)}) collective-permute-start(bf16[128,4096]{1,0:T(8,128)(2,1)} %collective-permute-done.2.refs_2_), channel_id=1, source_target_pairs={{0,12},{1,13},{2,14},{3,15},{4,0},{5,1},{6,2},{7,3},{8,4},{9,5},{1... | collective-permute-start | bytes 3145736 | tf_op jit(solution)/shard_map/ppermute | solution.py:68
  31.1 59.0 %copy-start = (bf16[1,256,4096]{2,1,0:T(8,128)(2,1)S(1)}, bf16[1,256,4096]{2,1,0:T(8,128)(2,1)}, u32[]{:S(2)}) copy-start(bf16[1,256,4096]{2,1,0:T(8,128)(2,1)} %param.9) | copy-start | bytes 6291460
  79.3 10.9 %collective-permute-start.6 = (bf16[4,256,256]{2,1,0:T(8,128)(2,1)S(1)}, bf16[4,256,256]{2,1,0:T(8,128)(2,1)S(1)}, u32[]{:S(2)}, u32[]{:S(2)}) collective-permute-start(bf16[4,256,256]{2,1,0:T(8,128)(2,1)S(1)} %get-tuple-element.18), channel_id=1, source_target_pairs={{0,2},{1,3},{2,0},{3,1},{4,6},{5,7},{6,4},{7,5},{8,10},{9,11},{10,... | collective-permute-start | bytes 1572872 | tf_op jit(solution)/shard_map/ppermute | solution.py:72
  80.1 15.6 %collective-permute-start.7 = (bf16[4,256,256]{2,1,0:T(8,128)(2,1)S(1)}, bf16[4,256,256]{2,1,0:T(8,128)(2,1)S(1)}, u32[]{:S(2)}, u32[]{:S(2)}) collective-permute-start(bf16[4,256,256]{2,1,0:T(8,128)(2,1)S(1)} %get-tuple-element.19), channel_id=1, source_target_pairs={{0,1},{1,2},{2,3},{3,0},{4,5},{5,6},{6,7},{7,4},{8,9},{9,10},{10,1... | collective-permute-start | bytes 1572872 | tf_op jit(solution)/shard_map/ppermute | solution.py:72
  80.7 15.0 %collective-permute-start.8 = (bf16[4,256,256]{2,1,0:T(8,128)(2,1)S(1)}, bf16[4,256,256]{2,1,0:T(8,128)(2,1)S(1)}, u32[]{:S(2)}, u32[]{:S(2)}) collective-permute-start(bf16[4,256,256]{2,1,0:T(8,128)(2,1)S(1)} %get-tuple-element.20), channel_id=1, source_target_pairs={{0,3},{1,0},{2,1},{3,2},{4,7},{5,4},{6,5},{7,6},{8,11},{9,8},{10,9... | collective-permute-start | bytes 1572872 | tf_op jit(solution)/shard_map/ppermute | solution.py:72
  93.0 16.1 %collective-permute-start.10 = (bf16[256,2048]{1,0:T(8,128)(2,1)S(1)}, bf16[256,2048]{1,0:T(8,128)(2,1)S(1)}, u32[]{:S(2)}, u32[]{:S(2)}) collective-permute-start(bf16[256,2048]{1,0:T(8,128)(2,1)S(1)} %part_ladder.10), channel_id=1, source_target_pairs={{0,1},{1,2},{2,3},{3,0},{4,5},{5,6},{6,7},{7,4},{8,9},{9,10},{10,1... | collective-permute-start | bytes 3145736 | tf_op jit(solution)/shard_map/ppermute | solution.py:72
  98.5 15.0 %collective-permute-start.13 = (bf16[256,2048]{1,0:T(8,128)(2,1)S(1)}, bf16[256,2048]{1,0:T(8,128)(2,1)S(1)}, u32[]{:S(2)}, u32[]{:S(2)}) collective-permute-start(bf16[256,2048]{1,0:T(8,128)(2,1)S(1)} %part_ladder.14), channel_id=1, source_target_pairs={{0,3},{1,0},{2,1},{3,2},{4,7},{5,4},{6,5},{7,6},{8,11},{9,8},{10,9... | collective-permute-start | bytes 3145736 | tf_op jit(solution)/shard_map/ppermute | solution.py:72
  102.2 18.1 %collective-permute-start.12 = (bf16[256,2048]{1,0:T(8,128)(2,1)S(1)}, bf16[256,2048]{1,0:T(8,128)(2,1)S(1)}, u32[]{:S(2)}, u32[]{:S(2)}) collective-permute-start(bf16[256,2048]{1,0:T(8,128)(2,1)S(1)} %part_ladder.12), channel_id=1, source_target_pairs={{0,1},{1,2},{2,3},{3,0},{4,5},{5,6},{6,7},{7,4},{8,9},{9,10},{10,1... | collective-permute-start | bytes 3145736 | tf_op jit(solution)/shard_map/ppermute | solution.py:72
  106.5 18.3 %collective-permute-start.9 = (bf16[256,2048]{1,0:T(8,128)(2,1)S(1)}, bf16[256,2048]{1,0:T(8,128)(2,1)S(1)}, u32[]{:S(2)}, u32[]{:S(2)}) collective-permute-start(bf16[256,2048]{1,0:T(8,128)(2,1)S(1)} %part_ladder.8), channel_id=1, source_target_pairs={{0,3},{1,0},{2,1},{3,2},{4,7},{5,4},{6,5},{7,6},{8,11},{9,8},{10,9... | collective-permute-start | bytes 3145736 | tf_op jit(solution)/shard_map/ppermute | solution.py:72
  111.9 19.6 %collective-permute-start.11 = (bf16[256,2048]{1,0:T(8,128)(2,1)S(1)}, bf16[256,2048]{1,0:T(8,128)(2,1)S(1)}, u32[]{:S(2)}, u32[]{:S(2)}) collective-permute-start(bf16[256,2048]{1,0:T(8,128)(2,1)S(1)} %part_ladder.11), channel_id=1, source_target_pairs={{0,1},{1,2},{2,3},{3,0},{4,5},{5,6},{6,7},{7,4},{8,9},{9,10},{10,1... | collective-permute-start | bytes 3145736 | tf_op jit(solution)/shard_map/ppermute | solution.py:72
  116.4 19.6 %collective-permute-start.14 = (bf16[256,2048]{1,0:T(8,128)(2,1)S(1)}, bf16[256,2048]{1,0:T(8,128)(2,1)S(1)}, u32[]{:S(2)}, u32[]{:S(2)}) collective-permute-start(bf16[256,2048]{1,0:T(8,128)(2,1)S(1)} %part_ladder.15), channel_id=1, source_target_pairs={{0,3},{1,0},{2,1},{3,2},{4,7},{5,4},{6,5},{7,6},{8,11},{9,8},{10,9... | collective-permute-start | bytes 3145736 | tf_op jit(solution)/shard_map/ppermute | solution.py:72

commit v5 on v4

--- a/solution.py
+++ b/solution.py
@@ -226,8 +226,8 @@
 def ladder_kernel(parts, a_ref, *refs):
     out_ref = refs[-1]
     total = jnp.dot(a_ref[0], refs[0][...], preferred_element_type=jnp.float32)
-    for o in range(1, SIDE):
-        block = jnp.concatenate([refs[2 * o - 1][...], refs[2 * o][...]], axis=0)
+    far = jnp.concatenate([refs[2][...], refs[3][...]], axis=0)
+    for o, block in ((1, refs[1][...]), (2, far), (3, refs[4][...])):
         total += jnp.dot(a_ref[o], block, preferred_element_type=jnp.float32)
     for other in refs[parts:-1]:
         total += other[...].astype(jnp.float32)
@@ -290,11 +290,11 @@
     where = jnp.stack([g, h, along_g, SIDE + 1 - along_g]).astype(jnp.int32)
 
     full = full_pp.reshape(ROWS, WIDTH)
-    top, low = full[: ROWS // 2], full[ROWS // 2 :]
-    left_top = move_g(top, 1)
-    right_low = move_g(low, 3)
-    left_low = move_g(low, 1)
-    right_top = move_g(top, 3)
+    left = move_g(full, 1)
+    right = move_g(full, 3)
+    far_top = move_g(left[: ROWS // 2], 1)
+    far_low = move_g(right[ROWS // 2 :], 3)
+    full_parts = (full, right, far_top, far_low, left)
 
     whole = pl.BlockSpec(memory_space=pltpu.VMEM)
     hbm = pl.BlockSpec(memory_space=pltpu.HBM)
@@ -321,10 +321,6 @@
         payload.reshape(DEVICES, CHUNK, LANES), AXES, split_axis=0, concat_axis=0, tiled=True
     ).reshape(DEVICES * CHUNK, LANES)
 
-    far_top = move_g(left_top, 1)
-    far_low = move_g(right_low, 3)
-    arrived, left_low, right_top = lax.optimization_barrier((arrived, left_low, right_top))
-    full_parts = (full, right_top, right_low, far_top, far_low, left_top, left_low)
 
     scalar = pl.BlockSpec(memory_space=pltpu.SMEM)
     pair_bubble = pl.pallas_call(

time: 138 us -> 135 us (0.978)
  waiting for transfers between devices: 63.8 us -> 60.1 us
  Pallas kernels: 38.4 us -> 37 us
    all_to_all x1, waiting for transfers between devices: 31.3 us -> 19.7 us  [per_device(): lax.all_to_all(payload.reshape(DEVICES, CHUNK, LANES), AXES, split_axis=0...]
    ppermute x6 -> x4, waiting for transfers between devices: 11.5 us -> 18.6 us  [move_g(): return lax.ppermute(array, AXES, pairs_along((0, 1), step))]
    pallas_call x8, Pallas kernels: 22.7 us -> 21.3 us  [part_ladder(): pl.pallas_call(functools.partial(ladder_kernel, len(full_parts)), grid=(s...]
    slice x1 -> x2, local copies, waits for them, and re-layouts: 3.06 us -> 3.44 us  [the longest x1 2.39 us: per_device(): far_low = move_g(right[ROWS // 2:], 3)]
    ppermute x6 -> x4, starting transfers between devices: 9.78 us -> 9.48 us  [move_g(): return lax.ppermute(array, AXES, pairs_along((0, 1), step))]
  transfers between devices with their start and end apart: 16 -> 14, of which waited for: 11 -> 11; matrix products, arithmetic and copies ran while one was open for 0% -> 3% of each run, Pallas kernels for 27% -> 26%
where the time goes in v5:
time: 135 us; the launch traced here: 134 us
  waiting for transfers between devices  60.1 us (45%)
  Pallas kernels  37 us (27%)
  starting transfers between devices  31.4 us (23%)
  local copies, waits for them, and re-layouts  3.46 us (3%)
  between operations  2.1 us (2%)
    ppermute x9, waiting for transfers between devices, move_h(): return lax.ppermute(array, AXES, pairs_along((1, 0), step))  21.8 us
    pallas_call x8, Pallas kernels, part_ladder(): pl.pallas_call(functools.partial(ladder_kernel, len(full_parts)), grid=(s...  21.3 us
    all_to_all x1, waiting for transfers between devices, per_device(): lax.all_to_all(payload.reshape(DEVICES, CHUNK, LANES), AXES, split_axis=0...  19.7 us
    ppermute x4, waiting for transfers between devices, move_g(): return lax.ppermute(array, AXES, pairs_along((0, 1), step))  18.6 us
    ppermute x9, starting transfers between devices, move_h(): return lax.ppermute(array, AXES, pairs_along((1, 0), step))  11.5 us
    all_to_all x1, starting transfers between devices, per_device(): lax.all_to_all(payload.reshape(DEVICES, CHUNK, LANES), AXES, split_axis=0...  10.4 us
    ppermute x4, starting transfers between devices, move_g(): return lax.ppermute(array, AXES, pairs_along((0, 1), step))  9.48 us
    pallas_call x1, Pallas kernels, per_device(): pl.pallas_call(place_kernel, in_specs=[whole, whole, hbm], out_specs=hbm,...  6.46 us
  transfers between devices with their start and end apart: 14, of which 11 were waited for; matrix products, arithmetic and copies ran while one was open for 3% of the time, Pallas kernels for 26%

profile of v5, /device:TPU:0, one launch (start us, length us, event | category | flops | bytes accessed | tf_op | source)
XLA Modules:
  0.0 134.2 jit_solution(13650903800227330725)
XLA Ops:
  3.9 6.5 %place.1 = bf16[13312,128]{1,0:T(8,128)(2,1)} custom-call(s32[1,256]{1,0:T(1,128)} %target_ref.1, s32[1,256]{1,0:T(1,128)} %shift_ref.1, bf16[256,4096]{1,0:T(8,128)(2,1)} %bitcast.24), custom_call_target="tpu_custom_call" | custom-call | flops 805306368 | bytes 5242880 | tf_op jit(solution)/shard_map/place/pallas_call | solution.py:302
  10.4 10.4 %all-to-all-start = ((bf16[128,104,128]{2,1,0:T(8,128)(2,1)}), bf16[128,104,128]{2,1,0:T(8,128)(2,1)}, u32[]{:S(2)}, u32[]{:S(2)}) async-start(bf16[128,104,128]{2,1,0:T(8,128)(2,1)} %bitcast.23), calls=%async_computation | async-start | bytes 6815744 | tf_op jit(solution)/shard_map/all_to_all | solution.py:320
  22.1 15.1 %collective-permute-done.1.refs_4_ = bf16[256,4096]{1,0:T(8,128)(2,1)S(1)} collective-permute-done((bf16[256,4096]{1,0:T(8,128)(2,1)}, bf16[256,4096]{1,0:T(8,128)(2,1)S(1)}, u32[]{:S(2)}, u32[]{:S(2)}) %collective-permute-start.1) | collective-permute-done | bytes 2097184 | tf_op jit(solution)/shard_map/ppermute | solution.py:68
  38.3 2.3 %collective-permute-start.2 = (bf16[128,4096]{1,0:T(8,128)(2,1)}, bf16[128,4096]{1,0:T(8,128)(2,1)S(1)}, u32[]{:S(2)}, u32[]{:S(2)}) collective-permute-start(bf16[128,4096]{1,0:T(8,128)(2,1)} %slice.8), channel_id=1, source_target_pairs={{0,4},{1,5},{2,6},{3,7},{4,8},{5,9},{6,10},{7,11},{8,12},{9,13},{1... | collective-permute-start | bytes 3145736 | tf_op jit(solution)/shard_map/ppermute | solution.py:68
  40.6 3.5 %collective-permute-done.refs_1_ = bf16[256,4096]{1,0:T(8,128)(2,1)} collective-permute-done((bf16[256,4096]{1,0:T(8,128)(2,1)}, bf16[256,4096]{1,0:T(8,128)(2,1)}, u32[]{:S(2)}, u32[]{:S(2)}) %collective-permute-start) | collective-permute-done | bytes 2097184 | tf_op jit(solution)/shard_map/ppermute | solution.py:68
  44.0 2.4 %slice.9 = bf16[128,4096]{1,0:T(8,128)(2,1)} slice(bf16[256,4096]{1,0:T(8,128)(2,1)} %collective-permute-done.refs_1_), slice={[128:256], [0:4096]} | slice | bytes 2097152 | tf_op jit(solution)/shard_map/slice | solution.py:296
  46.4 3.9 %collective-permute-start.3 = (bf16[128,4096]{1,0:T(8,128)(2,1)}, bf16[128,4096]{1,0:T(8,128)(2,1)}, u32[]{:S(2)}, u32[]{:S(2)}) collective-permute-start(bf16[128,4096]{1,0:T(8,128)(2,1)} %slice.9), channel_id=1, source_target_pairs={{0,12},{1,13},{2,14},{3,15},{4,0},{5,1},{6,2},{7,3},{8,4},{9,5},{1... | collective-permute-start | bytes 3145736 | tf_op jit(solution)/shard_map/ppermute | solution.py:68
  51.1 19.7 %all-to-all-done = bf16[128,104,128]{2,1,0:T(8,128)(2,1)} async-done(((bf16[128,104,128]{2,1,0:T(8,128)(2,1)}), bf16[128,104,128]{2,1,0:T(8,128)(2,1)}, u32[]{:S(2)}, u32[]{:S(2)}) %all-to-all-start) | async-done | bytes 3407904 | tf_op jit(solution)/shard_map/all_to_all | solution.py:320
  70.8 5.3 %collect.1 = (f32[256,4096]{1,0:T(8,128)}, bf16[4,256,256]{2,1,0:T(8,128)(2,1)S(1)}, bf16[4,256,256]{2,1,0:T(8,128)(2,1)S(1)}, bf16[4,256,256]{2,1,0:T(8,128)(2,1)S(1)}, bf16[4,256,256]{2,1,0:T(8,128)(2,1)S(1)}) custom-call(s32[4]{0:T(128)S(1)} %pad_add_fusion.where_ref, f32[1,4096]{1,0:T(1,128)S(1)} %bubble.1.bubble_ref, bf16[13312,128]{1,0:T(8,128)(2,1)} %bitcast.7.box_ref), custom_call_target="tpu_custom_call" | custom-call | flops 805306368 | bytes 9437184 | tf_op jit(solution)/shard_map/collect/pallas_call | solution.py:339
  77.7 2.6 %collective-permute-start.6 = (bf16[4,256,256]{2,1,0:T(8,128)(2,1)S(1)}, bf16[4,256,256]{2,1,0:T(8,128)(2,1)S(1)}, u32[]{:S(2)}, u32[]{:S(2)}) collective-permute-start(bf16[4,256,256]{2,1,0:T(8,128)(2,1)S(1)} %get-tuple-element.14), channel_id=1, source_target_pairs={{0,3},{1,0},{2,1},{3,2},{4,7},{5,4},{6,5},{7,6},{8,11},{9,8},{10,9... | collective-permute-start | bytes 1572872 | tf_op jit(solution)/shard_map/ppermute | solution.py:72
  80.3 6.7 %collective-permute-done.4.a_ref = bf16[4,256,256]{2,1,0:T(8,128)(2,1)S(1)} collective-permute-done((bf16[4,256,256]{2,1,0:T(8,128)(2,1)S(1)}, bf16[4,256,256]{2,1,0:T(8,128)(2,1)S(1)}, u32[]{:S(2)}, u32[]{:S(2)}) %collective-permute-start.4) | collective-permute-done | bytes 524320 | tf_op jit(solution)/shard_map/ppermute | solution.py:72
  87.1 2.6 %part_ladder.10 = bf16[256,2048]{1,0:T(8,128)(2,1)S(1)} custom-call(bf16[4,256,256]{2,1,0:T(8,128)(2,1)S(1)} %collective-permute-done.4.a_ref, bf16[256,4096]{1,0:T(8,128)(2,1)S(1)} %bitcast.13, bf16[256,4096]{1,0:T(8,128)(2,1)} %collective-permute-done.refs_1_, bf16[128,4096]{1,0:T(8,128)(2,1)S(1)} %collective-permute-done.2.refs_2_, ...), custom_call_target="tpu_custom_call" | custom-call | flops 1073741824 | bytes 6291456 | tf_op jit(solution)/shard_map/part_ladder/pallas_call | solution.py:243
  92.6 2.6 %part_ladder.14 = bf16[256,2048]{1,0:T(8,128)(2,1)S(1)} custom-call(bf16[4,256,256]{2,1,0:T(8,128)(2,1)S(1)} %collective-permute-done.4.a_ref, bf16[256,4096]{1,0:T(8,128)(2,1)S(1)} %bitcast.14, bf16[256,4096]{1,0:T(8,128)(2,1)} %collective-permute-done.refs_1_, bf16[128,4096]{1,0:T(8,128)(2,1)S(1)} %collective-permute-done.2.refs_2_, ...), custom_call_target="tpu_custom_call" | custom-call | flops 1073741824 | bytes 6291456 | tf_op jit(solution)/shard_map/part_ladder/pallas_call | solution.py:243
  95.9 2.6 %part_ladder.12 = bf16[256,2048]{1,0:T(8,128)(2,1)S(1)} custom-call(bf16[4,256,256]{2,1,0:T(8,128)(2,1)S(1)} %collective-permute-done.6.a_ref, bf16[256,4096]{1,0:T(8,128)(2,1)S(1)} %bitcast.15, bf16[256,4096]{1,0:T(8,128)(2,1)} %collective-permute-done.refs_1_, bf16[128,4096]{1,0:T(8,128)(2,1)S(1)} %collective-permute-done.2.refs_2_, ...), custom_call_target="tpu_custom_call" | custom-call | flops 1073741824 | bytes 6291456 | tf_op jit(solution)/shard_map/part_ladder/pallas_call | solution.py:243
  100.2 2.6 %part_ladder.8 = bf16[256,2048]{1,0:T(8,128)(2,1)S(1)} custom-call(bf16[4,256,256]{2,1,0:T(8,128)(2,1)S(1)} %collective-permute-done.5.a_ref, bf16[256,4096]{1,0:T(8,128)(2,1)S(1)} %bitcast.16, bf16[256,4096]{1,0:T(8,128)(2,1)} %collective-permute-done.refs_1_, bf16[128,4096]{1,0:T(8,128)(2,1)S(1)} %collective-permute-done.2.refs_2_, ...), custom_call_target="tpu_custom_call" | custom-call | flops 1073741824 | bytes 6291456 | tf_op jit(solution)/shard_map/part_ladder/pallas_call | solution.py:243
  102.9 1.9 %collective-permute-start.7 = (bf16[256,2048]{1,0:T(8,128)(2,1)S(1)}, bf16[256,2048]{1,0:T(8,128)(2,1)S(1)}, u32[]{:S(2)}, u32[]{:S(2)}) collective-permute-start(bf16[256,2048]{1,0:T(8,128)(2,1)S(1)} %part_ladder.8), channel_id=1, source_target_pairs={{0,3},{1,0},{2,1},{3,2},{4,7},{5,4},{6,5},{7,6},{8,11},{9,8},{10,9... | collective-permute-start | bytes 3145736 | tf_op jit(solution)/shard_map/ppermute | solution.py:72
  105.8 2.7 %part_ladder.11 = bf16[256,2048]{1,0:T(8,128)(2,1)S(1)} custom-call(bf16[4,256,256]{2,1,0:T(8,128)(2,1)S(1)} %collective-permute-done.6.a_ref, bf16[256,4096]{1,0:T(8,128)(2,1)S(1)} %bitcast.17, bf16[256,4096]{1,0:T(8,128)(2,1)} %collective-permute-done.refs_1_, bf16[128,4096]{1,0:T(8,128)(2,1)S(1)} %collective-permute-done.2.refs_2_, ...), custom_call_target="tpu_custom_call" | custom-call | flops 1073741824 | bytes 6291456 | tf_op jit(solution)/shard_map/part_ladder/pallas_call | solution.py:243
  110.1 2.7 %part_ladder.15 = bf16[256,2048]{1,0:T(8,128)(2,1)S(1)} custom-call(bf16[4,256,256]{2,1,0:T(8,128)(2,1)S(1)} %collective-permute-done.5.a_ref, bf16[256,4096]{1,0:T(8,128)(2,1)S(1)} %bitcast.18, bf16[256,4096]{1,0:T(8,128)(2,1)} %collective-permute-done.refs_1_, bf16[128,4096]{1,0:T(8,128)(2,1)S(1)} %collective-permute-done.2.refs_2_, ...), custom_call_target="tpu_custom_call" | custom-call | flops 1073741824 | bytes 6291456 | tf_op jit(solution)/shard_map/part_ladder/pallas_call | solution.py:243
  112.8 1.9 %collective-permute-start.12 = (bf16[256,2048]{1,0:T(8,128)(2,1)S(1)}, bf16[256,2048]{1,0:T(8,128)(2,1)S(1)}, u32[]{:S(2)}, u32[]{:S(2)}) collective-permute-start(bf16[256,2048]{1,0:T(8,128)(2,1)S(1)} %part_ladder.15), channel_id=1, source_target_pairs={{0,3},{1,0},{2,1},{3,2},{4,7},{5,4},{6,5},{7,6},{8,11},{9,8},{10,9... | collective-permute-start | bytes 3145736 | tf_op jit(solution)/shard_map/ppermute | solution.py:72
  114.7 2.4 %collective-permute-done.10.refs_5_ = bf16[256,2048]{1,0:T(8,128)(2,1)S(1)} collective-permute-done((bf16[256,2048]{1,0:T(8,128)(2,1)S(1)}, bf16[256,2048]{1,0:T(8,128)(2,1)S(1)}, u32[]{:S(2)}, u32[]{:S(2)}) %collective-permute-start.10) | collective-permute-done | bytes 1048608 | tf_op jit(solution)/shard_map/ppermute | solution.py:72
  117.0 2.7 %part_ladder.13.refs_1_ = f32[256,2048]{1,0:T(8,128)S(1)} custom-call(bf16[4,256,256]{2,1,0:T(8,128)(2,1)S(1)} %get-tuple-element.11.a_ref, bf16[256,4096]{1,0:T(8,128)(2,1)S(1)} %bitcast.19, bf16[256,4096]{1,0:T(8,128)(2,1)} %collective-permute-done.refs_1_, bf16[128,4096]{1,0:T(8,128)(2,1)S(1)} %collective-permute-done.2.refs_2_, ...), custom_call_target="tpu_custom_call" | custom-call | flops 1073741824 | bytes 6291456 | tf_op jit(solution)/shard_map/part_ladder/pallas_call | solution.py:243
  121.3 2.7 %part_ladder.9.refs_0_ = f32[256,2048]{1,0:T(8,128)S(1)} custom-call(bf16[4,256,256]{2,1,0:T(8,128)(2,1)S(1)} %get-tuple-element.11.a_ref, bf16[256,4096]{1,0:T(8,128)(2,1)S(1)} %bitcast.20, bf16[256,4096]{1,0:T(8,128)(2,1)} %collective-permute-done.refs_1_, bf16[128,4096]{1,0:T(8,128)(2,1)S(1)} %collective-permute-done.2.refs_2_, ...), custom_call_target="tpu_custom_call" | custom-call | flops 1073741824 | bytes 6291456 | tf_op jit(solution)/shard_map/part_ladder/pallas_call | solution.py:243
  124.1 4.2 %collective-permute-done.9.refs_1_ = bf16[256,2048]{1,0:T(8,128)(2,1)S(1)} collective-permute-done((bf16[256,2048]{1,0:T(8,128)(2,1)S(1)}, bf16[256,2048]{1,0:T(8,128)(2,1)S(1)}, u32[]{:S(2)}, u32[]{:S(2)}) %collective-permute-start.9) | collective-permute-done | bytes 1048608 | tf_op jit(solution)/shard_map/ppermute | solution.py:72
  129.9 2.7 %collective-permute-done.12.refs_2_ = bf16[256,2048]{1,0:T(8,128)(2,1)S(1)} collective-permute-done((bf16[256,2048]{1,0:T(8,128)(2,1)S(1)}, bf16[256,2048]{1,0:T(8,128)(2,1)S(1)}, u32[]{:S(2)}, u32[]{:S(2)}) %collective-permute-start.12) | collective-permute-done | bytes 1048608 | tf_op jit(solution)/shard_map/ppermute | solution.py:72
  (26 shorter events, 19.3 us)
Async XLA Ops:
  0.6 36.6 %collective-permute-start.1 = (bf16[256,4096]{1,0:T(8,128)(2,1)}, bf16[256,4096]{1,0:T(8,128)(2,1)S(1)}, u32[]{:S(2)}, u32[]{:S(2)}) collective-permute-start(bf16[256,4096]{1,0:T(8,128)(2,1)} %bitcast.11), channel_id=1, source_target_pairs={{0,4},{1,5},{2,6},{3,7},{4,8},{5,9},{6,10},{7,11},{8,12},{9,13},{1... | collective-permute-start | bytes 6291464 | tf_op jit(solution)/shard_map/ppermute | solution.py:68
  2.3 41.8 %collective-permute-start = (bf16[256,4096]{1,0:T(8,128)(2,1)}, bf16[256,4096]{1,0:T(8,128)(2,1)}, u32[]{:S(2)}, u32[]{:S(2)}) collective-permute-start(bf16[256,4096]{1,0:T(8,128)(2,1)} %bitcast.12), channel_id=1, source_target_pairs={{0,12},{1,13},{2,14},{3,15},{4,0},{5,1},{6,2},{7,3},{8,4},{9,5},{1... | collective-permute-start | bytes 6291464 | tf_op jit(solution)/shard_map/ppermute | solution.py:68
  10.4 60.4 %all-to-all-start = ((bf16[128,104,128]{2,1,0:T(8,128)(2,1)}), bf16[128,104,128]{2,1,0:T(8,128)(2,1)}, u32[]{:S(2)}, u32[]{:S(2)}) async-start(bf16[128,104,128]{2,1,0:T(8,128)(2,1)} %bitcast.23), calls=%async_computation | async-start | bytes 6815744 | tf_op jit(solution)/shard_map/all_to_all | solution.py:320
  22.1 28.2 %copy-start.1 = (s32[64,64]{1,0:T(8,128)S(1)}, s32[64,64]{1,0:T(8,128)}, u32[]{:S(2)}) copy-start(s32[64,64]{1,0:T(8,128)} %table_ref.1) | copy-start | bytes 49156
  22.1 28.2 %copy-start.2 = (f32[64]{0:T(128)S(1)}, f32[64]{0:T(128)}, u32[]{:S(2)}) copy-start(f32[64]{0:T(128)} %param.14) | copy-start | bytes 772
  38.3 42.0 %collective-permute-start.2 = (bf16[128,4096]{1,0:T(8,128)(2,1)}, bf16[128,4096]{1,0:T(8,128)(2,1)S(1)}, u32[]{:S(2)}, u32[]{:S(2)}) collective-permute-start(bf16[128,4096]{1,0:T(8,128)(2,1)} %slice.8), channel_id=1, source_target_pairs={{0,4},{1,5},{2,6},{3,7},{4,8},{5,9},{6,10},{7,11},{8,12},{9,13},{1... | collective-permute-start | bytes 3145736 | tf_op jit(solution)/shard_map/ppermute | solution.py:68
  46.4 33.9 %collective-permute-start.3 = (bf16[128,4096]{1,0:T(8,128)(2,1)}, bf16[128,4096]{1,0:T(8,128)(2,1)}, u32[]{:S(2)}, u32[]{:S(2)}) collective-permute-start(bf16[128,4096]{1,0:T(8,128)(2,1)} %slice.9), channel_id=1, source_target_pairs={{0,12},{1,13},{2,14},{3,15},{4,0},{5,1},{6,2},{7,3},{8,4},{9,5},{1... | collective-permute-start | bytes 3145736 | tf_op jit(solution)/shard_map/ppermute | solution.py:68
  70.8 16.2 %copy-start = (bf16[1,256,4096]{2,1,0:T(8,128)(2,1)S(1)}, bf16[1,256,4096]{2,1,0:T(8,128)(2,1)}, u32[]{:S(2)}) copy-start(bf16[1,256,4096]{2,1,0:T(8,128)(2,1)} %param.9) | copy-start | bytes 6291460
  76.2 10.9 %collective-permute-start.4 = (bf16[4,256,256]{2,1,0:T(8,128)(2,1)S(1)}, bf16[4,256,256]{2,1,0:T(8,128)(2,1)S(1)}, u32[]{:S(2)}, u32[]{:S(2)}) collective-permute-start(bf16[4,256,256]{2,1,0:T(8,128)(2,1)S(1)} %get-tuple-element.12), channel_id=1, source_target_pairs={{0,2},{1,3},{2,0},{3,1},{4,6},{5,7},{6,4},{7,5},{8,10},{9,11},{10,... | collective-permute-start | bytes 1572872 | tf_op jit(solution)/shard_map/ppermute | solution.py:72
  77.1 15.5 %collective-permute-start.5 = (bf16[4,256,256]{2,1,0:T(8,128)(2,1)S(1)}, bf16[4,256,256]{2,1,0:T(8,128)(2,1)S(1)}, u32[]{:S(2)}, u32[]{:S(2)}) collective-permute-start(bf16[4,256,256]{2,1,0:T(8,128)(2,1)S(1)} %get-tuple-element.13), channel_id=1, source_target_pairs={{0,1},{1,2},{2,3},{3,0},{4,5},{5,6},{6,7},{7,4},{8,9},{9,10},{10,1... | collective-permute-start | bytes 1572872 | tf_op jit(solution)/shard_map/ppermute | solution.py:72
  77.7 14.9 %collective-permute-start.6 = (bf16[4,256,256]{2,1,0:T(8,128)(2,1)S(1)}, bf16[4,256,256]{2,1,0:T(8,128)(2,1)S(1)}, u32[]{:S(2)}, u32[]{:S(2)}) collective-permute-start(bf16[4,256,256]{2,1,0:T(8,128)(2,1)S(1)} %get-tuple-element.14), channel_id=1, source_target_pairs={{0,3},{1,0},{2,1},{3,2},{4,7},{5,4},{6,5},{7,6},{8,11},{9,8},{10,9... | collective-permute-start | bytes 1572872 | tf_op jit(solution)/shard_map/ppermute | solution.py:72
  89.7 16.1 %collective-permute-start.8 = (bf16[256,2048]{1,0:T(8,128)(2,1)S(1)}, bf16[256,2048]{1,0:T(8,128)(2,1)S(1)}, u32[]{:S(2)}, u32[]{:S(2)}) collective-permute-start(bf16[256,2048]{1,0:T(8,128)(2,1)S(1)} %part_ladder.10), channel_id=1, source_target_pairs={{0,1},{1,2},{2,3},{3,0},{4,5},{5,6},{6,7},{7,4},{8,9},{9,10},{10,1... | collective-permute-start | bytes 3145736 | tf_op jit(solution)/shard_map/ppermute | solution.py:72
  95.2 14.9 %collective-permute-start.11 = (bf16[256,2048]{1,0:T(8,128)(2,1)S(1)}, bf16[256,2048]{1,0:T(8,128)(2,1)S(1)}, u32[]{:S(2)}, u32[]{:S(2)}) collective-permute-start(bf16[256,2048]{1,0:T(8,128)(2,1)S(1)} %part_ladder.14), channel_id=1, source_target_pairs={{0,3},{1,0},{2,1},{3,2},{4,7},{5,4},{6,5},{7,6},{8,11},{9,8},{10,9... | collective-permute-start | bytes 3145736 | tf_op jit(solution)/shard_map/ppermute | solution.py:72
  98.6 18.5 %collective-permute-start.10 = (bf16[256,2048]{1,0:T(8,128)(2,1)S(1)}, bf16[256,2048]{1,0:T(8,128)(2,1)S(1)}, u32[]{:S(2)}, u32[]{:S(2)}) collective-permute-start(bf16[256,2048]{1,0:T(8,128)(2,1)S(1)} %part_ladder.12), channel_id=1, source_target_pairs={{0,1},{1,2},{2,3},{3,0},{4,5},{5,6},{6,7},{7,4},{8,9},{9,10},{10,1... | collective-permute-start | bytes 3145736 | tf_op jit(solution)/shard_map/ppermute | solution.py:72
  102.9 18.5 %collective-permute-start.7 = (bf16[256,2048]{1,0:T(8,128)(2,1)S(1)}, bf16[256,2048]{1,0:T(8,128)(2,1)S(1)}, u32[]{:S(2)}, u32[]{:S(2)}) collective-permute-start(bf16[256,2048]{1,0:T(8,128)(2,1)S(1)} %part_ladder.8), channel_id=1, source_target_pairs={{0,3},{1,0},{2,1},{3,2},{4,7},{5,4},{6,5},{7,6},{8,11},{9,8},{10,9... | collective-permute-start | bytes 3145736 | tf_op jit(solution)/shard_map/ppermute | solution.py:72
  108.4 19.8 %collective-permute-start.9 = (bf16[256,2048]{1,0:T(8,128)(2,1)S(1)}, bf16[256,2048]{1,0:T(8,128)(2,1)S(1)}, u32[]{:S(2)}, u32[]{:S(2)}) collective-permute-start(bf16[256,2048]{1,0:T(8,128)(2,1)S(1)} %part_ladder.11), channel_id=1, source_target_pairs={{0,1},{1,2},{2,3},{3,0},{4,5},{5,6},{6,7},{7,4},{8,9},{9,10},{10,1... | collective-permute-start | bytes 3145736 | tf_op jit(solution)/shard_map/ppermute | solution.py:72
  112.8 19.8 %collective-permute-start.12 = (bf16[256,2048]{1,0:T(8,128)(2,1)S(1)}, bf16[256,2048]{1,0:T(8,128)(2,1)S(1)}, u32[]{:S(2)}, u32[]{:S(2)}) collective-permute-start(bf16[256,2048]{1,0:T(8,128)(2,1)S(1)} %part_ladder.15), channel_id=1, source_target_pairs={{0,3},{1,0},{2,1},{3,2},{4,7},{5,4},{6,5},{7,6},{8,11},{9,8},{10,9... | collective-permute-start | bytes 3145736 | tf_op jit(solution)/shard_map/ppermute | solution.py:72

commit v6 on v5

--- a/solution.py
+++ b/solution.py
@@ -172,10 +172,8 @@
         copy.wait()
 
 
-def collect_kernel(
-    where_ref, bubble_ref, box_ref, gamma_ref, w0, w1, w2, w3,
-    box, wide, gamma_held, in_sems, out_sems,
-):
+def collect_kernel(turns, where_ref, bubble_ref, box_ref, *refs):
+    gamma_ref, *w_refs, box, wide, gamma_held, in_sems, out_sems = refs[-6 - len(turns) :]
     parts = 8
     rows = DEVICES * CHUNK // parts
     copies = []
@@ -195,7 +193,7 @@
     collector = jnp.concatenate([one_hot(row_of == label[k : k + 1]) for k in range(CAP)], axis=1)
 
     copies = []
-    for d, w_ref in enumerate((w0, w1, w2, w3)):
+    for turn, (d, w_ref) in enumerate(zip(turns, w_refs)):
         for o in range(SIDE):
             slab = ((g + o) % SIDE) * along_g + ((h + d) % SIDE) * along_h
             columns = pl.ds(pl.multiple_of(slab * ROWS, ROWS), ROWS)
@@ -210,7 +208,7 @@
                 collector, jnp.concatenate(came, axis=0), preferred_element_type=jnp.float32
             )
             gamma = HUBBARD + summed
-            at = d * SIDE + o
+            at = turn * SIDE + o
             gamma_held[at] = gamma
             copies.append(
                 pltpu.make_async_copy(
@@ -336,31 +334,39 @@
     )(trans_mom, trans_bose, energies.reshape(1, NQ), pair_table)
 
     block = jax.ShapeDtypeStruct((SIDE, ROWS, ROWS), jnp.bfloat16)
-    gamma, own, w1, w2, w3 = pl.pallas_call(
-        collect_kernel,
-        in_specs=[pl.BlockSpec(memory_space=pltpu.SMEM), whole, hbm],
-        out_specs=[hbm] + [whole] * 4,
-        out_shape=[jax.ShapeDtypeStruct((ROWS, WIDTH), jnp.float32)] + [block] * 4,
-        scratch_shapes=[
-            pltpu.VMEM(slots, jnp.bfloat16),
-            pltpu.VMEM(slots, jnp.float32),
-            pltpu.VMEM((SIDE * SIDE, ROWS, ROWS), jnp.float32),
-            pltpu.SemaphoreType.DMA((8,)),
-            pltpu.SemaphoreType.DMA((SIDE * SIDE,)),
-        ],
-        compiler_params=pltpu.CompilerParams(vmem_limit_bytes=24 * MIB),
-        cost_estimate=pl.CostEstimate(
-            flops=2 * 384 * ROWS * WIDTH, bytes_accessed=9 * MIB, transcendentals=0
-        ),
-        name="collect",
-    )(where, pair_bubble, arrived)
+    def collect(turns, *into):
+        return pl.pallas_call(
+            functools.partial(collect_kernel, turns),
+            in_specs=[pl.BlockSpec(memory_space=pltpu.SMEM), whole, hbm] + [hbm] * len(into),
+            out_specs=[hbm] + [whole] * len(turns),
+            out_shape=[jax.ShapeDtypeStruct((ROWS, WIDTH), jnp.float32)] + [block] * len(turns),
+            input_output_aliases={3: 0} if into else {},
+            scratch_shapes=[
+                pltpu.VMEM(slots, jnp.bfloat16),
+                pltpu.VMEM(slots, jnp.float32),
+                pltpu.VMEM((len(turns) * SIDE, ROWS, ROWS), jnp.float32),
+                pltpu.SemaphoreType.DMA((8,)),
+                pltpu.SemaphoreType.DMA((len(turns) * SIDE,)),
+            ],
+            compiler_params=pltpu.CompilerParams(vmem_limit_bytes=24 * MIB),
+            cost_estimate=pl.CostEstimate(
+                flops=2 * 384 * ROWS * WIDTH * len(turns) // SIDE,
+                bytes_accessed=(4 + len(turns)) * MIB,
+                transcendentals=0,
+            ),
+            name="collect",
+        )(where, pair_bubble, arrived, *into)
+
+    gamma, w2 = collect((2,))
+    gamma, w1, w3, own = collect((1, 3, 0), gamma)
 
     part = functools.partial(part_ladder, full_parts=full_parts)
     bf16, f32 = jnp.bfloat16, jnp.float32
     from_far, from_low, from_high = move_h(w2, 2), move_h(w1, 1), move_h(w3, 3)
     far_left = move_h(part(from_far, side=0, dtype=bf16), 1)
-    from_far, from_low, from_high = lax.optimization_barrier((from_far, from_low, from_high))
-    far_right = move_h(part(from_far, side=1, dtype=bf16), 3)
+    far_right = part(from_far, side=1, dtype=bf16)
+    far_right, from_low, from_high = lax.optimization_barrier((far_right, from_low, from_high))
+    far_right = move_h(far_right, 3)
     high_right = move_h(part(from_high, side=1, dtype=bf16), 1)
     low_left = move_h(part(from_low, side=0, dtype=bf16), 3)
     high_left = move_h(part_ladder(from_high, full_parts, 0, bf16, far_left), 1)

time: 135 us -> 133 us (0.985)
  waiting for transfers between devices: 60.1 us -> 50.4 us
  Pallas kernels: 37 us -> 40.5 us
  starting transfers between devices: 31.4 us -> 34.5 us
    ppermute x9, waiting for transfers between devices: 21.8 us -> 12.1 us  [move_h(): return lax.ppermute(array, AXES, pairs_along((1, 0), step))]
    pallas_call x1 -> x2, Pallas kernels: 5.34 us -> 8.84 us  [collect(): pl.pallas_call(functools.partial(collect_kernel, turns), in_specs=[pl.Blo...]
    ppermute x9, starting transfers between devices: 11.5 us -> 14.6 us  [move_h(): return lax.ppermute(array, AXES, pairs_along((1, 0), step))]
  transfers between devices with their start and end apart: 14 -> 14, of which waited for: 11 -> 8; matrix products, arithmetic and copies ran while one was open for 3% -> 3% of each run, Pallas kernels for 26% -> 30%
where the time goes in v6:
time: 133 us; the launch traced here: 131 us
  waiting for transfers between devices  50.4 us (38%)
  Pallas kernels  40.5 us (30%)
  starting transfers between devices  34.5 us (26%)
  local copies, waits for them, and re-layouts  3.46 us (3%)
  between operations  2.14 us (2%)
    pallas_call x8, Pallas kernels, part_ladder(): pl.pallas_call(functools.partial(ladder_kernel, len(full_parts)), grid=(s...  21.3 us
    all_to_all x1, waiting for transfers between devices, per_device(): lax.all_to_all(payload.reshape(DEVICES, CHUNK, LANES), AXES, split_axis=0...  19.7 us
    ppermute x4, waiting for transfers between devices, move_g(): return lax.ppermute(array, AXES, pairs_along((0, 1), step))  18.6 us
    ppermute x9, starting transfers between devices, move_h(): return lax.ppermute(array, AXES, pairs_along((1, 0), step))  14.6 us
    ppermute x9, waiting for transfers between devices, move_h(): return lax.ppermute(array, AXES, pairs_along((1, 0), step))  12.1 us
    all_to_all x1, starting transfers between devices, per_device(): lax.all_to_all(payload.reshape(DEVICES, CHUNK, LANES), AXES, split_axis=0...  10.4 us
    ppermute x4, starting transfers between devices, move_g(): return lax.ppermute(array, AXES, pairs_along((0, 1), step))  9.48 us
    pallas_call x2, Pallas kernels, collect(): pl.pallas_call(functools.partial(collect_kernel, turns), in_specs=[pl.Blo...  8.84 us
  transfers between devices with their start and end apart: 14, of which 8 were waited for; matrix products, arithmetic and copies ran while one was open for 3% of the time, Pallas kernels for 30%

profile of v6, /device:TPU:0, one launch (start us, length us, event | category | flops | bytes accessed | tf_op | source)
XLA Modules:
  0.0 131.2 jit_solution(17368433235247585534)
XLA Ops:
  3.9 6.5 %place.1 = bf16[13312,128]{1,0:T(8,128)(2,1)} custom-call(s32[1,256]{1,0:T(1,128)} %target_ref.1, s32[1,256]{1,0:T(1,128)} %shift_ref.1, bf16[256,4096]{1,0:T(8,128)(2,1)} %bitcast.25), custom_call_target="tpu_custom_call" | custom-call | flops 805306368 | bytes 5242880 | tf_op jit(solution)/shard_map/place/pallas_call | solution.py:300
  10.4 10.4 %all-to-all-start = ((bf16[128,104,128]{2,1,0:T(8,128)(2,1)}), bf16[128,104,128]{2,1,0:T(8,128)(2,1)}, u32[]{:S(2)}, u32[]{:S(2)}) async-start(bf16[128,104,128]{2,1,0:T(8,128)(2,1)} %bitcast.23), calls=%async_computation | async-start | bytes 6815744 | tf_op jit(solution)/shard_map/all_to_all | solution.py:318
  22.2 15.1 %collective-permute-done.1.refs_4_ = bf16[256,4096]{1,0:T(8,128)(2,1)S(1)} collective-permute-done((bf16[256,4096]{1,0:T(8,128)(2,1)}, bf16[256,4096]{1,0:T(8,128)(2,1)S(1)}, u32[]{:S(2)}, u32[]{:S(2)}) %collective-permute-start.1) | collective-permute-done | bytes 2097184 | tf_op jit(solution)/shard_map/ppermute | solution.py:68
  38.3 2.3 %collective-permute-start.2 = (bf16[128,4096]{1,0:T(8,128)(2,1)}, bf16[128,4096]{1,0:T(8,128)(2,1)S(1)}, u32[]{:S(2)}, u32[]{:S(2)}) collective-permute-start(bf16[128,4096]{1,0:T(8,128)(2,1)} %slice.8), channel_id=1, source_target_pairs={{0,4},{1,5},{2,6},{3,7},{4,8},{5,9},{6,10},{7,11},{8,12},{9,13},{1... | collective-permute-start | bytes 3145736 | tf_op jit(solution)/shard_map/ppermute | solution.py:68
  40.6 3.5 %collective-permute-done.refs_1_ = bf16[256,4096]{1,0:T(8,128)(2,1)} collective-permute-done((bf16[256,4096]{1,0:T(8,128)(2,1)}, bf16[256,4096]{1,0:T(8,128)(2,1)}, u32[]{:S(2)}, u32[]{:S(2)}) %collective-permute-start) | collective-permute-done | bytes 2097184 | tf_op jit(solution)/shard_map/ppermute | solution.py:68
  44.0 2.4 %slice.9 = bf16[128,4096]{1,0:T(8,128)(2,1)} slice(bf16[256,4096]{1,0:T(8,128)(2,1)} %collective-permute-done.refs_1_), slice={[128:256], [0:4096]} | slice | bytes 2097152 | tf_op jit(solution)/shard_map/slice | solution.py:294
  46.4 3.9 %collective-permute-start.3 = (bf16[128,4096]{1,0:T(8,128)(2,1)}, bf16[128,4096]{1,0:T(8,128)(2,1)}, u32[]{:S(2)}, u32[]{:S(2)}) collective-permute-start(bf16[128,4096]{1,0:T(8,128)(2,1)} %slice.9), channel_id=1, source_target_pairs={{0,12},{1,13},{2,14},{3,15},{4,0},{5,1},{6,2},{7,3},{8,4},{9,5},{1... | collective-permute-start | bytes 3145736 | tf_op jit(solution)/shard_map/ppermute | solution.py:68
  51.1 19.7 %all-to-all-done = bf16[128,104,128]{2,1,0:T(8,128)(2,1)} async-done(((bf16[128,104,128]{2,1,0:T(8,128)(2,1)}), bf16[128,104,128]{2,1,0:T(8,128)(2,1)}, u32[]{:S(2)}, u32[]{:S(2)}) %all-to-all-start) | async-done | bytes 3407904 | tf_op jit(solution)/shard_map/all_to_all | solution.py:318
  70.8 3.9 %collect.2 = (f32[256,4096]{1,0:T(8,128)}, bf16[4,256,256]{2,1,0:T(8,128)(2,1)S(1)}) custom-call(s32[4]{0:T(128)S(1)} %pad_add_fusion.where_ref, f32[1,4096]{1,0:T(1,128)S(1)} %bubble.1.bubble_ref, bf16[13312,128]{1,0:T(8,128)(2,1)} %bitcast.7.box_ref), custom_call_target="tpu_custom_call" | custom-call | flops 201326592 | bytes 5242880 | tf_op jit(solution)/shard_map/collect/pallas_call | solution.py:338
  75.7 4.9 %collect.3 = (f32[256,4096]{1,0:T(8,128)}, bf16[4,256,256]{2,1,0:T(8,128)(2,1)S(1)}, bf16[4,256,256]{2,1,0:T(8,128)(2,1)S(1)}, bf16[4,256,256]{2,1,0:T(8,128)(2,1)S(1)}) custom-call(s32[4]{0:T(128)S(1)} %pad_add_fusion.where_ref, f32[1,4096]{1,0:T(1,128)S(1)} %bubble.1.bubble_ref, ...), custom_call_target="tpu_custom_call", output_to_operand_aliasing={{0}: (3, {})} | custom-call | flops 603979776 | bytes 7340032 | tf_op jit(solution)/shard_map/collect/pallas_call | solution.py:338
  81.3 2.6 %collective-permute-start.6 = (bf16[4,256,256]{2,1,0:T(8,128)(2,1)S(1)}, bf16[4,256,256]{2,1,0:T(8,128)(2,1)S(1)}, u32[]{:S(2)}, u32[]{:S(2)}) collective-permute-start(bf16[4,256,256]{2,1,0:T(8,128)(2,1)S(1)} %get-tuple-element.16), channel_id=1, source_target_pairs={{0,3},{1,0},{2,1},{3,2},{4,7},{5,4},{6,5},{7,6},{8,11},{9,8},{10,9... | collective-permute-start | bytes 1572872 | tf_op jit(solution)/shard_map/ppermute | solution.py:72
  85.6 2.6 %part_ladder.11 = bf16[256,2048]{1,0:T(8,128)(2,1)S(1)} custom-call(bf16[4,256,256]{2,1,0:T(8,128)(2,1)S(1)} %collective-permute-done.4.a_ref, bf16[256,4096]{1,0:T(8,128)(2,1)S(1)} %bitcast.13, bf16[256,4096]{1,0:T(8,128)(2,1)} %collective-permute-done.refs_1_, bf16[128,4096]{1,0:T(8,128)(2,1)S(1)} %collective-permute-done.2.refs_2_, ...), custom_call_target="tpu_custom_call" | custom-call | flops 1073741824 | bytes 6291456 | tf_op jit(solution)/shard_map/part_ladder/pallas_call | solution.py:241
  89.3 2.6 %part_ladder.8 = bf16[256,2048]{1,0:T(8,128)(2,1)S(1)} custom-call(bf16[4,256,256]{2,1,0:T(8,128)(2,1)S(1)} %collective-permute-done.4.a_ref, bf16[256,4096]{1,0:T(8,128)(2,1)S(1)} %bitcast.14, bf16[256,4096]{1,0:T(8,128)(2,1)} %collective-permute-done.refs_1_, bf16[128,4096]{1,0:T(8,128)(2,1)S(1)} %collective-permute-done.2.refs_2_, ...), custom_call_target="tpu_custom_call" | custom-call | flops 1073741824 | bytes 6291456 | tf_op jit(solution)/shard_map/part_ladder/pallas_call | solution.py:241
  92.0 2.4 %collective-permute-start.11 = (bf16[256,2048]{1,0:T(8,128)(2,1)S(1)}, bf16[256,2048]{1,0:T(8,128)(2,1)S(1)}, u32[]{:S(2)}, u32[]{:S(2)}) collective-permute-start(bf16[256,2048]{1,0:T(8,128)(2,1)S(1)} %part_ladder.8), channel_id=1, source_target_pairs={{0,3},{1,0},{2,1},{3,2},{4,7},{5,4},{6,5},{7,6},{8,11},{9,8},{10,9... | collective-permute-start | bytes 3145736 | tf_op jit(solution)/shard_map/ppermute | solution.py:72
  94.4 2.6 %part_ladder.13 = bf16[256,2048]{1,0:T(8,128)(2,1)S(1)} custom-call(bf16[4,256,256]{2,1,0:T(8,128)(2,1)S(1)} %collective-permute-done.6.a_ref, bf16[256,4096]{1,0:T(8,128)(2,1)S(1)} %bitcast.15, bf16[256,4096]{1,0:T(8,128)(2,1)} %collective-permute-done.refs_1_, bf16[128,4096]{1,0:T(8,128)(2,1)S(1)} %collective-permute-done.2.refs_2_, ...), custom_call_target="tpu_custom_call" | custom-call | flops 1073741824 | bytes 6291456 | tf_op jit(solution)/shard_map/part_ladder/pallas_call | solution.py:241
  97.2 2.7 %part_ladder.9 = bf16[256,2048]{1,0:T(8,128)(2,1)S(1)} custom-call(bf16[4,256,256]{2,1,0:T(8,128)(2,1)S(1)} %collective-permute-done.5.a_ref, bf16[256,4096]{1,0:T(8,128)(2,1)S(1)} %bitcast.16, bf16[256,4096]{1,0:T(8,128)(2,1)} %collective-permute-done.refs_1_, bf16[128,4096]{1,0:T(8,128)(2,1)S(1)} %collective-permute-done.2.refs_2_, ...), custom_call_target="tpu_custom_call" | custom-call | flops 1073741824 | bytes 6291456 | tf_op jit(solution)/shard_map/part_ladder/pallas_call | solution.py:241
  99.8 3.3 %collective-permute-start.7 = (bf16[256,2048]{1,0:T(8,128)(2,1)S(1)}, bf16[256,2048]{1,0:T(8,128)(2,1)S(1)}, u32[]{:S(2)}, u32[]{:S(2)}) collective-permute-start(bf16[256,2048]{1,0:T(8,128)(2,1)S(1)} %part_ladder.9), channel_id=1, source_target_pairs={{0,3},{1,0},{2,1},{3,2},{4,7},{5,4},{6,5},{7,6},{8,11},{9,8},{10,9... | collective-permute-start | bytes 3145736 | tf_op jit(solution)/shard_map/ppermute | solution.py:72
  104.3 2.7 %part_ladder.12 = bf16[256,2048]{1,0:T(8,128)(2,1)S(1)} custom-call(bf16[4,256,256]{2,1,0:T(8,128)(2,1)S(1)} %collective-permute-done.6.a_ref, bf16[256,4096]{1,0:T(8,128)(2,1)S(1)} %bitcast.17, bf16[256,4096]{1,0:T(8,128)(2,1)} %collective-permute-done.refs_1_, bf16[128,4096]{1,0:T(8,128)(2,1)S(1)} %collective-permute-done.2.refs_2_, ...), custom_call_target="tpu_custom_call" | custom-call | flops 1073741824 | bytes 6291456 | tf_op jit(solution)/shard_map/part_ladder/pallas_call | solution.py:241
  107.1 2.7 %part_ladder.15 = bf16[256,2048]{1,0:T(8,128)(2,1)S(1)} custom-call(bf16[4,256,256]{2,1,0:T(8,128)(2,1)S(1)} %collective-permute-done.5.a_ref, bf16[256,4096]{1,0:T(8,128)(2,1)S(1)} %bitcast.18, bf16[256,4096]{1,0:T(8,128)(2,1)} %collective-permute-done.refs_1_, bf16[128,4096]{1,0:T(8,128)(2,1)S(1)} %collective-permute-done.2.refs_2_, ...), custom_call_target="tpu_custom_call" | custom-call | flops 1073741824 | bytes 6291456 | tf_op jit(solution)/shard_map/part_ladder/pallas_call | solution.py:241
  109.7 3.4 %collective-permute-start.12 = (bf16[256,2048]{1,0:T(8,128)(2,1)S(1)}, bf16[256,2048]{1,0:T(8,128)(2,1)S(1)}, u32[]{:S(2)}, u32[]{:S(2)}) collective-permute-start(bf16[256,2048]{1,0:T(8,128)(2,1)S(1)} %part_ladder.15), channel_id=1, source_target_pairs={{0,3},{1,0},{2,1},{3,2},{4,7},{5,4},{6,5},{7,6},{8,11},{9,8},{10,9... | collective-permute-start | bytes 3145736 | tf_op jit(solution)/shard_map/ppermute | solution.py:72
  113.2 2.3 %collective-permute-done.10.refs_5_ = bf16[256,2048]{1,0:T(8,128)(2,1)S(1)} collective-permute-done((bf16[256,2048]{1,0:T(8,128)(2,1)S(1)}, bf16[256,2048]{1,0:T(8,128)(2,1)S(1)}, u32[]{:S(2)}, u32[]{:S(2)}) %collective-permute-start.10) | collective-permute-done | bytes 1048608 | tf_op jit(solution)/shard_map/ppermute | solution.py:72
  115.5 2.7 %part_ladder.14.refs_1_ = f32[256,2048]{1,0:T(8,128)S(1)} custom-call(bf16[4,256,256]{2,1,0:T(8,128)(2,1)S(1)} %get-tuple-element.13.a_ref, bf16[256,4096]{1,0:T(8,128)(2,1)S(1)} %bitcast.19, bf16[256,4096]{1,0:T(8,128)(2,1)} %collective-permute-done.refs_1_, bf16[128,4096]{1,0:T(8,128)(2,1)S(1)} %collective-permute-done.2.refs_2_, ...), custom_call_target="tpu_custom_call" | custom-call | flops 1073741824 | bytes 6291456 | tf_op jit(solution)/shard_map/part_ladder/pallas_call | solution.py:241
  118.3 2.7 %part_ladder.10.refs_0_ = f32[256,2048]{1,0:T(8,128)S(1)} custom-call(bf16[4,256,256]{2,1,0:T(8,128)(2,1)S(1)} %get-tuple-element.13.a_ref, bf16[256,4096]{1,0:T(8,128)(2,1)S(1)} %bitcast.20, bf16[256,4096]{1,0:T(8,128)(2,1)} %collective-permute-done.refs_1_, bf16[128,4096]{1,0:T(8,128)(2,1)S(1)} %collective-permute-done.2.refs_2_, ...), custom_call_target="tpu_custom_call" | custom-call | flops 1073741824 | bytes 6291456 | tf_op jit(solution)/shard_map/part_ladder/pallas_call | solution.py:241
  121.0 5.7 %collective-permute-done.9.refs_1_ = bf16[256,2048]{1,0:T(8,128)(2,1)S(1)} collective-permute-done((bf16[256,2048]{1,0:T(8,128)(2,1)S(1)}, bf16[256,2048]{1,0:T(8,128)(2,1)S(1)}, u32[]{:S(2)}, u32[]{:S(2)}) %collective-permute-start.9) | collective-permute-done | bytes 1048608 | tf_op jit(solution)/shard_map/ppermute | solution.py:72
  (27 shorter events, 15.3 us)
Async XLA Ops:
  0.6 36.6 %collective-permute-start.1 = (bf16[256,4096]{1,0:T(8,128)(2,1)}, bf16[256,4096]{1,0:T(8,128)(2,1)S(1)}, u32[]{:S(2)}, u32[]{:S(2)}) collective-permute-start(bf16[256,4096]{1,0:T(8,128)(2,1)} %bitcast.11), channel_id=1, source_target_pairs={{0,4},{1,5},{2,6},{3,7},{4,8},{5,9},{6,10},{7,11},{8,12},{9,13},{1... | collective-permute-start | bytes 6291464 | tf_op jit(solution)/shard_map/ppermute | solution.py:68
  2.3 41.8 %collective-permute-start = (bf16[256,4096]{1,0:T(8,128)(2,1)}, bf16[256,4096]{1,0:T(8,128)(2,1)}, u32[]{:S(2)}, u32[]{:S(2)}) collective-permute-start(bf16[256,4096]{1,0:T(8,128)(2,1)} %bitcast.12), channel_id=1, source_target_pairs={{0,12},{1,13},{2,14},{3,15},{4,0},{5,1},{6,2},{7,3},{8,4},{9,5},{1... | collective-permute-start | bytes 6291464 | tf_op jit(solution)/shard_map/ppermute | solution.py:68
  10.4 60.4 %all-to-all-start = ((bf16[128,104,128]{2,1,0:T(8,128)(2,1)}), bf16[128,104,128]{2,1,0:T(8,128)(2,1)}, u32[]{:S(2)}, u32[]{:S(2)}) async-start(bf16[128,104,128]{2,1,0:T(8,128)(2,1)} %bitcast.23), calls=%async_computation | async-start | bytes 6815744 | tf_op jit(solution)/shard_map/all_to_all | solution.py:318
  20.8 29.5 %copy-start.1 = (s32[64,64]{1,0:T(8,128)S(1)}, s32[64,64]{1,0:T(8,128)}, u32[]{:S(2)}) copy-start(s32[64,64]{1,0:T(8,128)} %table_ref.1) | copy-start | bytes 49156
  20.8 29.5 %copy-start.2 = (f32[64]{0:T(128)S(1)}, f32[64]{0:T(128)}, u32[]{:S(2)}) copy-start(f32[64]{0:T(128)} %param.14) | copy-start | bytes 772
  38.3 45.6 %collective-permute-start.2 = (bf16[128,4096]{1,0:T(8,128)(2,1)}, bf16[128,4096]{1,0:T(8,128)(2,1)S(1)}, u32[]{:S(2)}, u32[]{:S(2)}) collective-permute-start(bf16[128,4096]{1,0:T(8,128)(2,1)} %slice.8), channel_id=1, source_target_pairs={{0,4},{1,5},{2,6},{3,7},{4,8},{5,9},{6,10},{7,11},{8,12},{9,13},{1... | collective-permute-start | bytes 3145736 | tf_op jit(solution)/shard_map/ppermute | solution.py:68
  46.4 37.5 %collective-permute-start.3 = (bf16[128,4096]{1,0:T(8,128)(2,1)}, bf16[128,4096]{1,0:T(8,128)(2,1)}, u32[]{:S(2)}, u32[]{:S(2)}) collective-permute-start(bf16[128,4096]{1,0:T(8,128)(2,1)} %slice.9), channel_id=1, source_target_pairs={{0,12},{1,13},{2,14},{3,15},{4,0},{5,1},{6,2},{7,3},{8,4},{9,5},{1... | collective-permute-start | bytes 3145736 | tf_op jit(solution)/shard_map/ppermute | solution.py:68
  74.8 10.8 %collective-permute-start.4 = (bf16[4,256,256]{2,1,0:T(8,128)(2,1)S(1)}, bf16[4,256,256]{2,1,0:T(8,128)(2,1)S(1)}, u32[]{:S(2)}, u32[]{:S(2)}) collective-permute-start(bf16[4,256,256]{2,1,0:T(8,128)(2,1)S(1)} %get-tuple-element.14), channel_id=1, source_target_pairs={{0,2},{1,3},{2,0},{3,1},{4,6},{5,7},{6,4},{7,5},{8,10},{9,11},{10,... | collective-permute-start | bytes 1572872 | tf_op jit(solution)/shard_map/ppermute | solution.py:72
  75.7 9.9 %copy-start = (bf16[1,256,4096]{2,1,0:T(8,128)(2,1)S(1)}, bf16[1,256,4096]{2,1,0:T(8,128)(2,1)}, u32[]{:S(2)}) copy-start(bf16[1,256,4096]{2,1,0:T(8,128)(2,1)} %param.9) | copy-start | bytes 6291460
  80.6 11.4 %collective-permute-start.5 = (bf16[4,256,256]{2,1,0:T(8,128)(2,1)S(1)}, bf16[4,256,256]{2,1,0:T(8,128)(2,1)S(1)}, u32[]{:S(2)}, u32[]{:S(2)}) collective-permute-start(bf16[4,256,256]{2,1,0:T(8,128)(2,1)S(1)} %get-tuple-element.15), channel_id=1, source_target_pairs={{0,1},{1,2},{2,3},{3,0},{4,5},{5,6},{6,7},{7,4},{8,9},{9,10},{10,1... | collective-permute-start | bytes 1572872 | tf_op jit(solution)/shard_map/ppermute | solution.py:72
  81.3 10.7 %collective-permute-start.6 = (bf16[4,256,256]{2,1,0:T(8,128)(2,1)S(1)}, bf16[4,256,256]{2,1,0:T(8,128)(2,1)S(1)}, u32[]{:S(2)}, u32[]{:S(2)}) collective-permute-start(bf16[4,256,256]{2,1,0:T(8,128)(2,1)S(1)} %get-tuple-element.16), channel_id=1, source_target_pairs={{0,3},{1,0},{2,1},{3,2},{4,7},{5,4},{6,5},{7,6},{8,11},{9,8},{10,9... | collective-permute-start | bytes 1572872 | tf_op jit(solution)/shard_map/ppermute | solution.py:72
  88.2 16.1 %collective-permute-start.8 = (bf16[256,2048]{1,0:T(8,128)(2,1)S(1)}, bf16[256,2048]{1,0:T(8,128)(2,1)S(1)}, u32[]{:S(2)}, u32[]{:S(2)}) collective-permute-start(bf16[256,2048]{1,0:T(8,128)(2,1)S(1)} %part_ladder.11), channel_id=1, source_target_pairs={{0,1},{1,2},{2,3},{3,0},{4,5},{5,6},{6,7},{7,4},{8,9},{9,10},{10,1... | collective-permute-start | bytes 3145736 | tf_op jit(solution)/shard_map/ppermute | solution.py:72
  92.0 15.0 %collective-permute-start.11 = (bf16[256,2048]{1,0:T(8,128)(2,1)S(1)}, bf16[256,2048]{1,0:T(8,128)(2,1)S(1)}, u32[]{:S(2)}, u32[]{:S(2)}) collective-permute-start(bf16[256,2048]{1,0:T(8,128)(2,1)S(1)} %part_ladder.8), channel_id=1, source_target_pairs={{0,3},{1,0},{2,1},{3,2},{4,7},{5,4},{6,5},{7,6},{8,11},{9,8},{10,9... | collective-permute-start | bytes 3145736 | tf_op jit(solution)/shard_map/ppermute | solution.py:72
  97.1 18.4 %collective-permute-start.10 = (bf16[256,2048]{1,0:T(8,128)(2,1)S(1)}, bf16[256,2048]{1,0:T(8,128)(2,1)S(1)}, u32[]{:S(2)}, u32[]{:S(2)}) collective-permute-start(bf16[256,2048]{1,0:T(8,128)(2,1)S(1)} %part_ladder.13), channel_id=1, source_target_pairs={{0,1},{1,2},{2,3},{3,0},{4,5},{5,6},{6,7},{7,4},{8,9},{9,10},{10,1... | collective-permute-start | bytes 3145736 | tf_op jit(solution)/shard_map/ppermute | solution.py:72
  99.8 18.5 %collective-permute-start.7 = (bf16[256,2048]{1,0:T(8,128)(2,1)S(1)}, bf16[256,2048]{1,0:T(8,128)(2,1)S(1)}, u32[]{:S(2)}, u32[]{:S(2)}) collective-permute-start(bf16[256,2048]{1,0:T(8,128)(2,1)S(1)} %part_ladder.9), channel_id=1, source_target_pairs={{0,3},{1,0},{2,1},{3,2},{4,7},{5,4},{6,5},{7,6},{8,11},{9,8},{10,9... | collective-permute-start | bytes 3145736 | tf_op jit(solution)/shard_map/ppermute | solution.py:72
  106.9 19.8 %collective-permute-start.9 = (bf16[256,2048]{1,0:T(8,128)(2,1)S(1)}, bf16[256,2048]{1,0:T(8,128)(2,1)S(1)}, u32[]{:S(2)}, u32[]{:S(2)}) collective-permute-start(bf16[256,2048]{1,0:T(8,128)(2,1)S(1)} %part_ladder.12), channel_id=1, source_target_pairs={{0,1},{1,2},{2,3},{3,0},{4,5},{5,6},{6,7},{7,4},{8,9},{9,10},{10,1... | collective-permute-start | bytes 3145736 | tf_op jit(solution)/shard_map/ppermute | solution.py:72
  109.7 19.8 %collective-permute-start.12 = (bf16[256,2048]{1,0:T(8,128)(2,1)S(1)}, bf16[256,2048]{1,0:T(8,128)(2,1)S(1)}, u32[]{:S(2)}, u32[]{:S(2)}) collective-permute-start(bf16[256,2048]{1,0:T(8,128)(2,1)S(1)} %part_ladder.15), channel_id=1, source_target_pairs={{0,3},{1,0},{2,1},{3,2},{4,7},{5,4},{6,5},{7,6},{8,11},{9,8},{10,9... | collective-permute-start | bytes 3145736 | tf_op jit(solution)/shard_map/ppermute | solution.py:72

commit v7 on v6

--- a/solution.py
+++ b/solution.py
@@ -297,6 +297,7 @@
     whole = pl.BlockSpec(memory_space=pltpu.VMEM)
     hbm = pl.BlockSpec(memory_space=pltpu.HBM)
     slots = (DEVICES * CHUNK, LANES)
+    spread = ((DEVICES + 1) * CHUNK, LANES)
     payload = pl.pallas_call(
         place_kernel,
         in_specs=[whole, whole, hbm],
@@ -304,7 +305,7 @@
         out_shape=jax.ShapeDtypeStruct(slots, jnp.bfloat16),
         scratch_shapes=[
             pltpu.VMEM((ROWS, WIDTH), jnp.bfloat16),
-            pltpu.VMEM(slots, jnp.float32),
+            pltpu.VMEM(spread, jnp.float32),
             pltpu.VMEM(slots, jnp.bfloat16),
             pltpu.SemaphoreType.DMA((4,)),
             pltpu.SemaphoreType.DMA((4,)),
@@ -343,7 +344,7 @@
             input_output_aliases={3: 0} if into else {},
             scratch_shapes=[
                 pltpu.VMEM(slots, jnp.bfloat16),
-                pltpu.VMEM(slots, jnp.float32),
+                pltpu.VMEM(spread, jnp.float32),
                 pltpu.VMEM((len(turns) * SIDE, ROWS, ROWS), jnp.float32),
                 pltpu.SemaphoreType.DMA((8,)),
                 pltpu.SemaphoreType.DMA((len(turns) * SIDE,)),

time: 133 us -> 133 us (level)
  no operation moved by 1% of the time
where the time goes in v7:
time: 133 us; the launch traced here: 131 us
  waiting for transfers between devices  50.4 us (38%)
  Pallas kernels  40.6 us (31%)
  starting transfers between devices  34.5 us (26%)
  local copies, waits for them, and re-layouts  3.46 us (3%)
  between operations  2.14 us (2%)
    pallas_call x8, Pallas kernels, part_ladder(): pl.pallas_call(functools.partial(ladder_kernel, len(full_parts)), grid=(s...  21.3 us
    all_to_all x1, waiting for transfers between devices, per_device(): lax.all_to_all(payload.reshape(DEVICES, CHUNK, LANES), AXES, split_axis=0...  19.7 us
    ppermute x4, waiting for transfers between devices, move_g(): return lax.ppermute(array, AXES, pairs_along((0, 1), step))  18.6 us
    ppermute x9, starting transfers between devices, move_h(): return lax.ppermute(array, AXES, pairs_along((1, 0), step))  14.6 us
    ppermute x9, waiting for transfers between devices, move_h(): return lax.ppermute(array, AXES, pairs_along((1, 0), step))  12.1 us
    all_to_all x1, starting transfers between devices, per_device(): lax.all_to_all(payload.reshape(DEVICES, CHUNK, LANES), AXES, split_axis=0...  10.4 us
    ppermute x4, starting transfers between devices, move_g(): return lax.ppermute(array, AXES, pairs_along((0, 1), step))  9.47 us
    pallas_call x2, Pallas kernels, collect(): pl.pallas_call(functools.partial(collect_kernel, turns), in_specs=[pl.Blo...  8.85 us
  transfers between devices with their start and end apart: 14, of which 8 were waited for; matrix products, arithmetic and copies ran while one was open for 3% of the time, Pallas kernels for 30%

profile of v7, /device:TPU:0, one launch (start us, length us, event | category | flops | bytes accessed | tf_op | source)
XLA Modules:
  0.0 131.2 jit_solution(16041172300637028434)
XLA Ops:
  3.9 6.5 %place.1 = bf16[13312,128]{1,0:T(8,128)(2,1)} custom-call(s32[1,256]{1,0:T(1,128)} %target_ref.1, s32[1,256]{1,0:T(1,128)} %shift_ref.1, bf16[256,4096]{1,0:T(8,128)(2,1)} %bitcast.25), custom_call_target="tpu_custom_call" | custom-call | flops 805306368 | bytes 5242880 | tf_op jit(solution)/shard_map/place/pallas_call | solution.py:301
  10.4 10.4 %all-to-all-start = ((bf16[128,104,128]{2,1,0:T(8,128)(2,1)}), bf16[128,104,128]{2,1,0:T(8,128)(2,1)}, u32[]{:S(2)}, u32[]{:S(2)}) async-start(bf16[128,104,128]{2,1,0:T(8,128)(2,1)} %bitcast.23), calls=%async_computation | async-start | bytes 6815744 | tf_op jit(solution)/shard_map/all_to_all | solution.py:319
  22.2 15.1 %collective-permute-done.1.refs_4_ = bf16[256,4096]{1,0:T(8,128)(2,1)S(1)} collective-permute-done((bf16[256,4096]{1,0:T(8,128)(2,1)}, bf16[256,4096]{1,0:T(8,128)(2,1)S(1)}, u32[]{:S(2)}, u32[]{:S(2)}) %collective-permute-start.1) | collective-permute-done | bytes 2097184 | tf_op jit(solution)/shard_map/ppermute | solution.py:68
  38.3 2.3 %collective-permute-start.2 = (bf16[128,4096]{1,0:T(8,128)(2,1)}, bf16[128,4096]{1,0:T(8,128)(2,1)S(1)}, u32[]{:S(2)}, u32[]{:S(2)}) collective-permute-start(bf16[128,4096]{1,0:T(8,128)(2,1)} %slice.8), channel_id=1, source_target_pairs={{0,4},{1,5},{2,6},{3,7},{4,8},{5,9},{6,10},{7,11},{8,12},{9,13},{1... | collective-permute-start | bytes 3145736 | tf_op jit(solution)/shard_map/ppermute | solution.py:68
  40.6 3.5 %collective-permute-done.refs_1_ = bf16[256,4096]{1,0:T(8,128)(2,1)} collective-permute-done((bf16[256,4096]{1,0:T(8,128)(2,1)}, bf16[256,4096]{1,0:T(8,128)(2,1)}, u32[]{:S(2)}, u32[]{:S(2)}) %collective-permute-start) | collective-permute-done | bytes 2097184 | tf_op jit(solution)/shard_map/ppermute | solution.py:68
  44.0 2.4 %slice.9 = bf16[128,4096]{1,0:T(8,128)(2,1)} slice(bf16[256,4096]{1,0:T(8,128)(2,1)} %collective-permute-done.refs_1_), slice={[128:256], [0:4096]} | slice | bytes 2097152 | tf_op jit(solution)/shard_map/slice | solution.py:294
  46.4 3.9 %collective-permute-start.3 = (bf16[128,4096]{1,0:T(8,128)(2,1)}, bf16[128,4096]{1,0:T(8,128)(2,1)}, u32[]{:S(2)}, u32[]{:S(2)}) collective-permute-start(bf16[128,4096]{1,0:T(8,128)(2,1)} %slice.9), channel_id=1, source_target_pairs={{0,12},{1,13},{2,14},{3,15},{4,0},{5,1},{6,2},{7,3},{8,4},{9,5},{1... | collective-permute-start | bytes 3145736 | tf_op jit(solution)/shard_map/ppermute | solution.py:68
  51.1 19.7 %all-to-all-done = bf16[128,104,128]{2,1,0:T(8,128)(2,1)} async-done(((bf16[128,104,128]{2,1,0:T(8,128)(2,1)}), bf16[128,104,128]{2,1,0:T(8,128)(2,1)}, u32[]{:S(2)}, u32[]{:S(2)}) %all-to-all-start) | async-done | bytes 3407904 | tf_op jit(solution)/shard_map/all_to_all | solution.py:319
  70.8 3.9 %collect.2 = (f32[256,4096]{1,0:T(8,128)}, bf16[4,256,256]{2,1,0:T(8,128)(2,1)S(1)}) custom-call(s32[4]{0:T(128)S(1)} %pad_add_fusion.where_ref, f32[1,4096]{1,0:T(1,128)S(1)} %bubble.1.bubble_ref, bf16[13312,128]{1,0:T(8,128)(2,1)} %bitcast.7.box_ref), custom_call_target="tpu_custom_call" | custom-call | flops 201326592 | bytes 5242880 | tf_op jit(solution)/shard_map/collect/pallas_call | solution.py:339
  75.7 4.9 %collect.3 = (f32[256,4096]{1,0:T(8,128)}, bf16[4,256,256]{2,1,0:T(8,128)(2,1)S(1)}, bf16[4,256,256]{2,1,0:T(8,128)(2,1)S(1)}, bf16[4,256,256]{2,1,0:T(8,128)(2,1)S(1)}) custom-call(s32[4]{0:T(128)S(1)} %pad_add_fusion.where_ref, f32[1,4096]{1,0:T(1,128)S(1)} %bubble.1.bubble_ref, ...), custom_call_target="tpu_custom_call", output_to_operand_aliasing={{0}: (3, {})} | custom-call | flops 603979776 | bytes 7340032 | tf_op jit(solution)/shard_map/collect/pallas_call | solution.py:339
  81.3 2.6 %collective-permute-start.6 = (bf16[4,256,256]{2,1,0:T(8,128)(2,1)S(1)}, bf16[4,256,256]{2,1,0:T(8,128)(2,1)S(1)}, u32[]{:S(2)}, u32[]{:S(2)}) collective-permute-start(bf16[4,256,256]{2,1,0:T(8,128)(2,1)S(1)} %get-tuple-element.16), channel_id=1, source_target_pairs={{0,3},{1,0},{2,1},{3,2},{4,7},{5,4},{6,5},{7,6},{8,11},{9,8},{10,9... | collective-permute-start | bytes 1572872 | tf_op jit(solution)/shard_map/ppermute | solution.py:72
  85.6 2.6 %part_ladder.11 = bf16[256,2048]{1,0:T(8,128)(2,1)S(1)} custom-call(bf16[4,256,256]{2,1,0:T(8,128)(2,1)S(1)} %collective-permute-done.4.a_ref, bf16[256,4096]{1,0:T(8,128)(2,1)S(1)} %bitcast.13, bf16[256,4096]{1,0:T(8,128)(2,1)} %collective-permute-done.refs_1_, bf16[128,4096]{1,0:T(8,128)(2,1)S(1)} %collective-permute-done.2.refs_2_, ...), custom_call_target="tpu_custom_call" | custom-call | flops 1073741824 | bytes 6291456 | tf_op jit(solution)/shard_map/part_ladder/pallas_call | solution.py:241
  89.3 2.6 %part_ladder.8 = bf16[256,2048]{1,0:T(8,128)(2,1)S(1)} custom-call(bf16[4,256,256]{2,1,0:T(8,128)(2,1)S(1)} %collective-permute-done.4.a_ref, bf16[256,4096]{1,0:T(8,128)(2,1)S(1)} %bitcast.14, bf16[256,4096]{1,0:T(8,128)(2,1)} %collective-permute-done.refs_1_, bf16[128,4096]{1,0:T(8,128)(2,1)S(1)} %collective-permute-done.2.refs_2_, ...), custom_call_target="tpu_custom_call" | custom-call | flops 1073741824 | bytes 6291456 | tf_op jit(solution)/shard_map/part_ladder/pallas_call | solution.py:241
  92.0 2.4 %collective-permute-start.11 = (bf16[256,2048]{1,0:T(8,128)(2,1)S(1)}, bf16[256,2048]{1,0:T(8,128)(2,1)S(1)}, u32[]{:S(2)}, u32[]{:S(2)}) collective-permute-start(bf16[256,2048]{1,0:T(8,128)(2,1)S(1)} %part_ladder.8), channel_id=1, source_target_pairs={{0,3},{1,0},{2,1},{3,2},{4,7},{5,4},{6,5},{7,6},{8,11},{9,8},{10,9... | collective-permute-start | bytes 3145736 | tf_op jit(solution)/shard_map/ppermute | solution.py:72
  94.4 2.6 %part_ladder.13 = bf16[256,2048]{1,0:T(8,128)(2,1)S(1)} custom-call(bf16[4,256,256]{2,1,0:T(8,128)(2,1)S(1)} %collective-permute-done.6.a_ref, bf16[256,4096]{1,0:T(8,128)(2,1)S(1)} %bitcast.15, bf16[256,4096]{1,0:T(8,128)(2,1)} %collective-permute-done.refs_1_, bf16[128,4096]{1,0:T(8,128)(2,1)S(1)} %collective-permute-done.2.refs_2_, ...), custom_call_target="tpu_custom_call" | custom-call | flops 1073741824 | bytes 6291456 | tf_op jit(solution)/shard_map/part_ladder/pallas_call | solution.py:241
  97.2 2.7 %part_ladder.9 = bf16[256,2048]{1,0:T(8,128)(2,1)S(1)} custom-call(bf16[4,256,256]{2,1,0:T(8,128)(2,1)S(1)} %collective-permute-done.5.a_ref, bf16[256,4096]{1,0:T(8,128)(2,1)S(1)} %bitcast.16, bf16[256,4096]{1,0:T(8,128)(2,1)} %collective-permute-done.refs_1_, bf16[128,4096]{1,0:T(8,128)(2,1)S(1)} %collective-permute-done.2.refs_2_, ...), custom_call_target="tpu_custom_call" | custom-call | flops 1073741824 | bytes 6291456 | tf_op jit(solution)/shard_map/part_ladder/pallas_call | solution.py:241
  99.8 3.3 %collective-permute-start.7 = (bf16[256,2048]{1,0:T(8,128)(2,1)S(1)}, bf16[256,2048]{1,0:T(8,128)(2,1)S(1)}, u32[]{:S(2)}, u32[]{:S(2)}) collective-permute-start(bf16[256,2048]{1,0:T(8,128)(2,1)S(1)} %part_ladder.9), channel_id=1, source_target_pairs={{0,3},{1,0},{2,1},{3,2},{4,7},{5,4},{6,5},{7,6},{8,11},{9,8},{10,9... | collective-permute-start | bytes 3145736 | tf_op jit(solution)/shard_map/ppermute | solution.py:72
  104.3 2.7 %part_ladder.12 = bf16[256,2048]{1,0:T(8,128)(2,1)S(1)} custom-call(bf16[4,256,256]{2,1,0:T(8,128)(2,1)S(1)} %collective-permute-done.6.a_ref, bf16[256,4096]{1,0:T(8,128)(2,1)S(1)} %bitcast.17, bf16[256,4096]{1,0:T(8,128)(2,1)} %collective-permute-done.refs_1_, bf16[128,4096]{1,0:T(8,128)(2,1)S(1)} %collective-permute-done.2.refs_2_, ...), custom_call_target="tpu_custom_call" | custom-call | flops 1073741824 | bytes 6291456 | tf_op jit(solution)/shard_map/part_ladder/pallas_call | solution.py:241
  107.1 2.7 %part_ladder.15 = bf16[256,2048]{1,0:T(8,128)(2,1)S(1)} custom-call(bf16[4,256,256]{2,1,0:T(8,128)(2,1)S(1)} %collective-permute-done.5.a_ref, bf16[256,4096]{1,0:T(8,128)(2,1)S(1)} %bitcast.18, bf16[256,4096]{1,0:T(8,128)(2,1)} %collective-permute-done.refs_1_, bf16[128,4096]{1,0:T(8,128)(2,1)S(1)} %collective-permute-done.2.refs_2_, ...), custom_call_target="tpu_custom_call" | custom-call | flops 1073741824 | bytes 6291456 | tf_op jit(solution)/shard_map/part_ladder/pallas_call | solution.py:241
  109.7 3.4 %collective-permute-start.12 = (bf16[256,2048]{1,0:T(8,128)(2,1)S(1)}, bf16[256,2048]{1,0:T(8,128)(2,1)S(1)}, u32[]{:S(2)}, u32[]{:S(2)}) collective-permute-start(bf16[256,2048]{1,0:T(8,128)(2,1)S(1)} %part_ladder.15), channel_id=1, source_target_pairs={{0,3},{1,0},{2,1},{3,2},{4,7},{5,4},{6,5},{7,6},{8,11},{9,8},{10,9... | collective-permute-start | bytes 3145736 | tf_op jit(solution)/shard_map/ppermute | solution.py:72
  113.2 2.3 %collective-permute-done.10.refs_5_ = bf16[256,2048]{1,0:T(8,128)(2,1)S(1)} collective-permute-done((bf16[256,2048]{1,0:T(8,128)(2,1)S(1)}, bf16[256,2048]{1,0:T(8,128)(2,1)S(1)}, u32[]{:S(2)}, u32[]{:S(2)}) %collective-permute-start.10) | collective-permute-done | bytes 1048608 | tf_op jit(solution)/shard_map/ppermute | solution.py:72
  115.5 2.7 %part_ladder.14.refs_1_ = f32[256,2048]{1,0:T(8,128)S(1)} custom-call(bf16[4,256,256]{2,1,0:T(8,128)(2,1)S(1)} %get-tuple-element.13.a_ref, bf16[256,4096]{1,0:T(8,128)(2,1)S(1)} %bitcast.19, bf16[256,4096]{1,0:T(8,128)(2,1)} %collective-permute-done.refs_1_, bf16[128,4096]{1,0:T(8,128)(2,1)S(1)} %collective-permute-done.2.refs_2_, ...), custom_call_target="tpu_custom_call" | custom-call | flops 1073741824 | bytes 6291456 | tf_op jit(solution)/shard_map/part_ladder/pallas_call | solution.py:241
  118.3 2.7 %part_ladder.10.refs_0_ = f32[256,2048]{1,0:T(8,128)S(1)} custom-call(bf16[4,256,256]{2,1,0:T(8,128)(2,1)S(1)} %get-tuple-element.13.a_ref, bf16[256,4096]{1,0:T(8,128)(2,1)S(1)} %bitcast.20, bf16[256,4096]{1,0:T(8,128)(2,1)} %collective-permute-done.refs_1_, bf16[128,4096]{1,0:T(8,128)(2,1)S(1)} %collective-permute-done.2.refs_2_, ...), custom_call_target="tpu_custom_call" | custom-call | flops 1073741824 | bytes 6291456 | tf_op jit(solution)/shard_map/part_ladder/pallas_call | solution.py:241
  121.0 5.7 %collective-permute-done.9.refs_1_ = bf16[256,2048]{1,0:T(8,128)(2,1)S(1)} collective-permute-done((bf16[256,2048]{1,0:T(8,128)(2,1)S(1)}, bf16[256,2048]{1,0:T(8,128)(2,1)S(1)}, u32[]{:S(2)}, u32[]{:S(2)}) %collective-permute-start.9) | collective-permute-done | bytes 1048608 | tf_op jit(solution)/shard_map/ppermute | solution.py:72
  (27 shorter events, 15.3 us)
Async XLA Ops:
  0.6 36.6 %collective-permute-start.1 = (bf16[256,4096]{1,0:T(8,128)(2,1)}, bf16[256,4096]{1,0:T(8,128)(2,1)S(1)}, u32[]{:S(2)}, u32[]{:S(2)}) collective-permute-start(bf16[256,4096]{1,0:T(8,128)(2,1)} %bitcast.11), channel_id=1, source_target_pairs={{0,4},{1,5},{2,6},{3,7},{4,8},{5,9},{6,10},{7,11},{8,12},{9,13},{1... | collective-permute-start | bytes 6291464 | tf_op jit(solution)/shard_map/ppermute | solution.py:68
  2.3 41.8 %collective-permute-start = (bf16[256,4096]{1,0:T(8,128)(2,1)}, bf16[256,4096]{1,0:T(8,128)(2,1)}, u32[]{:S(2)}, u32[]{:S(2)}) collective-permute-start(bf16[256,4096]{1,0:T(8,128)(2,1)} %bitcast.12), channel_id=1, source_target_pairs={{0,12},{1,13},{2,14},{3,15},{4,0},{5,1},{6,2},{7,3},{8,4},{9,5},{1... | collective-permute-start | bytes 6291464 | tf_op jit(solution)/shard_map/ppermute | solution.py:68
  10.4 60.4 %all-to-all-start = ((bf16[128,104,128]{2,1,0:T(8,128)(2,1)}), bf16[128,104,128]{2,1,0:T(8,128)(2,1)}, u32[]{:S(2)}, u32[]{:S(2)}) async-start(bf16[128,104,128]{2,1,0:T(8,128)(2,1)} %bitcast.23), calls=%async_computation | async-start | bytes 6815744 | tf_op jit(solution)/shard_map/all_to_all | solution.py:319
  20.8 29.5 %copy-start.1 = (s32[64,64]{1,0:T(8,128)S(1)}, s32[64,64]{1,0:T(8,128)}, u32[]{:S(2)}) copy-start(s32[64,64]{1,0:T(8,128)} %table_ref.1) | copy-start | bytes 49156
  20.8 29.5 %copy-start.2 = (f32[64]{0:T(128)S(1)}, f32[64]{0:T(128)}, u32[]{:S(2)}) copy-start(f32[64]{0:T(128)} %param.14) | copy-start | bytes 772
  38.3 45.6 %collective-permute-start.2 = (bf16[128,4096]{1,0:T(8,128)(2,1)}, bf16[128,4096]{1,0:T(8,128)(2,1)S(1)}, u32[]{:S(2)}, u32[]{:S(2)}) collective-permute-start(bf16[128,4096]{1,0:T(8,128)(2,1)} %slice.8), channel_id=1, source_target_pairs={{0,4},{1,5},{2,6},{3,7},{4,8},{5,9},{6,10},{7,11},{8,12},{9,13},{1... | collective-permute-start | bytes 3145736 | tf_op jit(solution)/shard_map/ppermute | solution.py:68
  46.4 37.5 %collective-permute-start.3 = (bf16[128,4096]{1,0:T(8,128)(2,1)}, bf16[128,4096]{1,0:T(8,128)(2,1)}, u32[]{:S(2)}, u32[]{:S(2)}) collective-permute-start(bf16[128,4096]{1,0:T(8,128)(2,1)} %slice.9), channel_id=1, source_target_pairs={{0,12},{1,13},{2,14},{3,15},{4,0},{5,1},{6,2},{7,3},{8,4},{9,5},{1... | collective-permute-start | bytes 3145736 | tf_op jit(solution)/shard_map/ppermute | solution.py:68
  74.8 10.8 %collective-permute-start.4 = (bf16[4,256,256]{2,1,0:T(8,128)(2,1)S(1)}, bf16[4,256,256]{2,1,0:T(8,128)(2,1)S(1)}, u32[]{:S(2)}, u32[]{:S(2)}) collective-permute-start(bf16[4,256,256]{2,1,0:T(8,128)(2,1)S(1)} %get-tuple-element.14), channel_id=1, source_target_pairs={{0,2},{1,3},{2,0},{3,1},{4,6},{5,7},{6,4},{7,5},{8,10},{9,11},{10,... | collective-permute-start | bytes 1572872 | tf_op jit(solution)/shard_map/ppermute | solution.py:72
  75.7 9.9 %copy-start = (bf16[1,256,4096]{2,1,0:T(8,128)(2,1)S(1)}, bf16[1,256,4096]{2,1,0:T(8,128)(2,1)}, u32[]{:S(2)}) copy-start(bf16[1,256,4096]{2,1,0:T(8,128)(2,1)} %param.9) | copy-start | bytes 6291460
  80.6 11.4 %collective-permute-start.5 = (bf16[4,256,256]{2,1,0:T(8,128)(2,1)S(1)}, bf16[4,256,256]{2,1,0:T(8,128)(2,1)S(1)}, u32[]{:S(2)}, u32[]{:S(2)}) collective-permute-start(bf16[4,256,256]{2,1,0:T(8,128)(2,1)S(1)} %get-tuple-element.15), channel_id=1, source_target_pairs={{0,1},{1,2},{2,3},{3,0},{4,5},{5,6},{6,7},{7,4},{8,9},{9,10},{10,1... | collective-permute-start | bytes 1572872 | tf_op jit(solution)/shard_map/ppermute | solution.py:72
  81.3 10.7 %collective-permute-start.6 = (bf16[4,256,256]{2,1,0:T(8,128)(2,1)S(1)}, bf16[4,256,256]{2,1,0:T(8,128)(2,1)S(1)}, u32[]{:S(2)}, u32[]{:S(2)}) collective-permute-start(bf16[4,256,256]{2,1,0:T(8,128)(2,1)S(1)} %get-tuple-element.16), channel_id=1, source_target_pairs={{0,3},{1,0},{2,1},{3,2},{4,7},{5,4},{6,5},{7,6},{8,11},{9,8},{10,9... | collective-permute-start | bytes 1572872 | tf_op jit(solution)/shard_map/ppermute | solution.py:72
  88.2 16.1 %collective-permute-start.8 = (bf16[256,2048]{1,0:T(8,128)(2,1)S(1)}, bf16[256,2048]{1,0:T(8,128)(2,1)S(1)}, u32[]{:S(2)}, u32[]{:S(2)}) collective-permute-start(bf16[256,2048]{1,0:T(8,128)(2,1)S(1)} %part_ladder.11), channel_id=1, source_target_pairs={{0,1},{1,2},{2,3},{3,0},{4,5},{5,6},{6,7},{7,4},{8,9},{9,10},{10,1... | collective-permute-start | bytes 3145736 | tf_op jit(solution)/shard_map/ppermute | solution.py:72
  92.0 15.0 %collective-permute-start.11 = (bf16[256,2048]{1,0:T(8,128)(2,1)S(1)}, bf16[256,2048]{1,0:T(8,128)(2,1)S(1)}, u32[]{:S(2)}, u32[]{:S(2)}) collective-permute-start(bf16[256,2048]{1,0:T(8,128)(2,1)S(1)} %part_ladder.8), channel_id=1, source_target_pairs={{0,3},{1,0},{2,1},{3,2},{4,7},{5,4},{6,5},{7,6},{8,11},{9,8},{10,9... | collective-permute-start | bytes 3145736 | tf_op jit(solution)/shard_map/ppermute | solution.py:72
  97.1 18.4 %collective-permute-start.10 = (bf16[256,2048]{1,0:T(8,128)(2,1)S(1)}, bf16[256,2048]{1,0:T(8,128)(2,1)S(1)}, u32[]{:S(2)}, u32[]{:S(2)}) collective-permute-start(bf16[256,2048]{1,0:T(8,128)(2,1)S(1)} %part_ladder.13), channel_id=1, source_target_pairs={{0,1},{1,2},{2,3},{3,0},{4,5},{5,6},{6,7},{7,4},{8,9},{9,10},{10,1... | collective-permute-start | bytes 3145736 | tf_op jit(solution)/shard_map/ppermute | solution.py:72
  99.8 18.5 %collective-permute-start.7 = (bf16[256,2048]{1,0:T(8,128)(2,1)S(1)}, bf16[256,2048]{1,0:T(8,128)(2,1)S(1)}, u32[]{:S(2)}, u32[]{:S(2)}) collective-permute-start(bf16[256,2048]{1,0:T(8,128)(2,1)S(1)} %part_ladder.9), channel_id=1, source_target_pairs={{0,3},{1,0},{2,1},{3,2},{4,7},{5,4},{6,5},{7,6},{8,11},{9,8},{10,9... | collective-permute-start | bytes 3145736 | tf_op jit(solution)/shard_map/ppermute | solution.py:72
  106.9 19.8 %collective-permute-start.9 = (bf16[256,2048]{1,0:T(8,128)(2,1)S(1)}, bf16[256,2048]{1,0:T(8,128)(2,1)S(1)}, u32[]{:S(2)}, u32[]{:S(2)}) collective-permute-start(bf16[256,2048]{1,0:T(8,128)(2,1)S(1)} %part_ladder.12), channel_id=1, source_target_pairs={{0,1},{1,2},{2,3},{3,0},{4,5},{5,6},{6,7},{7,4},{8,9},{9,10},{10,1... | collective-permute-start | bytes 3145736 | tf_op jit(solution)/shard_map/ppermute | solution.py:72
  109.7 19.8 %collective-permute-start.12 = (bf16[256,2048]{1,0:T(8,128)(2,1)S(1)}, bf16[256,2048]{1,0:T(8,128)(2,1)S(1)}, u32[]{:S(2)}, u32[]{:S(2)}) collective-permute-start(bf16[256,2048]{1,0:T(8,128)(2,1)S(1)} %part_ladder.15), channel_id=1, source_target_pairs={{0,3},{1,0},{2,1},{3,2},{4,7},{5,4},{6,5},{7,6},{8,11},{9,8},{10,9... | collective-permute-start | bytes 3145736 | tf_op jit(solution)/shard_map/ppermute | solution.py:72

commit v8 on v7

--- a/solution.py
+++ b/solution.py
@@ -260,13 +260,12 @@
 
 
 def join(side, own, other, into=()):
-    steps = HALF // CUT
-    part = pl.BlockSpec((ROWS, CUT), lambda n: (0, n))
+    part = pl.BlockSpec((ROWS // 2, HALF), lambda n: (n, 0))
     return pl.pallas_call(
         join_kernel,
-        grid=(steps,),
+        grid=(2,),
         in_specs=[pl.BlockSpec(memory_space=pl.ANY)] * len(into) + [part, part],
-        out_specs=pl.BlockSpec((ROWS, CUT), lambda n: (0, side * steps + n)),
+        out_specs=pl.BlockSpec((ROWS // 2, HALF), lambda n: (n, side)),
         out_shape=jax.ShapeDtypeStruct((ROWS, WIDTH), jnp.float32),
         input_output_aliases={0: 0} if into else {},
         compiler_params=pltpu.CompilerParams(vmem_limit_bytes=8 * MIB),
@@ -359,7 +358,8 @@
         )(where, pair_bubble, arrived, *into)
 
     gamma, w2 = collect((2,))
-    gamma, w1, w3, own = collect((1, 3, 0), gamma)
+    gamma, w1, w3 = collect((1, 3), gamma)
+    gamma, own = collect((0,), gamma)
 
     part = functools.partial(part_ladder, full_parts=full_parts)
     bf16, f32 = jnp.bfloat16, jnp.float32

time: 133 us -> 132 us (level)
  Pallas kernels: 40.6 us -> 43.6 us
  waiting for transfers between devices: 50.4 us -> 48.3 us
  starting transfers between devices: 34.5 us -> 33.1 us
    pallas_call x2 -> x3, Pallas kernels: 8.85 us -> 12.4 us  [collect(): pl.pallas_call(functools.partial(collect_kernel, turns), in_specs=[pl.Blo...]
    ppermute x9, waiting for transfers between devices: 12.1 us -> 9.98 us  [move_h(): return lax.ppermute(array, AXES, pairs_along((1, 0), step))]
    ppermute x9, starting transfers between devices: 14.6 us -> 13.3 us  [move_h(): return lax.ppermute(array, AXES, pairs_along((1, 0), step))]
  transfers between devices with their start and end apart: 14 -> 14, of which waited for: 8 -> 8; matrix products, arithmetic and copies ran while one was open for 3% -> 3% of each run, Pallas kernels for 30% -> 32%
where the time goes in v8:
time: 132 us; the launch traced here: 131 us
  waiting for transfers between devices  48.3 us (37%)
  Pallas kernels  43.6 us (33%)
  starting transfers between devices  33.1 us (25%)
  local copies, waits for them, and re-layouts  3.45 us (3%)
  between operations  2.16 us (2%)
    pallas_call x8, Pallas kernels, part_ladder(): pl.pallas_call(functools.partial(ladder_kernel, len(full_parts)), grid=(s...  21.4 us
    all_to_all x1, waiting for transfers between devices, per_device(): lax.all_to_all(payload.reshape(DEVICES, CHUNK, LANES), AXES, split_axis=0...  19.7 us
    ppermute x4, waiting for transfers between devices, move_g(): return lax.ppermute(array, AXES, pairs_along((0, 1), step))  18.6 us
    ppermute x9, starting transfers between devices, move_h(): return lax.ppermute(array, AXES, pairs_along((1, 0), step))  13.3 us
    pallas_call x3, Pallas kernels, collect(): pl.pallas_call(functools.partial(collect_kernel, turns), in_specs=[pl.Blo...  12.4 us
    all_to_all x1, starting transfers between devices, per_device(): lax.all_to_all(payload.reshape(DEVICES, CHUNK, LANES), AXES, split_axis=0...  10.4 us
    ppermute x9, waiting for transfers between devices, move_h(): return lax.ppermute(array, AXES, pairs_along((1, 0), step))  9.98 us
    ppermute x4, starting transfers between devices, move_g(): return lax.ppermute(array, AXES, pairs_along((0, 1), step))  9.47 us
  transfers between devices with their start and end apart: 14, of which 8 were waited for; matrix products, arithmetic and copies ran while one was open for 3% of the time, Pallas kernels for 32%

profile of v8, /device:TPU:0, one launch (start us, length us, event | category | flops | bytes accessed | tf_op | source)
XLA Modules:
  0.0 130.8 jit_solution(17286892164995632932)
XLA Ops:
  3.9 6.5 %place.1 = bf16[13312,128]{1,0:T(8,128)(2,1)} custom-call(s32[1,256]{1,0:T(1,128)} %target_ref.1, s32[1,256]{1,0:T(1,128)} %shift_ref.1, bf16[256,4096]{1,0:T(8,128)(2,1)} %bitcast.25), custom_call_target="tpu_custom_call" | custom-call | flops 805306368 | bytes 5242880 | tf_op jit(solution)/shard_map/place/pallas_call | solution.py:300
  10.4 10.4 %all-to-all-start = ((bf16[128,104,128]{2,1,0:T(8,128)(2,1)}), bf16[128,104,128]{2,1,0:T(8,128)(2,1)}, u32[]{:S(2)}, u32[]{:S(2)}) async-start(bf16[128,104,128]{2,1,0:T(8,128)(2,1)} %bitcast.24), calls=%async_computation | async-start | bytes 6815744 | tf_op jit(solution)/shard_map/all_to_all | solution.py:318
  22.2 15.1 %collective-permute-done.1.refs_4_ = bf16[256,4096]{1,0:T(8,128)(2,1)S(1)} collective-permute-done((bf16[256,4096]{1,0:T(8,128)(2,1)}, bf16[256,4096]{1,0:T(8,128)(2,1)S(1)}, u32[]{:S(2)}, u32[]{:S(2)}) %collective-permute-start.1) | collective-permute-done | bytes 2097184 | tf_op jit(solution)/shard_map/ppermute | solution.py:68
  38.3 2.3 %collective-permute-start.2 = (bf16[128,4096]{1,0:T(8,128)(2,1)}, bf16[128,4096]{1,0:T(8,128)(2,1)S(1)}, u32[]{:S(2)}, u32[]{:S(2)}) collective-permute-start(bf16[128,4096]{1,0:T(8,128)(2,1)} %slice.8), channel_id=1, source_target_pairs={{0,4},{1,5},{2,6},{3,7},{4,8},{5,9},{6,10},{7,11},{8,12},{9,13},{1... | collective-permute-start | bytes 3145736 | tf_op jit(solution)/shard_map/ppermute | solution.py:68
  40.6 3.5 %collective-permute-done.refs_1_ = bf16[256,4096]{1,0:T(8,128)(2,1)} collective-permute-done((bf16[256,4096]{1,0:T(8,128)(2,1)}, bf16[256,4096]{1,0:T(8,128)(2,1)}, u32[]{:S(2)}, u32[]{:S(2)}) %collective-permute-start) | collective-permute-done | bytes 2097184 | tf_op jit(solution)/shard_map/ppermute | solution.py:68
  44.0 2.4 %slice.9 = bf16[128,4096]{1,0:T(8,128)(2,1)} slice(bf16[256,4096]{1,0:T(8,128)(2,1)} %collective-permute-done.refs_1_), slice={[128:256], [0:4096]} | slice | bytes 2097152 | tf_op jit(solution)/shard_map/slice | solution.py:293
  46.4 3.9 %collective-permute-start.3 = (bf16[128,4096]{1,0:T(8,128)(2,1)}, bf16[128,4096]{1,0:T(8,128)(2,1)}, u32[]{:S(2)}, u32[]{:S(2)}) collective-permute-start(bf16[128,4096]{1,0:T(8,128)(2,1)} %slice.9), channel_id=1, source_target_pairs={{0,12},{1,13},{2,14},{3,15},{4,0},{5,1},{6,2},{7,3},{8,4},{9,5},{1... | collective-permute-start | bytes 3145736 | tf_op jit(solution)/shard_map/ppermute | solution.py:68
  51.1 19.7 %all-to-all-done = bf16[128,104,128]{2,1,0:T(8,128)(2,1)} async-done(((bf16[128,104,128]{2,1,0:T(8,128)(2,1)}), bf16[128,104,128]{2,1,0:T(8,128)(2,1)}, u32[]{:S(2)}, u32[]{:S(2)}) %all-to-all-start) | async-done | bytes 3407904 | tf_op jit(solution)/shard_map/all_to_all | solution.py:318
  70.8 3.9 %collect.3 = (f32[256,4096]{1,0:T(8,128)}, bf16[4,256,256]{2,1,0:T(8,128)(2,1)S(1)}) custom-call(s32[4]{0:T(128)S(1)} %pad_add_fusion.where_ref, f32[1,4096]{1,0:T(1,128)S(1)} %bubble.1.bubble_ref, bf16[13312,128]{1,0:T(8,128)(2,1)} %bitcast.7.box_ref), custom_call_target="tpu_custom_call" | custom-call | flops 201326592 | bytes 5242880 | tf_op jit(solution)/shard_map/collect/pallas_call | solution.py:338
  75.7 4.5 %collect.4 = (f32[256,4096]{1,0:T(8,128)}, bf16[4,256,256]{2,1,0:T(8,128)(2,1)S(1)}, bf16[4,256,256]{2,1,0:T(8,128)(2,1)S(1)}) custom-call(s32[4]{0:T(128)S(1)} %pad_add_fusion.where_ref, f32[1,4096]{1,0:T(1,128)S(1)} %bubble.1.bubble_ref, bf16[13312,128]{1,0:T(8,128)(2,1)} %bitcast.7.box_ref, ...), custom_call_target="tpu_custom_call", output_to_operand_aliasing={{0}: (3, {})} | custom-call | flops 402653184 | bytes 6291456 | tf_op jit(solution)/shard_map/collect/pallas_call | solution.py:338
  80.8 2.6 %collective-permute-start.6 = (bf16[4,256,256]{2,1,0:T(8,128)(2,1)S(1)}, bf16[4,256,256]{2,1,0:T(8,128)(2,1)S(1)}, u32[]{:S(2)}, u32[]{:S(2)}) collective-permute-start(bf16[4,256,256]{2,1,0:T(8,128)(2,1)S(1)} %get-tuple-element.18), channel_id=1, source_target_pairs={{0,3},{1,0},{2,1},{3,2},{4,7},{5,4},{6,5},{7,6},{8,11},{9,8},{10,9... | collective-permute-start | bytes 1572872 | tf_op jit(solution)/shard_map/ppermute | solution.py:72
  85.6 2.6 %part_ladder.11 = bf16[256,2048]{1,0:T(8,128)(2,1)S(1)} custom-call(bf16[4,256,256]{2,1,0:T(8,128)(2,1)S(1)} %collective-permute-done.4.a_ref, bf16[256,4096]{1,0:T(8,128)(2,1)S(1)} %bitcast.13, bf16[256,4096]{1,0:T(8,128)(2,1)} %collective-permute-done.refs_1_, bf16[128,4096]{1,0:T(8,128)(2,1)S(1)} %collective-permute-done.2.refs_2_, ...), custom_call_target="tpu_custom_call" | custom-call | flops 1073741824 | bytes 6291456 | tf_op jit(solution)/shard_map/part_ladder/pallas_call | solution.py:241
  89.4 2.6 %part_ladder.8 = bf16[256,2048]{1,0:T(8,128)(2,1)S(1)} custom-call(bf16[4,256,256]{2,1,0:T(8,128)(2,1)S(1)} %collective-permute-done.4.a_ref, bf16[256,4096]{1,0:T(8,128)(2,1)S(1)} %bitcast.14, bf16[256,4096]{1,0:T(8,128)(2,1)} %collective-permute-done.refs_1_, bf16[128,4096]{1,0:T(8,128)(2,1)S(1)} %collective-permute-done.2.refs_2_, ...), custom_call_target="tpu_custom_call" | custom-call | flops 1073741824 | bytes 6291456 | tf_op jit(solution)/shard_map/part_ladder/pallas_call | solution.py:241
  92.0 2.3 %collective-permute-start.11 = (bf16[256,2048]{1,0:T(8,128)(2,1)S(1)}, bf16[256,2048]{1,0:T(8,128)(2,1)S(1)}, u32[]{:S(2)}, u32[]{:S(2)}) collective-permute-start(bf16[256,2048]{1,0:T(8,128)(2,1)S(1)} %part_ladder.8), channel_id=1, source_target_pairs={{0,3},{1,0},{2,1},{3,2},{4,7},{5,4},{6,5},{7,6},{8,11},{9,8},{10,9... | collective-permute-start | bytes 3145736 | tf_op jit(solution)/shard_map/ppermute | solution.py:72
  94.3 2.6 %part_ladder.9 = bf16[256,2048]{1,0:T(8,128)(2,1)S(1)} custom-call(bf16[4,256,256]{2,1,0:T(8,128)(2,1)S(1)} %collective-permute-done.5.a_ref, bf16[256,4096]{1,0:T(8,128)(2,1)S(1)} %bitcast.15, bf16[256,4096]{1,0:T(8,128)(2,1)} %collective-permute-done.refs_1_, bf16[128,4096]{1,0:T(8,128)(2,1)S(1)} %collective-permute-done.2.refs_2_, ...), custom_call_target="tpu_custom_call" | custom-call | flops 1073741824 | bytes 6291456 | tf_op jit(solution)/shard_map/part_ladder/pallas_call | solution.py:241
  97.3 2.6 %part_ladder.13 = bf16[256,2048]{1,0:T(8,128)(2,1)S(1)} custom-call(bf16[4,256,256]{2,1,0:T(8,128)(2,1)S(1)} %collective-permute-done.6.a_ref, bf16[256,4096]{1,0:T(8,128)(2,1)S(1)} %bitcast.16, bf16[256,4096]{1,0:T(8,128)(2,1)} %collective-permute-done.refs_1_, bf16[128,4096]{1,0:T(8,128)(2,1)S(1)} %collective-permute-done.2.refs_2_, ...), custom_call_target="tpu_custom_call" | custom-call | flops 1073741824 | bytes 6291456 | tf_op jit(solution)/shard_map/part_ladder/pallas_call | solution.py:241
  101.9 2.4 %collective-permute-done.8.refs_5_ = bf16[256,2048]{1,0:T(8,128)(2,1)S(1)} collective-permute-done((bf16[256,2048]{1,0:T(8,128)(2,1)S(1)}, bf16[256,2048]{1,0:T(8,128)(2,1)S(1)}, u32[]{:S(2)}, u32[]{:S(2)}) %collective-permute-start.8) | collective-permute-done | bytes 1048608 | tf_op jit(solution)/shard_map/ppermute | solution.py:72
  104.3 2.7 %part_ladder.12 = bf16[256,2048]{1,0:T(8,128)(2,1)S(1)} custom-call(bf16[4,256,256]{2,1,0:T(8,128)(2,1)S(1)} %collective-permute-done.6.a_ref, bf16[256,4096]{1,0:T(8,128)(2,1)S(1)} %bitcast.17, bf16[256,4096]{1,0:T(8,128)(2,1)} %collective-permute-done.refs_1_, bf16[128,4096]{1,0:T(8,128)(2,1)S(1)} %collective-permute-done.2.refs_2_, ...), custom_call_target="tpu_custom_call" | custom-call | flops 1073741824 | bytes 6291456 | tf_op jit(solution)/shard_map/part_ladder/pallas_call | solution.py:241
  107.1 2.7 %part_ladder.15 = bf16[256,2048]{1,0:T(8,128)(2,1)S(1)} custom-call(bf16[4,256,256]{2,1,0:T(8,128)(2,1)S(1)} %collective-permute-done.5.a_ref, bf16[256,4096]{1,0:T(8,128)(2,1)S(1)} %bitcast.18, bf16[256,4096]{1,0:T(8,128)(2,1)} %collective-permute-done.refs_1_, bf16[128,4096]{1,0:T(8,128)(2,1)S(1)} %collective-permute-done.2.refs_2_, ...), custom_call_target="tpu_custom_call" | custom-call | flops 1073741824 | bytes 6291456 | tf_op jit(solution)/shard_map/part_ladder/pallas_call | solution.py:241
  109.8 3.3 %collective-permute-start.12 = (bf16[256,2048]{1,0:T(8,128)(2,1)S(1)}, bf16[256,2048]{1,0:T(8,128)(2,1)S(1)}, u32[]{:S(2)}, u32[]{:S(2)}) collective-permute-start(bf16[256,2048]{1,0:T(8,128)(2,1)S(1)} %part_ladder.15), channel_id=1, source_target_pairs={{0,3},{1,0},{2,1},{3,2},{4,7},{5,4},{6,5},{7,6},{8,11},{9,8},{10,9... | collective-permute-start | bytes 3145736 | tf_op jit(solution)/shard_map/ppermute | solution.py:72
  113.0 3.9 %collect.5 = (f32[256,4096]{1,0:T(8,128)}, bf16[4,256,256]{2,1,0:T(8,128)(2,1)S(1)}) custom-call(s32[4]{0:T(128)S(1)} %pad_add_fusion.where_ref, f32[1,4096]{1,0:T(1,128)S(1)} %bubble.1.bubble_ref, bf16[13312,128]{1,0:T(8,128)(2,1)} %bitcast.7.box_ref, f32[256,4096]{1,0:T(8,128)} %get-tuple-element.13.refs_0_), custom_call_target="tpu_custom_call", output_to_operand_aliasing={{0}: (3, {})} | custom-call | flops 201326592 | bytes 5242880 | tf_op jit(solution)/shard_map/collect/pallas_call | solution.py:338
  118.1 2.7 %part_ladder.10.refs_0_ = f32[256,2048]{1,0:T(8,128)S(1)} custom-call(bf16[4,256,256]{2,1,0:T(8,128)(2,1)S(1)} %get-tuple-element.15.a_ref, bf16[256,4096]{1,0:T(8,128)(2,1)S(1)} %bitcast.19, bf16[256,4096]{1,0:T(8,128)(2,1)} %collective-permute-done.refs_1_, bf16[128,4096]{1,0:T(8,128)(2,1)S(1)} %collective-permute-done.2.refs_2_, ...), custom_call_target="tpu_custom_call" | custom-call | flops 1073741824 | bytes 6291456 | tf_op jit(solution)/shard_map/part_ladder/pallas_call | solution.py:241
  120.9 2.8 %part_ladder.14.refs_1_ = f32[256,2048]{1,0:T(8,128)S(1)} custom-call(bf16[4,256,256]{2,1,0:T(8,128)(2,1)S(1)} %get-tuple-element.15.a_ref, bf16[256,4096]{1,0:T(8,128)(2,1)S(1)} %bitcast.20, bf16[256,4096]{1,0:T(8,128)(2,1)} %collective-permute-done.refs_1_, bf16[128,4096]{1,0:T(8,128)(2,1)S(1)} %collective-permute-done.2.refs_2_, ...), custom_call_target="tpu_custom_call" | custom-call | flops 1073741824 | bytes 6291456 | tf_op jit(solution)/shard_map/part_ladder/pallas_call | solution.py:241
  123.6 3.6 %collective-permute-done.9.refs_1_ = bf16[256,2048]{1,0:T(8,128)(2,1)S(1)} collective-permute-done((bf16[256,2048]{1,0:T(8,128)(2,1)S(1)}, bf16[256,2048]{1,0:T(8,128)(2,1)S(1)}, u32[]{:S(2)}, u32[]{:S(2)}) %collective-permute-start.9) | collective-permute-done | bytes 1048608 | tf_op jit(solution)/shard_map/ppermute | solution.py:72
  (28 shorter events, 17.0 us)
Async XLA Ops:
  0.6 36.6 %collective-permute-start.1 = (bf16[256,4096]{1,0:T(8,128)(2,1)}, bf16[256,4096]{1,0:T(8,128)(2,1)S(1)}, u32[]{:S(2)}, u32[]{:S(2)}) collective-permute-start(bf16[256,4096]{1,0:T(8,128)(2,1)} %bitcast.11), channel_id=1, source_target_pairs={{0,4},{1,5},{2,6},{3,7},{4,8},{5,9},{6,10},{7,11},{8,12},{9,13},{1... | collective-permute-start | bytes 6291464 | tf_op jit(solution)/shard_map/ppermute | solution.py:68
  2.3 41.8 %collective-permute-start = (bf16[256,4096]{1,0:T(8,128)(2,1)}, bf16[256,4096]{1,0:T(8,128)(2,1)}, u32[]{:S(2)}, u32[]{:S(2)}) collective-permute-start(bf16[256,4096]{1,0:T(8,128)(2,1)} %bitcast.12), channel_id=1, source_target_pairs={{0,12},{1,13},{2,14},{3,15},{4,0},{5,1},{6,2},{7,3},{8,4},{9,5},{1... | collective-permute-start | bytes 6291464 | tf_op jit(solution)/shard_map/ppermute | solution.py:68
  10.4 60.4 %all-to-all-start = ((bf16[128,104,128]{2,1,0:T(8,128)(2,1)}), bf16[128,104,128]{2,1,0:T(8,128)(2,1)}, u32[]{:S(2)}, u32[]{:S(2)}) async-start(bf16[128,104,128]{2,1,0:T(8,128)(2,1)} %bitcast.24), calls=%async_computation | async-start | bytes 6815744 | tf_op jit(solution)/shard_map/all_to_all | solution.py:318
  20.8 29.5 %copy-start.1 = (s32[64,64]{1,0:T(8,128)S(1)}, s32[64,64]{1,0:T(8,128)}, u32[]{:S(2)}) copy-start(s32[64,64]{1,0:T(8,128)} %table_ref.1) | copy-start | bytes 49156
  20.8 29.5 %copy-start.2 = (f32[64]{0:T(128)S(1)}, f32[64]{0:T(128)}, u32[]{:S(2)}) copy-start(f32[64]{0:T(128)} %param.14) | copy-start | bytes 772
  38.3 45.2 %collective-permute-start.2 = (bf16[128,4096]{1,0:T(8,128)(2,1)}, bf16[128,4096]{1,0:T(8,128)(2,1)S(1)}, u32[]{:S(2)}, u32[]{:S(2)}) collective-permute-start(bf16[128,4096]{1,0:T(8,128)(2,1)} %slice.8), channel_id=1, source_target_pairs={{0,4},{1,5},{2,6},{3,7},{4,8},{5,9},{6,10},{7,11},{8,12},{9,13},{1... | collective-permute-start | bytes 3145736 | tf_op jit(solution)/shard_map/ppermute | solution.py:68
  46.4 37.0 %collective-permute-start.3 = (bf16[128,4096]{1,0:T(8,128)(2,1)}, bf16[128,4096]{1,0:T(8,128)(2,1)}, u32[]{:S(2)}, u32[]{:S(2)}) collective-permute-start(bf16[128,4096]{1,0:T(8,128)(2,1)} %slice.9), channel_id=1, source_target_pairs={{0,12},{1,13},{2,14},{3,15},{4,0},{5,1},{6,2},{7,3},{8,4},{9,5},{1... | collective-permute-start | bytes 3145736 | tf_op jit(solution)/shard_map/ppermute | solution.py:68
  74.8 10.8 %collective-permute-start.4 = (bf16[4,256,256]{2,1,0:T(8,128)(2,1)S(1)}, bf16[4,256,256]{2,1,0:T(8,128)(2,1)S(1)}, u32[]{:S(2)}, u32[]{:S(2)}) collective-permute-start(bf16[4,256,256]{2,1,0:T(8,128)(2,1)S(1)} %get-tuple-element.16), channel_id=1, source_target_pairs={{0,2},{1,3},{2,0},{3,1},{4,6},{5,7},{6,4},{7,5},{8,10},{9,11},{10,... | collective-permute-start | bytes 1572872 | tf_op jit(solution)/shard_map/ppermute | solution.py:72
  75.7 9.9 %copy-start = (bf16[1,256,4096]{2,1,0:T(8,128)(2,1)S(1)}, bf16[1,256,4096]{2,1,0:T(8,128)(2,1)}, u32[]{:S(2)}) copy-start(bf16[1,256,4096]{2,1,0:T(8,128)(2,1)} %param.9) | copy-start | bytes 6291460
  80.2 11.8 %collective-permute-start.5 = (bf16[4,256,256]{2,1,0:T(8,128)(2,1)S(1)}, bf16[4,256,256]{2,1,0:T(8,128)(2,1)S(1)}, u32[]{:S(2)}, u32[]{:S(2)}) collective-permute-start(bf16[4,256,256]{2,1,0:T(8,128)(2,1)S(1)} %get-tuple-element.17), channel_id=1, source_target_pairs={{0,1},{1,2},{2,3},{3,0},{4,5},{5,6},{6,7},{7,4},{8,9},{9,10},{10,1... | collective-permute-start | bytes 1572872 | tf_op jit(solution)/shard_map/ppermute | solution.py:72
  80.8 11.2 %collective-permute-start.6 = (bf16[4,256,256]{2,1,0:T(8,128)(2,1)S(1)}, bf16[4,256,256]{2,1,0:T(8,128)(2,1)S(1)}, u32[]{:S(2)}, u32[]{:S(2)}) collective-permute-start(bf16[4,256,256]{2,1,0:T(8,128)(2,1)S(1)} %get-tuple-element.18), channel_id=1, source_target_pairs={{0,3},{1,0},{2,1},{3,2},{4,7},{5,4},{6,5},{7,6},{8,11},{9,8},{10,9... | collective-permute-start | bytes 1572872 | tf_op jit(solution)/shard_map/ppermute | solution.py:72
  88.2 16.1 %collective-permute-start.8 = (bf16[256,2048]{1,0:T(8,128)(2,1)S(1)}, bf16[256,2048]{1,0:T(8,128)(2,1)S(1)}, u32[]{:S(2)}, u32[]{:S(2)}) collective-permute-start(bf16[256,2048]{1,0:T(8,128)(2,1)S(1)} %part_ladder.11), channel_id=1, source_target_pairs={{0,1},{1,2},{2,3},{3,0},{4,5},{5,6},{6,7},{7,4},{8,9},{9,10},{10,1... | collective-permute-start | bytes 3145736 | tf_op jit(solution)/shard_map/ppermute | solution.py:72
  92.0 15.0 %collective-permute-start.11 = (bf16[256,2048]{1,0:T(8,128)(2,1)S(1)}, bf16[256,2048]{1,0:T(8,128)(2,1)S(1)}, u32[]{:S(2)}, u32[]{:S(2)}) collective-permute-start(bf16[256,2048]{1,0:T(8,128)(2,1)S(1)} %part_ladder.8), channel_id=1, source_target_pairs={{0,3},{1,0},{2,1},{3,2},{4,7},{5,4},{6,5},{7,6},{8,11},{9,8},{10,9... | collective-permute-start | bytes 3145736 | tf_op jit(solution)/shard_map/ppermute | solution.py:72
  96.9 21.2 %collective-permute-start.7 = (bf16[256,2048]{1,0:T(8,128)(2,1)S(1)}, bf16[256,2048]{1,0:T(8,128)(2,1)S(1)}, u32[]{:S(2)}, u32[]{:S(2)}) collective-permute-start(bf16[256,2048]{1,0:T(8,128)(2,1)S(1)} %part_ladder.9), channel_id=1, source_target_pairs={{0,3},{1,0},{2,1},{3,2},{4,7},{5,4},{6,5},{7,6},{8,11},{9,8},{10,9... | collective-permute-start | bytes 3145736 | tf_op jit(solution)/shard_map/ppermute | solution.py:72
  99.9 20.9 %collective-permute-start.10 = (bf16[256,2048]{1,0:T(8,128)(2,1)S(1)}, bf16[256,2048]{1,0:T(8,128)(2,1)S(1)}, u32[]{:S(2)}, u32[]{:S(2)}) collective-permute-start(bf16[256,2048]{1,0:T(8,128)(2,1)S(1)} %part_ladder.13), channel_id=1, source_target_pairs={{0,1},{1,2},{2,3},{3,0},{4,5},{5,6},{6,7},{7,4},{8,9},{9,10},{10,1... | collective-permute-start | bytes 3145736 | tf_op jit(solution)/shard_map/ppermute | solution.py:72
  107.0 20.2 %collective-permute-start.9 = (bf16[256,2048]{1,0:T(8,128)(2,1)S(1)}, bf16[256,2048]{1,0:T(8,128)(2,1)S(1)}, u32[]{:S(2)}, u32[]{:S(2)}) collective-permute-start(bf16[256,2048]{1,0:T(8,128)(2,1)S(1)} %part_ladder.12), channel_id=1, source_target_pairs={{0,1},{1,2},{2,3},{3,0},{4,5},{5,6},{6,7},{7,4},{8,9},{9,10},{10,1... | collective-permute-start | bytes 3145736 | tf_op jit(solution)/shard_map/ppermute | solution.py:72
  109.8 19.6 %collective-permute-start.12 = (bf16[256,2048]{1,0:T(8,128)(2,1)S(1)}, bf16[256,2048]{1,0:T(8,128)(2,1)S(1)}, u32[]{:S(2)}, u32[]{:S(2)}) collective-permute-start(bf16[256,2048]{1,0:T(8,128)(2,1)S(1)} %part_ladder.15), channel_id=1, source_target_pairs={{0,3},{1,0},{2,1},{3,2},{4,7},{5,4},{6,5},{7,6},{8,11},{9,8},{10,9... | collective-permute-start | bytes 3145736 | tf_op jit(solution)/shard_map/ppermute | solution.py:72
